TPU v7x, 256 devices: a whole 4x4x8 slice. The times are simulated.
256 devices in a mesh: order: 16 (over z_lo, x), lat: 16 (over y, z_hi, core).
Axes of the slice: x: 4, y: 4, z: 8 (z_hi: 2, z_lo: 4; z = z_hi * 4 + z_lo), core: 2. Of those that a mesh axis runs over, the one named last changes fastest.
Arguments:
- coeffs: bfloat16 [1536, 32, 32, 274], P('order', 'lat'), may hold values from -6 to 6
- coupling: bfloat16 [4, 1536, 32, 32, 64], P(None, 'order', 'lat'), may hold values from -0.75 to 0.75
- pattern: int32 [4, 1536, 32], P(None, 'order', 'lat'), may hold values from 0 to 1
- assign: int32 [1536], replicated, may hold values from 0 to 1535, as said below
Outputs:
- spectral: bfloat16 [1536, 32, 32, 274], P('order', 'lat')
Inputs may be any that keep to these rules, and one draw needn't show every extreme that they name: `assign`: each of the 1536 orders appears exactly once. Entries k * 96 + c * 6 + j, for j below 6, hold orders from c * 96 to (c + 1) * 96 - 1.
All inputs are finite; a program needn't handle non-finite values.
Results may differ from a plain program's by a relative error of at most 0.0064.
Values may be sent and summed in bfloat16 or wider, within the bound.
No kernel may reach another device: no remote copies, remote signals or barrier semaphores. Data moves between devices by JAX's collectives and lax.ppermute only.
A program may use at most 128 MiB of HBM per device.

v0:
```python
import jax
import jax.numpy as jnp
from jax import lax
from jax.sharding import PartitionSpec as P

LEVELS = 4


def from_partner(value, axis, bit):
    return lax.ppermute(value, axis, [(i, i ^ 1 << bit) for i in range(lax.axis_size(axis))])


def combine_blocks(weights, own_part, far_part):
    rank_size = own_part.shape[-2]
    total = jnp.einsum(
        "obij,objc->obic", weights[..., :rank_size], own_part, preferred_element_type=jnp.float32
    )
    total = total + jnp.einsum(
        "obij,objc->obic", weights[..., rank_size:], far_part, preferred_element_type=jnp.float32
    )
    return total.astype(jnp.bfloat16)


def per_device(coeffs, coupling, pattern, assign):
    log_lat = lax.axis_size("lat").bit_length() - 1
    blocks = coeffs
    for level_idx in range(LEVELS):
        flip_bit = level_idx % log_lat
        partner = from_partner(blocks, "lat", flip_bit)
        chosen = jnp.take_along_axis(partner, pattern[level_idx][:, :, None, None], axis=1)
        blocks = combine_blocks(coupling[level_idx], blocks, chosen)
    order_count = lax.axis_size("order")
    local_orders = blocks.shape[0]
    per_peer = local_orders // order_count
    grouped = blocks.reshape((order_count, per_peer) + blocks.shape[1:])
    arrived = lax.all_to_all(grouped, "order", split_axis=0, concat_axis=0, tiled=True).reshape(
        blocks.shape
    )
    my_index = lax.axis_index("order")
    slot_table = assign.reshape(order_count, order_count, per_peer)
    my_orders = lax.dynamic_index_in_dim(slot_table, my_index, 1, keepdims=False).reshape(
        local_orders
    )
    my_orders = my_orders - my_index * local_orders
    inverse = (
        jnp.zeros((local_orders,), jnp.int32)
        .at[my_orders]
        .set(jnp.arange(local_orders, dtype=jnp.int32))
    )
    return jnp.take(arrived, inverse, axis=0)


def solution(mesh):
    return jax.shard_map(
        per_device,
        mesh=mesh,
        in_specs=(
            P("order", "lat", None, None),
            P(None, "order", "lat", None, None),
            P(None, "order", "lat"),
            P(),
        ),
        out_specs=P("order", "lat", None, None),
        check_vma=False,
    )
```

profile of v0, /device:TPU:32, one launch (start us, length us, event | category | flops | bytes accessed | tf_op | source)
XLA Modules:
  0.0 674.2 jit_solution(16640311660326927530)
XLA Ops:
  0.0 0.0 collective-permute-start
  0.0 8.5 %copy.52 = bf16[96,2,32,274]{3,2,1,0:T(8,128)(2,1)} copy(bf16[96,2,32,274]{0,2,3,1:T(8,128)(2,1)} %param.6) | data formatting | bytes 6733824 | tf_op args[0]
  8.5 0.0 copy-start
  8.5 4.3 fusion.44
  12.8 3.3 copy.72
  16.1 0.0 copy-done
  16.1 0.1 copy.54
  16.2 0.1 reshape.123
  16.3 0.1 copy.53
  16.5 7.3 %fusion.35 = f32[96,2,32,274]{3,2,1,0:T(8,128)} fusion(bf16[96,2,32,274]{3,2,1,0:T(8,128)(2,1)} %copy.52, bf16[96,2,32,64]{3,2,1,0:T(8,128)(2,1)S(1)} %bitcast.79), kind=kOutput, calls=%fused_computation.38 | convolution fusion | flops 107741184 | bytes 10887168 | tf_op jit(solution)/shard_map/obij,objc->obic/dot_general | solution.py:15
  23.8 0.0 collective-permute-done
  23.8 8.5 %copy.55 = bf16[96,2,32,274]{3,2,1,0:T(8,128)(2,1)} copy(bf16[96,2,32,274]{0,2,3,1:T(8,128)(2,1)} %collective-permute-done) | data formatting | bytes 6733824 | tf_op jit(solution)/shard_map/ppermute | solution.py:10
  32.3 6.8 %gather_fusion.1 = bf16[192,32,274]{2,1,0:T(8,128)(2,1)} fusion(bf16[96,2,32,274]{3,2,1,0:T(8,128)(2,1)} %copy.55, s32[192]{0:T(256)S(1)} %reshape.123), kind=kCustom, calls=%fused_computation.clone | custom fusion | bytes 6735360 | tf_op jit(solution)/shard_map/jit(take_along_axis)/gather | solution.py:30
  39.0 8.9 %fusion = bf16[96,2,32,274]{3,2,1,0:T(8,128)(2,1)} fusion(f32[96,2,32,274]{3,2,1,0:T(8,128)} %fusion.35, bf16[96,2,32,274]{3,2,1,0:T(8,128)(2,1)} %bitcast.75, pred[96,2]{1,0:T(8,128)(4,1)S(1)} %copy.53, bf16[96,2,32,64]{3,2,1,0:T(8,128)(2,1)S(1)} %bitcast.80), kind=kOutput, calls=%fused_computation.7 | convolution fusion | flops 112791552 | bytes 14254272 | tf_op jit(solution)/shard_map/obij,objc->obic/dot_general | solution.py:18
  47.9 8.8 %copy.58 = bf16[96,2,32,274]{0,2,3,1:T(8,128)(2,1)} copy(bf16[96,2,32,274]{3,2,1,0:T(8,128)(2,1)} %fusion) | data formatting | bytes 6733824 | tf_op jit(solution)/shard_map/convert_element_type | solution.py:21
  56.7 6.3 collective-permute-start.1
  63.0 3.3 copy.73
  66.3 0.1 copy.59
  66.4 0.1 reshape.128
  66.5 0.1 copy.57
  66.7 7.3 %fusion.32 = f32[96,2,274,32]{2,3,1,0:T(8,128)} fusion(bf16[96,2,32,274]{3,2,1,0:T(8,128)(2,1)} %fusion, bf16[96,2,32,64]{3,2,1,0:T(8,128)(2,1)S(1)} %bitcast.81), kind=kOutput, calls=%fused_computation.35 | convolution fusion | flops 107741184 | bytes 10887168 | tf_op jit(solution)/shard_map/obij,objc->obic/dot_general | solution.py:15
  74.0 173.5 %collective-permute-done.1 = bf16[96,2,32,274]{0,2,3,1:T(8,128)(2,1)} collective-permute-done((bf16[96,2,32,274]{0,2,3,1:T(8,128)(2,1)}, bf16[96,2,32,274]{0,2,3,1:T(8,128)(2,1)}, u32[]{:S(2)}, u32[]{:S(2)}) %collective-permute-start.1) | collective-permute-done | bytes 3366944 | tf_op jit(solution)/shard_map/ppermute | solution.py:10
  247.5 8.5 %copy.60 = bf16[96,2,32,274]{3,2,1,0:T(8,128)(2,1)} copy(bf16[96,2,32,274]{0,2,3,1:T(8,128)(2,1)} %collective-permute-done.1) | data formatting | bytes 6733824 | tf_op jit(solution)/shard_map/ppermute | solution.py:10
  255.9 6.8 %gather_fusion.2 = bf16[192,32,274]{2,1,0:T(8,128)(2,1)} fusion(bf16[96,2,32,274]{3,2,1,0:T(8,128)(2,1)} %copy.60, s32[192]{0:T(256)S(1)} %reshape.128), kind=kCustom, calls=%fused_computation.1.clone | custom fusion | bytes 6735360 | tf_op jit(solution)/shard_map/jit(take_along_axis)/gather | solution.py:30
  262.7 8.9 %add_convert_fusion.2 = bf16[96,2,274,32]{2,3,1,0:T(8,128)(2,1)} fusion(f32[96,2,274,32]{2,3,1,0:T(8,128)} %fusion.32, bf16[96,2,32,274]{3,2,1,0:T(8,128)(2,1)} %bitcast.76, pred[96,2]{1,0:T(8,128)(4,1)S(1)} %copy.57, bf16[96,2,32,64]{3,2,1,0:T(8,128)(2,1)S(1)} %bitcast.82), kind=kOutput, calls=%fused_computation.10 | convolution fusion | flops 112791552 | bytes 14254272 | tf_op jit(solution)/shard_map/obij,objc->obic/dot_general | solution.py:18
  271.6 8.8 %copy.63 = bf16[96,2,32,274]{0,2,3,1:T(8,128)(2,1)} copy(bf16[96,2,32,274]{3,2,1,0:T(8,128)(2,1)} %bitcast.73) | data formatting | bytes 6733824 | tf_op jit(solution)/shard_map/convert_element_type | solution.py:21
  280.4 1.3 collective-permute-start.2
  281.7 3.3 copy.74
  285.0 0.1 copy.64
  285.1 0.1 reshape.133
  285.2 0.1 copy.62
  285.4 7.3 %fusion.29 = f32[96,2,274,32]{2,3,1,0:T(8,128)} fusion(bf16[96,2,274,32]{2,3,1,0:T(8,128)(2,1)} %add_convert_fusion.2, bf16[96,2,32,64]{3,2,1,0:T(8,128)(2,1)S(1)} %bitcast.83), kind=kOutput, calls=%fused_computation.32 | convolution fusion | flops 107741184 | bytes 10887168 | tf_op jit(solution)/shard_map/obij,objc->obic/dot_general | solution.py:15
  292.7 86.4 %collective-permute-done.2 = bf16[96,2,32,274]{0,2,3,1:T(8,128)(2,1)} collective-permute-done((bf16[96,2,32,274]{0,2,3,1:T(8,128)(2,1)}, bf16[96,2,32,274]{0,2,3,1:T(8,128)(2,1)}, u32[]{:S(2)}, u32[]{:S(2)}) %collective-permute-start.2) | collective-permute-done | bytes 3366944 | tf_op jit(solution)/shard_map/ppermute | solution.py:10
  379.1 8.5 %copy.65 = bf16[96,2,32,274]{3,2,1,0:T(8,128)(2,1)} copy(bf16[96,2,32,274]{0,2,3,1:T(8,128)(2,1)} %collective-permute-done.2) | data formatting | bytes 6733824 | tf_op jit(solution)/shard_map/ppermute | solution.py:10
  387.6 6.8 %gather_fusion.3 = bf16[192,32,274]{2,1,0:T(8,128)(2,1)} fusion(bf16[96,2,32,274]{3,2,1,0:T(8,128)(2,1)} %copy.65, s32[192]{0:T(256)S(1)} %reshape.133), kind=kCustom, calls=%fused_computation.2.clone | custom fusion | bytes 6735360 | tf_op jit(solution)/shard_map/jit(take_along_axis)/gather | solution.py:30
  394.3 8.9 %add_convert_fusion.1 = bf16[96,2,274,32]{2,3,1,0:T(8,128)(2,1)} fusion(f32[96,2,274,32]{2,3,1,0:T(8,128)} %fusion.29, bf16[96,2,32,274]{3,2,1,0:T(8,128)(2,1)} %bitcast.77, pred[96,2]{1,0:T(8,128)(4,1)S(1)} %copy.62, bf16[96,2,32,64]{3,2,1,0:T(8,128)(2,1)S(1)} %bitcast.84), kind=kOutput, calls=%fused_computation.9 | convolution fusion | flops 112791552 | bytes 14254272 | tf_op jit(solution)/shard_map/obij,objc->obic/dot_general | solution.py:18
  403.2 8.8 %copy.68 = bf16[96,2,32,274]{0,2,3,1:T(8,128)(2,1)} copy(bf16[96,2,32,274]{3,2,1,0:T(8,128)(2,1)} %bitcast.72) | data formatting | bytes 6733824 | tf_op jit(solution)/shard_map/convert_element_type | solution.py:21
  412.0 3.2 collective-permute-start.3
  415.2 0.1 copy.69
  415.3 0.1 reshape.138
  415.4 2.4 copy.75
  417.8 0.1 copy.67
  417.9 7.3 %fusion.26 = f32[96,2,274,32]{2,3,1,0:T(8,128)} fusion(bf16[96,2,274,32]{2,3,1,0:T(8,128)(2,1)} %add_convert_fusion.1, bf16[96,2,32,64]{3,2,1,0:T(8,128)(2,1)S(1)} %bitcast.85), kind=kOutput, calls=%fused_computation.29 | convolution fusion | flops 107741184 | bytes 10887168 | tf_op jit(solution)/shard_map/obij,objc->obic/dot_general | solution.py:15
  425.2 86.1 %collective-permute-done.3 = bf16[96,2,32,274]{0,2,3,1:T(8,128)(2,1)} collective-permute-done((bf16[96,2,32,274]{0,2,3,1:T(8,128)(2,1)}, bf16[96,2,32,274]{0,2,3,1:T(8,128)(2,1)}, u32[]{:S(2)}, u32[]{:S(2)}) %collective-permute-start.3) | collective-permute-done | bytes 3366944 | tf_op jit(solution)/shard_map/ppermute | solution.py:10
  511.4 8.5 %copy.70 = bf16[96,2,32,274]{3,2,1,0:T(8,128)(2,1)} copy(bf16[96,2,32,274]{0,2,3,1:T(8,128)(2,1)} %collective-permute-done.3) | data formatting | bytes 6733824 | tf_op jit(solution)/shard_map/ppermute | solution.py:10
  519.9 6.9 %gather_fusion.4 = bf16[192,32,274]{2,1,0:T(8,128)(2,1)} fusion(bf16[96,2,32,274]{3,2,1,0:T(8,128)(2,1)} %copy.70, s32[192]{0:T(256)S(1)} %reshape.138), kind=kCustom, calls=%fused_computation.3.clone | custom fusion | bytes 6735360 | tf_op jit(solution)/shard_map/jit(take_along_axis)/gather | solution.py:30
  526.8 8.8 %add_convert_fusion = bf16[96,2,274,32]{2,3,1,0:T(8,128)(2,1)} fusion(f32[96,2,274,32]{2,3,1,0:T(8,128)} %fusion.26, bf16[96,2,32,274]{3,2,1,0:T(8,128)(2,1)} %bitcast.78, pred[96,2]{1,0:T(8,128)(4,1)S(1)} %copy.67, bf16[96,2,32,64]{3,2,1,0:T(8,128)(2,1)S(1)} %bitcast.86), kind=kOutput, calls=%fused_computation.8 | convolution fusion | flops 112791552 | bytes 14254272 | tf_op jit(solution)/shard_map/obij,objc->obic/dot_general | solution.py:18
  535.5 0.0 copy-start.1
  535.5 19.7 %all-to-all-start = ((bf16[16,6,2,32,274]{4,3,2,1,0:T(8,128)(2,1)}), bf16[16,6,2,32,274]{4,3,2,1,0:T(8,128)(2,1)}, u32[]{:S(2)}, u32[]{:S(2)}) async-start(bf16[16,6,2,32,274]{4,3,2,1,0:T(8,128)(2,1)} %bitcast.74), calls=%async_computation | async-start | bytes 9437184 | tf_op jit(solution)/shard_map/all_to_all | solution.py:36
  555.2 0.0 copy-done.1
  555.2 0.1 reshape.55
  555.4 0.1 sub.18
  555.5 0.9 scatter_custom_fusion
  556.4 97.9 %all-to-all-done = bf16[16,6,2,32,274]{4,3,2,1,0:T(8,128)(2,1)} async-done(((bf16[16,6,2,32,274]{4,3,2,1,0:T(8,128)(2,1)}), bf16[16,6,2,32,274]{4,3,2,1,0:T(8,128)(2,1)}, u32[]{:S(2)}, u32[]{:S(2)}) %all-to-all-start) | async-done | bytes 3366944 | tf_op jit(solution)/shard_map/all_to_all | solution.py:36
  654.4 6.0 gather_fusion
  660.3 5.1 broadcast_select_fusion
  665.4 8.8 %copy.71 = bf16[96,2,32,274]{0,2,3,1:T(8,128)(2,1)} copy(bf16[96,2,32,274]{3,2,1,0:T(8,128)(2,1)} %broadcast_select_fusion) | data formatting | bytes 6733824 | tf_op jit(solution)/shard_map/jit(_take)/select_n | solution.py:50
  (8 shorter events, 0.1 us)
Async XLA Ops:
  0.0 23.8 %collective-permute-start = (bf16[96,2,32,274]{0,2,3,1:T(8,128)(2,1)}, bf16[96,2,32,274]{0,2,3,1:T(8,128)(2,1)}, u32[]{:S(2)}, u32[]{:S(2)}) collective-permute-start(bf16[96,2,32,274]{0,2,3,1:T(8,128)(2,1)} %param.6), channel_id=1, source_target_pairs={{0,1},{1,0},{2,3},{3,2},{4,5},{5,4},{6,7},{7,6},{8,9},{9,8},{10,11... | collective-permute-start | bytes 10100744 | tf_op jit(solution)/shard_map/ppermute | solution.py:10
  8.5 7.6 %copy-start = (s32[4,96,2]{1,2,0:T(2,128)S(1)}, s32[4,96,2]{1,2,0:T(2,128)}, u32[]{:S(2)}) copy-start(s32[4,96,2]{1,2,0:T(2,128)} %param.8) | copy-start | bytes 9220
  56.7 190.8 %collective-permute-start.1 = (bf16[96,2,32,274]{0,2,3,1:T(8,128)(2,1)}, bf16[96,2,32,274]{0,2,3,1:T(8,128)(2,1)}, u32[]{:S(2)}, u32[]{:S(2)}) collective-permute-start(bf16[96,2,32,274]{0,2,3,1:T(8,128)(2,1)} %copy.58), channel_id=1, source_target_pairs={{0,2},{1,3},{2,0},{3,1},{4,6},{5,7},{6,4},{7,5},{8,10},{9,11},{10,... | collective-permute-start | bytes 10100744 | tf_op jit(solution)/shard_map/ppermute | solution.py:10
  280.4 98.7 %collective-permute-start.2 = (bf16[96,2,32,274]{0,2,3,1:T(8,128)(2,1)}, bf16[96,2,32,274]{0,2,3,1:T(8,128)(2,1)}, u32[]{:S(2)}, u32[]{:S(2)}) collective-permute-start(bf16[96,2,32,274]{0,2,3,1:T(8,128)(2,1)} %copy.63), channel_id=1, source_target_pairs={{0,4},{1,5},{2,6},{3,7},{4,0},{5,1},{6,2},{7,3},{8,12},{9,13},{10,... | collective-permute-start | bytes 10100744 | tf_op jit(solution)/shard_map/ppermute | solution.py:10
  412.0 99.3 %collective-permute-start.3 = (bf16[96,2,32,274]{0,2,3,1:T(8,128)(2,1)}, bf16[96,2,32,274]{0,2,3,1:T(8,128)(2,1)}, u32[]{:S(2)}, u32[]{:S(2)}) collective-permute-start(bf16[96,2,32,274]{0,2,3,1:T(8,128)(2,1)} %copy.68), channel_id=1, source_target_pairs={{0,8},{1,9},{2,10},{3,11},{4,12},{5,13},{6,14},{7,15},{8,0},{9,1},... | collective-permute-start | bytes 10100744 | tf_op jit(solution)/shard_map/ppermute | solution.py:10
  535.5 19.7 %copy-start.1 = (s32[1536]{0:T(1024)S(1)}, s32[1536]{0:T(1024)}, u32[]{:S(2)}) copy-start(s32[1536]{0:T(1024)} %param.9) | copy-start | bytes 18436
  535.5 118.8 %all-to-all-start = ((bf16[16,6,2,32,274]{4,3,2,1,0:T(8,128)(2,1)}), bf16[16,6,2,32,274]{4,3,2,1,0:T(8,128)(2,1)}, u32[]{:S(2)}, u32[]{:S(2)}) async-start(bf16[16,6,2,32,274]{4,3,2,1,0:T(8,128)(2,1)} %bitcast.74), calls=%async_computation | async-start | bytes 9437184 | tf_op jit(solution)/shard_map/all_to_all | solution.py:36
where the time goes:
time: 679 us; the launch traced here: 674 us
  waiting for transfers between devices  444 us (65%)
  local copies, waits for them, and re-layouts  130 us (19%)
  matrix products  64.7 us (10%)
  starting transfers between devices  30.5 us (4%)
    ppermute x4, waiting for transfers between devices, from_partner(): lax.ppermute(value, axis, [(i, i ^ 1 << bit) for i in range(lax.axis_size...  346 us
    all_to_all x1, waiting for transfers between devices, per_device(): lax.all_to_all(grouped, 'order', split_axis=0, concat_axis=0, tiled=True)  97.9 us
    dot_general x4, matrix products, combine_blocks(): jnp.einsum('obij,objc->obic', weights[..., rank_size:], far_part, preferr...  35.4 us
    ppermute x4, local copies, waits for them, and re-layouts, from_partner(): lax.ppermute(value, axis, [(i, i ^ 1 << bit) for i in range(lax.axis_size...  33.9 us
    dot_general x4, matrix products, combine_blocks(): jnp.einsum('obij,objc->obic', weights[..., :rank_size], own_part, preferr...  29.3 us
    gather x12, local copies, waits for them, and re-layouts, per_device(): jnp.take_along_axis(partner, pattern[level_idx][:, :, None, None], axis=1)  28.1 us
    convert_element_type x3, local copies, waits for them, and re-layouts, combine_blocks(): return total.astype(jnp.bfloat16)  26.4 us
    unnamed x9, local copies, waits for them, and re-layouts  20.7 us
  transfers between devices with their start and end apart: 5, of which 4 were waited for; matrix products, arithmetic and copies ran while one was open for 8% of the time, Pallas kernels for 0%

commit v1 on v0

v1 whole, which is shorter than its diff:
```python
import functools

import jax
import jax.numpy as jnp
from jax import lax
from jax.experimental import pallas as pl
from jax.experimental.pallas import tpu as pltpu
from jax.sharding import PartitionSpec as P

LEVELS = 4
LANES = 128


def from_partner(value, bit):
    size = lax.axis_size("lat")
    return lax.ppermute(value, "lat", [(i, i ^ 1 << bit) for i in range(size)])


def level_kernel(spec, lev, tail_w, pat_ref, w_ref, *refs):
    n_in = spec["n_in"]
    own, far, outs = refs[:n_in], refs[n_in : 2 * n_in], refs[2 * n_in :]
    groups, per_peer = w_ref.shape[0], w_ref.shape[1]
    boxes = w_ref.shape[2]
    lane = lax.broadcasted_iota(jnp.int32, (w_ref.shape[3], LANES), 1)
    base = pl.program_id(0) * groups
    total = pl.num_programs(0) * groups * per_peer

    def group(c, carry):
        for out, slots in zip(outs, spec["slots"]):
            for at, slot in enumerate(slots):
                for g in range(boxes):

                    def product(order, src, idx):
                        sel = pat_ref[(lev * total + (base + c) * per_peer + order) * boxes + g]
                        rhs = jnp.concatenate([own[src][c, idx, g], far[src][c, idx, sel]], axis=0)
                        return jnp.dot(w_ref[c, order, g], rhs, preferred_element_type=jnp.float32)

                    if slot[0] == "m":
                        acc = product(slot[3], slot[1], slot[2])
                    else:
                        acc = product(0, slot[1], slot[2])
                        for j in range(1, per_peer):
                            acc = jnp.where(lane < j * tail_w, acc, product(j, slot[1], slot[2]))
                    out[c, at, g] = acc.astype(jnp.bfloat16)
        return carry

    lax.fori_loop(0, groups, group, 0)


def run_level(lev, tail_w, slots, pattern, weights, own, far, steps=4):
    peers, per_peer, boxes, rank, _ = weights.shape
    step = peers // steps
    spec = {"n_in": len(own), "slots": slots}
    blk = lambda shape: pl.BlockSpec((step,) + tuple(shape[1:]), lambda i, p: (i,) + (0,) * (len(shape) - 1))
    out_shapes = [jax.ShapeDtypeStruct((peers, len(s), boxes, rank, LANES), jnp.bfloat16) for s in slots]
    dots = sum(sum(1 if x[0] == "m" else per_peer for x in s) for s in slots) * peers * boxes
    moved = sum(a.size for a in (*own, *far, weights)) * 2 + sum(o.size for o in out_shapes) * 2
    return pl.pallas_call(
        functools.partial(level_kernel, spec, lev, tail_w),
        grid_spec=pltpu.PrefetchScalarGridSpec(
            num_scalar_prefetch=1,
            grid=(steps,),
            in_specs=[blk(weights.shape)] + [blk(a.shape) for a in (*own, *far)],
            out_specs=[blk(o.shape) for o in out_shapes],
        ),
        out_shape=out_shapes,
        cost_estimate=pl.CostEstimate(
            flops=dots * 2 * rank * 2 * rank * LANES, bytes_accessed=moved, transcendentals=0
        ),
    )(pattern, weights, *own, *far)


def place_kernel(tail_w, n_main, me_ref, assign_ref, *refs):
    ins, out_ref = refs[:-1], refs[-1]
    peers = ins[0].shape[0]
    per_peer = n_main
    boxes, rank = ins[0].shape[2], ins[0].shape[3]
    local = peers * per_peer
    me = me_ref[0]
    half = per_peer // 2

    def peer(k, carry):
        for j in range(per_peer):
            to = assign_ref[k * local + me * per_peer + j] - me * local
            for g in range(boxes):
                a = ins[j // half][k, j % half, g]
                b = ins[2][k, 1 + j, g] if j < half else ins[3][k, j - half, g]
                t = ins[2][k, 0, g].astype(jnp.float32)
                if j:
                    t = pltpu.roll(t, LANES - j * tail_w, 1)
                out_ref[to, g, :, 0:LANES] = a
                out_ref[to, g, :, LANES : 2 * LANES] = b
                out_ref[to, g, :, 2 * LANES : 2 * LANES + tail_w] = t[:, :tail_w].astype(jnp.bfloat16)
        return carry

    lax.fori_loop(0, peers, peer, 0)


def place(tail_w, me, assign, parts, cols):
    peers, _, boxes, rank, _ = parts[0].shape
    per_peer = parts[0].shape[1] * 2
    local = peers * per_peer
    vmem = pl.BlockSpec(memory_space=pltpu.VMEM)
    smem = pl.BlockSpec(memory_space=pltpu.SMEM)
    return pl.pallas_call(
        functools.partial(place_kernel, tail_w, per_peer),
        in_specs=[smem, smem] + [vmem] * len(parts),
        out_specs=vmem,
        out_shape=jax.ShapeDtypeStruct((local, boxes, rank, cols), jnp.bfloat16),
        compiler_params=pltpu.CompilerParams(vmem_limit_bytes=32 << 20),
        cost_estimate=pl.CostEstimate(
            flops=0, bytes_accessed=4 * local * boxes * rank * cols, transcendentals=0
        ),
    )(me, assign, *parts)


def per_device(coeffs, coupling, pattern, assign):
    local, boxes, rank, cols = coeffs.shape
    peers = lax.axis_size("order")
    per_peer = local // peers
    half = per_peer // 2
    tail_w = cols - 2 * LANES
    flat_pattern = pattern.reshape(-1)
    weights = [
        coupling[l].reshape(peers, per_peer, boxes, rank, 2 * rank) for l in range(LEVELS)
    ]

    def six(x):
        return x.reshape(peers, per_peer, boxes, rank, x.shape[-1])

    first = six(coeffs[..., :LANES])
    second = six(coeffs[..., LANES : 2 * LANES])
    tail = six(coeffs[..., 2 * LANES :]).transpose(0, 2, 3, 1, 4).reshape(peers, boxes, rank, per_peer * tail_w)
    tail = jnp.pad(tail, ((0, 0), (0, 0), (0, 0), (0, LANES - per_peer * tail_w)))[:, None]

    low = range(half)
    high = range(half, per_peer)
    a0, a1 = run_level(
        0, tail_w, [[("m", 0, j, j) for j in low], [("m", 0, j, j) for j in high]],
        flat_pattern, weights[0], [first], [from_partner(first, 0)],
    )
    b0, b1 = run_level(
        0, tail_w,
        [[("t", 1, 0)] + [("m", 0, j, j) for j in low], [("m", 0, j, j) for j in high]],
        flat_pattern, weights[0], [second, tail], [from_partner(second, 0), from_partner(tail, 0)],
    )
    chunks = [a0, a1, b0, b1]
    slot_lists = [
        [("m", 0, j, j) for j in low],
        [("m", 0, j - half, j) for j in high],
        [("t", 0, 0)] + [("m", 0, 1 + j, j) for j in low],
        [("m", 0, j - half, j) for j in high],
    ]
    done = []
    for chunk, slots in zip(chunks, slot_lists):
        for lev in range(1, LEVELS):
            far = from_partner(chunk, lev)
            (chunk,) = run_level(lev, tail_w, [slots], flat_pattern, weights[lev], [chunk], [far])
        done.append(lax.all_to_all(chunk, "order", split_axis=0, concat_axis=0, tiled=True))
    me = lax.axis_index("order").astype(jnp.int32).reshape(1)
    return place(tail_w, me, assign, done, cols)


def solution(mesh):
    return jax.shard_map(
        per_device,
        mesh=mesh,
        in_specs=(
            P("order", "lat", None, None),
            P(None, "order", "lat", None, None),
            P(None, "order", "lat"),
            P(),
        ),
        out_specs=P("order", "lat", None, None),
        check_vma=False,
    )
```

time: 679 us -> 384 us (0.57)
  waiting for transfers between devices: 444 us -> 181 us
  Pallas kernels: 0 us -> 85.6 us
  local copies, waits for them, and re-layouts: 130 us -> 51.8 us
  matrix products: 64.7 us -> 0 us
  starting transfers between devices: 30.5 us -> 62.9 us
    ppermute x4 -> x15, waiting for transfers between devices: 346 us -> 107 us  [from_partner(): return lax.ppermute(value, 'lat', [(i, i ^ 1 << bit) for i in range(size)])]
    pallas_call x0 -> x15, Pallas kernels: none -> 85.6 us  [the longest x14 83.4 us: run_level(): pl.pallas_call(functools.partial(level_kernel, spec, lev, tail_w), grid_s...]
    dot_general x8 -> x0, matrix products: 64.7 us -> none  [the longest x4 35.4 us: combine_blocks(): jnp.einsum('obij,objc->obic', weights[..., rank_size:], far_part, preferr...]
    gather x13 -> x0, local copies, waits for them, and re-layouts: 34.1 us -> none  [the longest x12 28.1 us: per_device(): jnp.take_along_axis(partner, pattern[level_idx][:, :, None, None], axis=1)]
    ppermute x4 -> x0, local copies, waits for them, and re-layouts: 33.9 us -> none  [from_partner(): lax.ppermute(value, axis, [(i, i ^ 1 << bit) for i in range(lax.axis_size...]
    slice x1 -> x11, local copies, waits for them, and re-layouts: 4.29 us -> 31.4 us  [the longest x5 17.7 us: per_device(): coupling[l].reshape(peers, per_peer, boxes, rank, 2 * rank)]
    convert_element_type x3 -> x0, local copies, waits for them, and re-layouts: 26.4 us -> none  [combine_blocks(): return total.astype(jnp.bfloat16)]
    ppermute x4 -> x15, starting transfers between devices: 10.8 us -> 36.9 us  [from_partner(): return lax.ppermute(value, 'lat', [(i, i ^ 1 << bit) for i in range(size)])]
  transfers between devices with their start and end apart: 5 -> 19, of which waited for: 4 -> 9; matrix products, arithmetic and copies ran while one was open for 8% -> 7% of each run, Pallas kernels for 0% -> 22%
where the time goes in v1:
time: 384 us; the launch traced here: 382 us
  waiting for transfers between devices  181 us (47%)
  Pallas kernels  85.6 us (22%)
  starting transfers between devices  62.9 us (16%)
  local copies, waits for them, and re-layouts  51.8 us (13%)
    ppermute x15, waiting for transfers between devices, from_partner(): return lax.ppermute(value, 'lat', [(i, i ^ 1 << bit) for i in range(size)])  107 us
    pallas_call x14, Pallas kernels, run_level(): pl.pallas_call(functools.partial(level_kernel, spec, lev, tail_w), grid_s...  83.4 us
    all_to_all x4, waiting for transfers between devices, per_device(): lax.all_to_all(chunk, 'order', split_axis=0, concat_axis=0, tiled=True)  73.7 us
    ppermute x15, starting transfers between devices, from_partner(): return lax.ppermute(value, 'lat', [(i, i ^ 1 << bit) for i in range(size)])  36.9 us
    all_to_all x4, starting transfers between devices, per_device(): lax.all_to_all(chunk, 'order', split_axis=0, concat_axis=0, tiled=True)  26 us
    slice x5, local copies, waits for them, and re-layouts, per_device(): coupling[l].reshape(peers, per_peer, boxes, rank, 2 * rank)  17.7 us
    slice x2, local copies, waits for them, and re-layouts, per_device(): second = six(coeffs[..., LANES:2 * LANES])  9.5 us
    pallas_call x1, local copies, waits for them, and re-layouts, place(): pl.pallas_call(functools.partial(place_kernel, tail_w, per_peer), in_spec...  8.79 us
  transfers between devices with their start and end apart: 19, of which 9 were waited for; matrix products, arithmetic and copies ran while one was open for 7% of the time, Pallas kernels for 22%

profile of v1, /device:TPU:32, one launch (start us, length us, event | category | flops | bytes accessed | tf_op | source)
XLA Modules:
  0.0 381.7 jit_solution(2284295233650434883)
XLA Ops:
  0.0 4.4 %fusion = (bf16[96,2,32,128]{0,2,3,1:T(8,128)(2,1)}, bf16[96,2,32,128]{0,2,3,1:T(8,128)(2,1)S(1)}) fusion(bf16[96,2,32,274]{0,2,3,1:T(8,128)(2,1)} %param.4), kind=kLoop, calls=%fused_computation.1 | loop fusion | bytes 6291456 | tf_op jit(solution)/shard_map/slice | solution.py:132
  4.4 5.1 %copy.19 = bf16[96,2,32,128]{3,2,1,0:T(8,128)(2,1)} copy(bf16[96,2,32,128]{0,2,3,1:T(8,128)(2,1)} %get-tuple-element.13) | data formatting | bytes 3145728 | tf_op jit(solution)/shard_map/slice | solution.py:132
  9.5 0.0 collective-permute-start.7
  9.5 0.7 copy.20
  10.2 1.4 copy.22
  11.5 0.1 pad_bitcast_fusion.refs_1_
  11.6 0.6 collective-permute-start.8
  12.2 3.5 copy.18
  15.8 0.0 collective-permute-start
  15.8 4.5 %fusion.1 = (bf16[1,96,2,32,64]{1,4,3,2,0:T(8,128)(2,1)}, bf16[1,96,2,32,64]{1,4,3,2,0:T(8,128)(2,1)S(1)}, bf16[1,96,2,32,64]{1,4,3,2,0:T(8,128)(2,1)S(1)}, bf16[1,96,2,32,64]{1,4,3,2,0:T(8,128)(2,1)S(1)}) fusion(bf16[4,96,2,32,64]{1,4,3,2,0:T(8,128)(2,1)} %param.5), kind=kLoop, calls=%fused_computation.2 | loop fusion | bytes 6291456 | tf_op jit(solution)/shard_map/slice | solution.py:125
  20.3 0.8 copy.13
  21.1 1.7 reshape.19.pat_ref
  22.8 4.0 %copy.17 = bf16[1,96,2,32,64]{4,3,2,1,0:T(8,128)(2,1)} copy(bf16[1,96,2,32,64]{1,4,3,2,0:T(8,128)(2,1)} %get-tuple-element.15) | data formatting | bytes 1572864 | tf_op jit(solution)/shard_map/slice | solution.py:125
  26.8 7.0 %shard_map.53 = (bf16[16,4,2,32,128]{4,3,2,1,0:T(8,128)(2,1)}, bf16[16,3,2,32,128]{4,3,2,1,0:T(8,128)(2,1)}) custom-call(s32[768]{0:T(1024)} %reshape.19.pat_ref, bf16[16,6,2,32,64]{4,3,2,1,0:T(8,128)(2,1)} %bitcast.26, bf16[16,6,2,32,128]{4,3,2,1,0:T(8,128)(2,1)} %bitcast.31, bf16[16,1,2,32,128]{4,3,2,1,0:T(8,128)(2,1)} %copy-done.2, ...), custom_call_target="tpu_custom_call" | custom-call | flops 201326592 | bytes 6291456 | tf_op jit(solution)/shard_map/pallas_call | solution.py:58
  33.8 6.3 %collective-permute-start.12 = (bf16[16,3,2,32,128]{4,3,2,1,0:T(8,128)(2,1)}, bf16[16,3,2,32,128]{4,3,2,1,0:T(8,128)(2,1)}, u32[]{:S(2)}, u32[]{:S(2)}) collective-permute-start(bf16[16,3,2,32,128]{4,3,2,1,0:T(8,128)(2,1)} %get-tuple-element.12.refs_0_), channel_id=1, source_target_pairs={{0,2},{1,3},{2,0},{3,1},{4,6},{5,7},{6,4},{7,5},{8,10},{9,11},{10,... | collective-permute-start | bytes 2359304 | tf_op jit(solution)/shard_map/ppermute | solution.py:16
  40.1 3.1 copy.16
  43.2 32.4 %collective-permute-done.12.refs_1_ = bf16[16,3,2,32,128]{4,3,2,1,0:T(8,128)(2,1)} collective-permute-done((bf16[16,3,2,32,128]{4,3,2,1,0:T(8,128)(2,1)}, bf16[16,3,2,32,128]{4,3,2,1,0:T(8,128)(2,1)}, u32[]{:S(2)}, u32[]{:S(2)}) %collective-permute-start.12) | collective-permute-done | bytes 786464 | tf_op jit(solution)/shard_map/ppermute | solution.py:16
  75.6 5.6 %shard_map.57.refs_0_ = bf16[16,3,2,32,128]{4,3,2,1,0:T(8,128)(2,1)} custom-call(s32[768]{0:T(1024)} %reshape.19.pat_ref, bf16[16,6,2,32,64]{4,3,2,1,0:T(8,128)(2,1)} %bitcast.18, bf16[16,3,2,32,128]{4,3,2,1,0:T(8,128)(2,1)} %get-tuple-element.12.refs_0_, bf16[16,3,2,32,128]{4,3,2,1,0:T(8,128)(2,1)} %collective-permute-done.12.refs_1_), custom_call_target="tpu_custom_call" | custom-call | flops 50331648 | bytes 3145728 | tf_op jit(solution)/shard_map/pallas_call | solution.py:58
  81.2 1.6 collective-permute-start.13
  82.8 6.4 %shard_map.46 = (bf16[16,3,2,32,128]{4,3,2,1,0:T(8,128)(2,1)}, bf16[16,3,2,32,128]{4,3,2,1,0:T(8,128)(2,1)}) custom-call(s32[768]{0:T(1024)} %reshape.19.pat_ref, bf16[16,6,2,32,64]{4,3,2,1,0:T(8,128)(2,1)} %bitcast.27, bf16[16,6,2,32,128]{4,3,2,1,0:T(8,128)(2,1)} %bitcast.29, bf16[16,6,2,32,128]{4,3,2,1,0:T(8,128)(2,1)} %collective-permute-done.refs_1_), custom_call_target="tpu_custom_call" | custom-call | flops 100663296 | bytes 5505024 | tf_op jit(solution)/shard_map/pallas_call | solution.py:58
  89.1 5.5 %collective-permute-start.4 = (bf16[16,3,2,32,128]{4,3,2,1,0:T(8,128)(2,1)}, bf16[16,3,2,32,128]{4,3,2,1,0:T(8,128)(2,1)}, u32[]{:S(2)}, u32[]{:S(2)}) collective-permute-start(bf16[16,3,2,32,128]{4,3,2,1,0:T(8,128)(2,1)} %get-tuple-element.10.refs_0_), channel_id=1, source_target_pairs={{0,2},{1,3},{2,0},{3,1},{4,6},{5,7},{6,4},{7,5},{8,10},{9,11},{10,... | collective-permute-start | bytes 2359304 | tf_op jit(solution)/shard_map/ppermute | solution.py:16
  94.6 3.1 copy.15
  97.7 2.9 collective-permute-done.13.refs_1_
  100.6 0.9 copy-done.9
  101.5 5.6 %shard_map.58.refs_0_ = bf16[16,3,2,32,128]{4,3,2,1,0:T(8,128)(2,1)} custom-call(s32[768]{0:T(1024)} %reshape.19.pat_ref, bf16[16,6,2,32,64]{4,3,2,1,0:T(8,128)(2,1)} %bitcast.14, bf16[16,3,2,32,128]{4,3,2,1,0:T(8,128)(2,1)} %shard_map.57.refs_0_, bf16[16,3,2,32,128]{4,3,2,1,0:T(8,128)(2,1)} %copy-done.9), custom_call_target="tpu_custom_call" | custom-call | flops 50331648 | bytes 3145728 | tf_op jit(solution)/shard_map/pallas_call | solution.py:58
  107.1 3.2 collective-permute-start.14
  110.3 14.7 %collective-permute-done.4.refs_1_ = bf16[16,3,2,32,128]{4,3,2,1,0:T(8,128)(2,1)} collective-permute-done((bf16[16,3,2,32,128]{4,3,2,1,0:T(8,128)(2,1)}, bf16[16,3,2,32,128]{4,3,2,1,0:T(8,128)(2,1)}, u32[]{:S(2)}, u32[]{:S(2)}) %collective-permute-start.4) | collective-permute-done | bytes 786464 | tf_op jit(solution)/shard_map/ppermute | solution.py:16
  125.0 5.6 %shard_map.50.refs_0_ = bf16[16,3,2,32,128]{4,3,2,1,0:T(8,128)(2,1)} custom-call(s32[768]{0:T(1024)} %reshape.19.pat_ref, bf16[16,6,2,32,64]{4,3,2,1,0:T(8,128)(2,1)} %bitcast.19, bf16[16,3,2,32,128]{4,3,2,1,0:T(8,128)(2,1)} %get-tuple-element.10.refs_0_, bf16[16,3,2,32,128]{4,3,2,1,0:T(8,128)(2,1)} %collective-permute-done.4.refs_1_), custom_call_target="tpu_custom_call" | custom-call | flops 50331648 | bytes 3145728 | tf_op jit(solution)/shard_map/pallas_call | solution.py:58
  130.6 0.5 collective-permute-start.5
  131.1 3.0 copy.14
  134.1 0.9 copy-done.10
  135.0 5.8 %shard_map.59 = bf16[16,3,2,32,128]{4,3,2,1,0:T(8,128)(2,1)} custom-call(s32[768]{0:T(1024)} %reshape.19.pat_ref, bf16[16,6,2,32,64]{4,3,2,1,0:T(8,128)(2,1)} %bitcast.22, bf16[16,3,2,32,128]{4,3,2,1,0:T(8,128)(2,1)} %shard_map.58.refs_0_, bf16[16,3,2,32,128]{4,3,2,1,0:T(8,128)(2,1)} %copy-done.10), custom_call_target="tpu_custom_call" | custom-call | flops 50331648 | bytes 3145728 | tf_op jit(solution)/shard_map/pallas_call | solution.py:58
  140.8 5.8 %all-to-all-start.3 = ((bf16[16,3,2,32,128]{4,3,2,1,0:T(8,128)(2,1)}), bf16[16,3,2,32,128]{4,3,2,1,0:T(8,128)(2,1)S(1)}, u32[]{:S(2)}, u32[]{:S(2)}) async-start(bf16[16,3,2,32,128]{4,3,2,1,0:T(8,128)(2,1)} %shard_map.59), calls=%async_computation.3 | async-start | bytes 1572864 | tf_op jit(solution)/shard_map/all_to_all | solution.py:159
  146.5 5.6 %collective-permute-start.1 = (bf16[16,3,2,32,128]{4,3,2,1,0:T(8,128)(2,1)S(1)}, bf16[16,3,2,32,128]{4,3,2,1,0:T(8,128)(2,1)}, u32[]{:S(2)}, u32[]{:S(2)}) collective-permute-start(bf16[16,3,2,32,128]{4,3,2,1,0:T(8,128)(2,1)S(1)} %copy-done.6), channel_id=1, source_target_pairs={{0,2},{1,3},{2,0},{3,1},{4,6},{5,7},{6,4},{7,5},{8,10},{9,11},{10,... | collective-permute-start | bytes 2359304 | tf_op jit(solution)/shard_map/ppermute | solution.py:16
  152.2 1.0 copy-done.7
  153.1 5.6 %shard_map.51.refs_0_ = bf16[16,3,2,32,128]{4,3,2,1,0:T(8,128)(2,1)} custom-call(s32[768]{0:T(1024)} %reshape.19.pat_ref, bf16[16,6,2,32,64]{4,3,2,1,0:T(8,128)(2,1)} %bitcast.15, bf16[16,3,2,32,128]{4,3,2,1,0:T(8,128)(2,1)} %shard_map.50.refs_0_, bf16[16,3,2,32,128]{4,3,2,1,0:T(8,128)(2,1)} %copy-done.7), custom_call_target="tpu_custom_call" | custom-call | flops 50331648 | bytes 3145728 | tf_op jit(solution)/shard_map/pallas_call | solution.py:58
  158.8 3.2 collective-permute-start.6
  162.0 3.2 collective-permute-start.9
  165.2 16.0 %collective-permute-done.1.refs_1_ = bf16[16,3,2,32,128]{4,3,2,1,0:T(8,128)(2,1)} collective-permute-done((bf16[16,3,2,32,128]{4,3,2,1,0:T(8,128)(2,1)S(1)}, bf16[16,3,2,32,128]{4,3,2,1,0:T(8,128)(2,1)}, u32[]{:S(2)}, u32[]{:S(2)}) %collective-permute-start.1) | collective-permute-done | bytes 786464 | tf_op jit(solution)/shard_map/ppermute | solution.py:16
  181.2 5.6 %shard_map.47.refs_0_ = bf16[16,3,2,32,128]{4,3,2,1,0:T(8,128)(2,1)} custom-call(s32[768]{0:T(1024)} %reshape.19.pat_ref, bf16[16,6,2,32,64]{4,3,2,1,0:T(8,128)(2,1)} %bitcast.20, bf16[16,3,2,32,128]{4,3,2,1,0:T(8,128)(2,1)} %get-tuple-element.9.refs_0_, bf16[16,3,2,32,128]{4,3,2,1,0:T(8,128)(2,1)} %collective-permute-done.1.refs_1_), custom_call_target="tpu_custom_call" | custom-call | flops 50331648 | bytes 3145728 | tf_op jit(solution)/shard_map/pallas_call | solution.py:58
  186.8 1.6 collective-permute-start.2
  188.4 5.6 %shard_map.52 = bf16[16,3,2,32,128]{4,3,2,1,0:T(8,128)(2,1)} custom-call(s32[768]{0:T(1024)} %reshape.19.pat_ref, bf16[16,6,2,32,64]{4,3,2,1,0:T(8,128)(2,1)} %bitcast.23, bf16[16,3,2,32,128]{4,3,2,1,0:T(8,128)(2,1)} %shard_map.51.refs_0_, bf16[16,3,2,32,128]{4,3,2,1,0:T(8,128)(2,1)} %collective-permute-done.6.refs_1_), custom_call_target="tpu_custom_call" | custom-call | flops 50331648 | bytes 3145728 | tf_op jit(solution)/shard_map/pallas_call | solution.py:58
  194.0 51.2 %all-to-all-done.3.refs_3_ = bf16[16,3,2,32,128]{4,3,2,1,0:T(8,128)(2,1)S(1)} async-done(((bf16[16,3,2,32,128]{4,3,2,1,0:T(8,128)(2,1)}), bf16[16,3,2,32,128]{4,3,2,1,0:T(8,128)(2,1)S(1)}, u32[]{:S(2)}, u32[]{:S(2)}) %all-to-all-start.3) | async-done | bytes 786464 | tf_op jit(solution)/shard_map/all_to_all | solution.py:159
  245.3 5.1 %all-to-all-start.1 = ((bf16[16,3,2,32,128]{4,3,2,1,0:T(8,128)(2,1)}), bf16[16,3,2,32,128]{4,3,2,1,0:T(8,128)(2,1)S(1)}, u32[]{:S(2)}, u32[]{:S(2)}) async-start(bf16[16,3,2,32,128]{4,3,2,1,0:T(8,128)(2,1)} %shard_map.52), calls=%async_computation.1 | async-start | bytes 1572864 | tf_op jit(solution)/shard_map/all_to_all | solution.py:159
  250.3 0.9 copy-done.8
  251.2 5.6 %shard_map.48.refs_0_ = bf16[16,3,2,32,128]{4,3,2,1,0:T(8,128)(2,1)} custom-call(s32[768]{0:T(1024)} %reshape.19.pat_ref, bf16[16,6,2,32,64]{4,3,2,1,0:T(8,128)(2,1)} %bitcast.16, bf16[16,3,2,32,128]{4,3,2,1,0:T(8,128)(2,1)} %shard_map.47.refs_0_, bf16[16,3,2,32,128]{4,3,2,1,0:T(8,128)(2,1)} %copy-done.8), custom_call_target="tpu_custom_call" | custom-call | flops 50331648 | bytes 3145728 | tf_op jit(solution)/shard_map/pallas_call | solution.py:58
  256.9 3.2 collective-permute-start.3
  260.0 6.4 %shard_map.54.refs_0_ = bf16[16,4,2,32,128]{4,3,2,1,0:T(8,128)(2,1)} custom-call(s32[768]{0:T(1024)} %reshape.19.pat_ref, bf16[16,6,2,32,64]{4,3,2,1,0:T(8,128)(2,1)} %bitcast.21, bf16[16,4,2,32,128]{4,3,2,1,0:T(8,128)(2,1)} %get-tuple-element.11.refs_0_, bf16[16,4,2,32,128]{4,3,2,1,0:T(8,128)(2,1)} %collective-permute-done.9.refs_1_), custom_call_target="tpu_custom_call" | custom-call | flops 150994944 | bytes 3932160 | tf_op jit(solution)/shard_map/pallas_call | solution.py:58
  266.4 0.7 collective-permute-start.10
  267.1 12.0 %collective-permute-done.3.refs_1_ = bf16[16,3,2,32,128]{4,3,2,1,0:T(8,128)(2,1)} collective-permute-done((bf16[16,3,2,32,128]{4,3,2,1,0:T(8,128)(2,1)}, bf16[16,3,2,32,128]{4,3,2,1,0:T(8,128)(2,1)}, u32[]{:S(2)}, u32[]{:S(2)}) %collective-permute-start.3) | collective-permute-done | bytes 786464 | tf_op jit(solution)/shard_map/ppermute | solution.py:16
  279.2 5.6 %shard_map.49 = bf16[16,3,2,32,128]{4,3,2,1,0:T(8,128)(2,1)} custom-call(s32[768]{0:T(1024)} %reshape.19.pat_ref, bf16[16,6,2,32,64]{4,3,2,1,0:T(8,128)(2,1)} %bitcast.24, bf16[16,3,2,32,128]{4,3,2,1,0:T(8,128)(2,1)} %shard_map.48.refs_0_, bf16[16,3,2,32,128]{4,3,2,1,0:T(8,128)(2,1)} %collective-permute-done.3.refs_1_), custom_call_target="tpu_custom_call" | custom-call | flops 50331648 | bytes 3145728 | tf_op jit(solution)/shard_map/pallas_call | solution.py:58
  284.8 7.5 %all-to-all-start = ((bf16[16,3,2,32,128]{4,3,2,1,0:T(8,128)(2,1)}), bf16[16,3,2,32,128]{4,3,2,1,0:T(8,128)(2,1)S(1)}, u32[]{:S(2)}, u32[]{:S(2)}) async-start(bf16[16,3,2,32,128]{4,3,2,1,0:T(8,128)(2,1)} %shard_map.49), calls=%async_computation | async-start | bytes 1572864 | tf_op jit(solution)/shard_map/all_to_all | solution.py:159
  292.3 7.0 %collective-permute-done.10.refs_1_ = bf16[16,4,2,32,128]{4,3,2,1,0:T(8,128)(2,1)S(1)} collective-permute-done((bf16[16,4,2,32,128]{4,3,2,1,0:T(8,128)(2,1)}, bf16[16,4,2,32,128]{4,3,2,1,0:T(8,128)(2,1)S(1)}, u32[]{:S(2)}, u32[]{:S(2)}) %collective-permute-start.10) | collective-permute-done | bytes 1048608 | tf_op jit(solution)/shard_map/ppermute | solution.py:16
  299.3 1.0 copy-done.4
  300.3 6.4 %shard_map.55.refs_0_ = bf16[16,4,2,32,128]{4,3,2,1,0:T(8,128)(2,1)} custom-call(s32[768]{0:T(1024)} %reshape.19.pat_ref, bf16[16,6,2,32,64]{4,3,2,1,0:T(8,128)(2,1)} %bitcast.17, bf16[16,4,2,32,128]{4,3,2,1,0:T(8,128)(2,1)} %shard_map.54.refs_0_, bf16[16,4,2,32,128]{4,3,2,1,0:T(8,128)(2,1)} %copy-done.4), custom_call_target="tpu_custom_call" | custom-call | flops 150994944 | bytes 3932160 | tf_op jit(solution)/shard_map/pallas_call | solution.py:58
  306.7 1.8 collective-permute-start.11
  308.5 22.5 %collective-permute-done.11.refs_1_ = bf16[16,4,2,32,128]{4,3,2,1,0:T(8,128)(2,1)S(1)} collective-permute-done((bf16[16,4,2,32,128]{4,3,2,1,0:T(8,128)(2,1)}, bf16[16,4,2,32,128]{4,3,2,1,0:T(8,128)(2,1)S(1)}, u32[]{:S(2)}, u32[]{:S(2)}) %collective-permute-start.11) | collective-permute-done | bytes 1048608 | tf_op jit(solution)/shard_map/ppermute | solution.py:16
  331.0 1.0 copy-done.5
  331.9 6.4 %shard_map.56 = bf16[16,4,2,32,128]{4,3,2,1,0:T(8,128)(2,1)} custom-call(s32[768]{0:T(1024)} %reshape.19.pat_ref, bf16[16,6,2,32,64]{4,3,2,1,0:T(8,128)(2,1)} %bitcast.25, bf16[16,4,2,32,128]{4,3,2,1,0:T(8,128)(2,1)} %shard_map.55.refs_0_, bf16[16,4,2,32,128]{4,3,2,1,0:T(8,128)(2,1)} %copy-done.5), custom_call_target="tpu_custom_call" | custom-call | flops 150994944 | bytes 3932160 | tf_op jit(solution)/shard_map/pallas_call | solution.py:58
  338.3 7.7 %all-to-all-start.2 = ((bf16[16,4,2,32,128]{4,3,2,1,0:T(8,128)(2,1)}), bf16[16,4,2,32,128]{4,3,2,1,0:T(8,128)(2,1)S(1)}, u32[]{:S(2)}, u32[]{:S(2)}) async-start(bf16[16,4,2,32,128]{4,3,2,1,0:T(8,128)(2,1)} %shard_map.56), calls=%async_computation.2 | async-start | bytes 2097152 | tf_op jit(solution)/shard_map/all_to_all | solution.py:159
  346.0 22.5 %all-to-all-done.2.refs_2_ = bf16[16,4,2,32,128]{4,3,2,1,0:T(8,128)(2,1)S(1)} async-done(((bf16[16,4,2,32,128]{4,3,2,1,0:T(8,128)(2,1)}), bf16[16,4,2,32,128]{4,3,2,1,0:T(8,128)(2,1)S(1)}, u32[]{:S(2)}, u32[]{:S(2)}) %all-to-all-start.2) | async-done | bytes 1048608 | tf_op jit(solution)/shard_map/all_to_all | solution.py:159
  368.5 2.3 shard_map.60
  370.8 2.1 copy-done
  372.9 8.8 %copy.23 = bf16[96,2,32,274]{0,2,3,1:T(8,128)(2,1)} copy(bf16[96,2,32,274]{3,2,1,0:T(8,128)(2,1)} %copy-done) | data formatting | bytes 6733824 | tf_op jit(solution)/shard_map/pallas_call | solution.py:105
  (29 shorter events, 0.1 us)
Async XLA Ops:
  4.4 5.1 %slice-start = ((bf16[96,2,32,274]{0,2,3,1:T(8,128)(2,1)}), bf16[96,2,32,18]{0,2,3,1:T(8,128)(2,1)S(1)}, s32[]{:S(2)}) async-start(bf16[96,2,32,274]{0,2,3,1:T(8,128)(2,1)} %param.4), calls=%async_computation.4 | async-start | bytes 589824 | tf_op jit(solution)/shard_map/slice | solution.py:133
  9.5 17.2 %collective-permute-start.7 = (bf16[16,6,2,32,128]{4,3,2,1,0:T(8,128)(2,1)}, bf16[16,6,2,32,128]{4,3,2,1,0:T(8,128)(2,1)}, u32[]{:S(2)}, u32[]{:S(2)}) collective-permute-start(bf16[16,6,2,32,128]{4,3,2,1,0:T(8,128)(2,1)} %bitcast.30), channel_id=1, source_target_pairs={{0,1},{1,0},{2,3},{3,2},{4,5},{5,4},{6,7},{7,6},{8,9},{9,8},{10,11... | collective-permute-start | bytes 4718600 | tf_op jit(solution)/shard_map/ppermute | solution.py:16
  11.6 8.7 %copy-start.2 = (bf16[16,1,2,32,128]{4,3,2,1,0:T(8,128)(2,1)}, bf16[16,1,2,32,128]{4,3,2,1,0:T(8,128)(2,1)S(1)}, u32[]{:S(2)}) copy-start(bf16[16,1,2,32,128]{4,3,2,1,0:T(8,128)(2,1)S(1)} %pad_bitcast_fusion.refs_1_) | copy-start | bytes 786436
  11.6 15.1 %collective-permute-start.8 = (bf16[16,1,2,32,128]{4,3,2,1,0:T(8,128)(2,1)S(1)}, bf16[16,1,2,32,128]{4,3,2,1,0:T(8,128)(2,1)}, u32[]{:S(2)}, u32[]{:S(2)}) collective-permute-start(bf16[16,1,2,32,128]{4,3,2,1,0:T(8,128)(2,1)S(1)} %pad_bitcast_fusion.refs_1_), channel_id=1, source_target_pairs={{0,1},{1,0},{2,3},{3,2},{4,5},{5,4},{6,7},{7,6},{8,9},{9,8},{10,11... | collective-permute-start | bytes 786440 | tf_op jit(solution)/shard_map/ppermute | solution.py:16
  15.8 4.5 %copy-start.11 = (s32[4,96,2]{1,2,0:T(2,128)S(1)}, s32[4,96,2]{1,2,0:T(2,128)}, u32[]{:S(2)}) copy-start(s32[4,96,2]{1,2,0:T(2,128)} %param.6) | copy-start | bytes 9220
  15.8 67.0 %collective-permute-start = (bf16[16,6,2,32,128]{4,3,2,1,0:T(8,128)(2,1)}, bf16[16,6,2,32,128]{4,3,2,1,0:T(8,128)(2,1)}, u32[]{:S(2)}, u32[]{:S(2)}) collective-permute-start(bf16[16,6,2,32,128]{4,3,2,1,0:T(8,128)(2,1)} %bitcast.28), channel_id=1, source_target_pairs={{0,1},{1,0},{2,3},{3,2},{4,5},{5,4},{6,7},{7,6},{8,9},{9,8},{10,11... | collective-permute-start | bytes 4718600 | tf_op jit(solution)/shard_map/ppermute | solution.py:16
  33.8 41.8 %collective-permute-start.12 = (bf16[16,3,2,32,128]{4,3,2,1,0:T(8,128)(2,1)}, bf16[16,3,2,32,128]{4,3,2,1,0:T(8,128)(2,1)}, u32[]{:S(2)}, u32[]{:S(2)}) collective-permute-start(bf16[16,3,2,32,128]{4,3,2,1,0:T(8,128)(2,1)} %get-tuple-element.12.refs_0_), channel_id=1, source_target_pairs={{0,2},{1,3},{2,0},{3,1},{4,6},{5,7},{6,4},{7,5},{8,10},{9,11},{10,... | collective-permute-start | bytes 2359304 | tf_op jit(solution)/shard_map/ppermute | solution.py:16
  81.2 19.4 %collective-permute-start.13 = (bf16[16,3,2,32,128]{4,3,2,1,0:T(8,128)(2,1)}, bf16[16,3,2,32,128]{4,3,2,1,0:T(8,128)(2,1)S(1)}, u32[]{:S(2)}, u32[]{:S(2)}) collective-permute-start(bf16[16,3,2,32,128]{4,3,2,1,0:T(8,128)(2,1)} %shard_map.57.refs_0_), channel_id=1, source_target_pairs={{0,4},{1,5},{2,6},{3,7},{4,0},{5,1},{6,2},{7,3},{8,12},{9,13},{10,... | collective-permute-start | bytes 2359304 | tf_op jit(solution)/shard_map/ppermute | solution.py:16
  89.1 35.8 %collective-permute-start.4 = (bf16[16,3,2,32,128]{4,3,2,1,0:T(8,128)(2,1)}, bf16[16,3,2,32,128]{4,3,2,1,0:T(8,128)(2,1)}, u32[]{:S(2)}, u32[]{:S(2)}) collective-permute-start(bf16[16,3,2,32,128]{4,3,2,1,0:T(8,128)(2,1)} %get-tuple-element.10.refs_0_), channel_id=1, source_target_pairs={{0,2},{1,3},{2,0},{3,1},{4,6},{5,7},{6,4},{7,5},{8,10},{9,11},{10,... | collective-permute-start | bytes 2359304 | tf_op jit(solution)/shard_map/ppermute | solution.py:16
  100.6 0.9 copy-start.9
  107.1 27.0 %collective-permute-start.14 = (bf16[16,3,2,32,128]{4,3,2,1,0:T(8,128)(2,1)}, bf16[16,3,2,32,128]{4,3,2,1,0:T(8,128)(2,1)S(1)}, u32[]{:S(2)}, u32[]{:S(2)}) collective-permute-start(bf16[16,3,2,32,128]{4,3,2,1,0:T(8,128)(2,1)} %shard_map.58.refs_0_), channel_id=1, source_target_pairs={{0,8},{1,9},{2,10},{3,11},{4,12},{5,13},{6,14},{7,15},{8,0},{9,1},... | collective-permute-start | bytes 2359304 | tf_op jit(solution)/shard_map/ppermute | solution.py:16
  130.6 21.6 %collective-permute-start.5 = (bf16[16,3,2,32,128]{4,3,2,1,0:T(8,128)(2,1)}, bf16[16,3,2,32,128]{4,3,2,1,0:T(8,128)(2,1)S(1)}, u32[]{:S(2)}, u32[]{:S(2)}) collective-permute-start(bf16[16,3,2,32,128]{4,3,2,1,0:T(8,128)(2,1)} %shard_map.50.refs_0_), channel_id=1, source_target_pairs={{0,4},{1,5},{2,6},{3,7},{4,0},{5,1},{6,2},{7,3},{8,12},{9,13},{10,... | collective-permute-start | bytes 2359304 | tf_op jit(solution)/shard_map/ppermute | solution.py:16
  134.1 0.9 copy-start.10
  135.0 11.5 %copy-start.6 = (bf16[16,3,2,32,128]{4,3,2,1,0:T(8,128)(2,1)S(1)}, bf16[16,3,2,32,128]{4,3,2,1,0:T(8,128)(2,1)}, u32[]{:S(2)}) copy-start(bf16[16,3,2,32,128]{4,3,2,1,0:T(8,128)(2,1)} %get-tuple-element.9.refs_0_) | copy-start | bytes 2359300
  140.8 104.5 %all-to-all-start.3 = ((bf16[16,3,2,32,128]{4,3,2,1,0:T(8,128)(2,1)}), bf16[16,3,2,32,128]{4,3,2,1,0:T(8,128)(2,1)S(1)}, u32[]{:S(2)}, u32[]{:S(2)}) async-start(bf16[16,3,2,32,128]{4,3,2,1,0:T(8,128)(2,1)} %shard_map.59), calls=%async_computation.3 | async-start | bytes 1572864 | tf_op jit(solution)/shard_map/all_to_all | solution.py:159
  146.5 15.4 %copy-start.3 = (bf16[16,4,2,32,128]{4,3,2,1,0:T(8,128)(2,1)S(1)}, bf16[16,4,2,32,128]{4,3,2,1,0:T(8,128)(2,1)}, u32[]{:S(2)}) copy-start(bf16[16,4,2,32,128]{4,3,2,1,0:T(8,128)(2,1)} %get-tuple-element.11.refs_0_) | copy-start | bytes 3145732
  146.5 34.6 %collective-permute-start.1 = (bf16[16,3,2,32,128]{4,3,2,1,0:T(8,128)(2,1)S(1)}, bf16[16,3,2,32,128]{4,3,2,1,0:T(8,128)(2,1)}, u32[]{:S(2)}, u32[]{:S(2)}) collective-permute-start(bf16[16,3,2,32,128]{4,3,2,1,0:T(8,128)(2,1)S(1)} %copy-done.6), channel_id=1, source_target_pairs={{0,2},{1,3},{2,0},{3,1},{4,6},{5,7},{6,4},{7,5},{8,10},{9,11},{10,... | collective-permute-start | bytes 2359304 | tf_op jit(solution)/shard_map/ppermute | solution.py:16
  152.2 1.0 copy-start.7
  158.8 29.6 %collective-permute-start.6 = (bf16[16,3,2,32,128]{4,3,2,1,0:T(8,128)(2,1)}, bf16[16,3,2,32,128]{4,3,2,1,0:T(8,128)(2,1)}, u32[]{:S(2)}, u32[]{:S(2)}) collective-permute-start(bf16[16,3,2,32,128]{4,3,2,1,0:T(8,128)(2,1)} %shard_map.51.refs_0_), channel_id=1, source_target_pairs={{0,8},{1,9},{2,10},{3,11},{4,12},{5,13},{6,14},{7,15},{8,0},{9,1},... | collective-permute-start | bytes 2359304 | tf_op jit(solution)/shard_map/ppermute | solution.py:16
  162.0 98.1 %collective-permute-start.9 = (bf16[16,4,2,32,128]{4,3,2,1,0:T(8,128)(2,1)S(1)}, bf16[16,4,2,32,128]{4,3,2,1,0:T(8,128)(2,1)}, u32[]{:S(2)}, u32[]{:S(2)}) collective-permute-start(bf16[16,4,2,32,128]{4,3,2,1,0:T(8,128)(2,1)S(1)} %copy-done.3), channel_id=1, source_target_pairs={{0,2},{1,3},{2,0},{3,1},{4,6},{5,7},{6,4},{7,5},{8,10},{9,11},{10,... | collective-permute-start | bytes 3145736 | tf_op jit(solution)/shard_map/ppermute | solution.py:16
  186.8 63.5 %collective-permute-start.2 = (bf16[16,3,2,32,128]{4,3,2,1,0:T(8,128)(2,1)}, bf16[16,3,2,32,128]{4,3,2,1,0:T(8,128)(2,1)S(1)}, u32[]{:S(2)}, u32[]{:S(2)}) collective-permute-start(bf16[16,3,2,32,128]{4,3,2,1,0:T(8,128)(2,1)} %shard_map.47.refs_0_), channel_id=1, source_target_pairs={{0,4},{1,5},{2,6},{3,7},{4,0},{5,1},{6,2},{7,3},{8,12},{9,13},{10,... | collective-permute-start | bytes 2359304 | tf_op jit(solution)/shard_map/ppermute | solution.py:16
  245.3 39.5 %all-to-all-start.1 = ((bf16[16,3,2,32,128]{4,3,2,1,0:T(8,128)(2,1)}), bf16[16,3,2,32,128]{4,3,2,1,0:T(8,128)(2,1)S(1)}, u32[]{:S(2)}, u32[]{:S(2)}) async-start(bf16[16,3,2,32,128]{4,3,2,1,0:T(8,128)(2,1)} %shard_map.52), calls=%async_computation.1 | async-start | bytes 1572864 | tf_op jit(solution)/shard_map/all_to_all | solution.py:159
  250.3 0.9 copy-start.8
  256.9 22.3 %collective-permute-start.3 = (bf16[16,3,2,32,128]{4,3,2,1,0:T(8,128)(2,1)}, bf16[16,3,2,32,128]{4,3,2,1,0:T(8,128)(2,1)}, u32[]{:S(2)}, u32[]{:S(2)}) collective-permute-start(bf16[16,3,2,32,128]{4,3,2,1,0:T(8,128)(2,1)} %shard_map.48.refs_0_), channel_id=1, source_target_pairs={{0,8},{1,9},{2,10},{3,11},{4,12},{5,13},{6,14},{7,15},{8,0},{9,1},... | collective-permute-start | bytes 2359304 | tf_op jit(solution)/shard_map/ppermute | solution.py:16
  266.4 32.8 %collective-permute-start.10 = (bf16[16,4,2,32,128]{4,3,2,1,0:T(8,128)(2,1)}, bf16[16,4,2,32,128]{4,3,2,1,0:T(8,128)(2,1)S(1)}, u32[]{:S(2)}, u32[]{:S(2)}) collective-permute-start(bf16[16,4,2,32,128]{4,3,2,1,0:T(8,128)(2,1)} %shard_map.54.refs_0_), channel_id=1, source_target_pairs={{0,4},{1,5},{2,6},{3,7},{4,0},{5,1},{6,2},{7,3},{8,12},{9,13},{10,... | collective-permute-start | bytes 3145736 | tf_op jit(solution)/shard_map/ppermute | solution.py:16
  284.8 53.5 %all-to-all-start = ((bf16[16,3,2,32,128]{4,3,2,1,0:T(8,128)(2,1)}), bf16[16,3,2,32,128]{4,3,2,1,0:T(8,128)(2,1)S(1)}, u32[]{:S(2)}, u32[]{:S(2)}) async-start(bf16[16,3,2,32,128]{4,3,2,1,0:T(8,128)(2,1)} %shard_map.49), calls=%async_computation | async-start | bytes 1572864 | tf_op jit(solution)/shard_map/all_to_all | solution.py:159
  299.3 1.0 copy-start.4
  306.7 24.3 %collective-permute-start.11 = (bf16[16,4,2,32,128]{4,3,2,1,0:T(8,128)(2,1)}, bf16[16,4,2,32,128]{4,3,2,1,0:T(8,128)(2,1)S(1)}, u32[]{:S(2)}, u32[]{:S(2)}) collective-permute-start(bf16[16,4,2,32,128]{4,3,2,1,0:T(8,128)(2,1)} %shard_map.55.refs_0_), channel_id=1, source_target_pairs={{0,8},{1,9},{2,10},{3,11},{4,12},{5,13},{6,14},{7,15},{8,0},{9,1},... | collective-permute-start | bytes 3145736 | tf_op jit(solution)/shard_map/ppermute | solution.py:16
  331.0 1.0 copy-start.5
  338.3 30.2 %copy-start.1 = (s32[1536]{0:T(1024)S(1)}, s32[1536]{0:T(1024)}, u32[]{:S(2)}) copy-start(s32[1536]{0:T(1024)} %assign_ref.1) | copy-start | bytes 18436
  338.3 30.1 %all-to-all-start.2 = ((bf16[16,4,2,32,128]{4,3,2,1,0:T(8,128)(2,1)}), bf16[16,4,2,32,128]{4,3,2,1,0:T(8,128)(2,1)S(1)}, u32[]{:S(2)}, u32[]{:S(2)}) async-start(bf16[16,4,2,32,128]{4,3,2,1,0:T(8,128)(2,1)} %shard_map.56), calls=%async_computation.2 | async-start | bytes 2097152 | tf_op jit(solution)/shard_map/all_to_all | solution.py:159
  370.7 2.1 copy-start

commit v2 on v1

v2 whole, which is shorter than its diff:
```python
import functools

import jax
import jax.numpy as jnp
from jax import lax
from jax.experimental import pallas as pl
from jax.experimental.pallas import tpu as pltpu
from jax.sharding import PartitionSpec as P

LEVELS = 4
LANES = 128
TAIL = -1
PIECE = 8
FIRST = ((0, 1, 2), (3, 4, 5))
SECOND = ((-1, 0, 1, 2), (3, 4, 5))
ORDER = ((0, 1), (1, 1), (0, 2), (0, 3), (1, 2), (2, 1), (1, 3), (2, 2), (3, 1), (3, 2), (2, 3), (3, 3))
WAITS = {(2, 3): (0,), (3, 3): (0,)}
EARLY = (3, 3)


def from_partner(value, bit):
    size = lax.axis_size("lat")
    return lax.ppermute(value, "lat", [(i, i ^ 1 << bit) for i in range(size)])


def level_kernel(spec, lev, tail_w, pat_ref, w_ref, *refs):
    n_in = spec["n_in"]
    own, far, outs = refs[:n_in], refs[n_in : 2 * n_in], refs[-len(spec["slots"]) :]
    groups, per_peer = w_ref.shape[0], w_ref.shape[1]
    boxes = w_ref.shape[2]
    lane = lax.broadcasted_iota(jnp.int32, (w_ref.shape[3], LANES), 1)
    total = groups * per_peer

    def group(c, carry):
        for out, slots in zip(outs, spec["slots"]):
            for at, slot in enumerate(slots):
                for g in range(boxes):

                    def product(order, src, idx):
                        sel = pat_ref[(lev * total + c * per_peer + order) * boxes + g]
                        rhs = jnp.concatenate([own[src][c, idx, g], far[src][c, idx, sel]], axis=0)
                        return jnp.dot(w_ref[c, order, g], rhs, preferred_element_type=jnp.float32)

                    if slot[0] == "m":
                        acc = product(slot[3], slot[1], slot[2])
                    else:
                        acc = product(0, slot[1], slot[2])
                        for j in range(1, per_peer):
                            acc = jnp.where(lane < j * tail_w, acc, product(j, slot[1], slot[2]))
                    out[c, at, g] = acc.astype(jnp.bfloat16)
        return carry

    lax.fori_loop(0, groups, group, 0, unroll=4)


def run_level(lev, tail_w, slots, pattern, weights, own, far, after):
    peers, per_peer, boxes, rank, _ = weights.shape
    spec = {"n_in": len(own), "slots": slots}
    vmem = pl.BlockSpec(memory_space=pltpu.VMEM)
    out_shapes = [jax.ShapeDtypeStruct((peers, len(s), boxes, rank, LANES), jnp.bfloat16) for s in slots]
    return pl.pallas_call(
        functools.partial(level_kernel, spec, lev, tail_w),
        in_specs=[pl.BlockSpec(memory_space=pltpu.SMEM)]
        + [vmem] * (1 + 2 * len(own))
        + [pl.BlockSpec(memory_space=pl.ANY)] * len(after),
        out_specs=[vmem] * len(slots),
        out_shape=out_shapes,
        cost_estimate=pl.CostEstimate(flops=1, bytes_accessed=1, transcendentals=0),
    )(pattern, weights, *own, *far, *after)


def place_kernel(tail_w, slots, me_ref, assign_ref, *refs):
    out_ref = refs[-1]
    peers, per_peer, boxes = refs[0].shape[0], len(slots), refs[0].shape[2]
    local = peers * per_peer
    me = me_ref[0]

    def peer(k, carry):
        for j, (src, at) in enumerate(slots):
            to = assign_ref[k * local + me * per_peer + j] - me * local
            for g in range(boxes):
                value = refs[src][k, at, g]
                if out_ref.shape[-1] < LANES:
                    value = value.astype(jnp.float32)
                    if j:
                        value = pltpu.roll(value, LANES - j * tail_w, 1)
                    value = value[:, :tail_w].astype(jnp.bfloat16)
                out_ref[to, g] = value
        return carry

    lax.fori_loop(0, peers, peer, 0, unroll=2)


def place(tail_w, slots, me, assign, parts, cols, after=()):
    peers, _, boxes, rank, _ = parts[0].shape
    vmem = pl.BlockSpec(memory_space=pltpu.VMEM)
    smem = pl.BlockSpec(memory_space=pltpu.SMEM)
    return pl.pallas_call(
        functools.partial(place_kernel, tail_w, slots),
        in_specs=[smem, smem] + [vmem] * len(parts) + [pl.BlockSpec(memory_space=pl.ANY)] * len(after),
        out_specs=vmem,
        out_shape=jax.ShapeDtypeStruct((peers * len(slots), boxes, rank, cols), jnp.bfloat16),
        cost_estimate=pl.CostEstimate(flops=1, bytes_accessed=1, transcendentals=0),
    )(me, assign, *parts, *after)


def store_kernel(start, *refs):
    piece, out, sems = refs[0], refs[-2], refs[-1]
    boxes, width = piece.shape[:2]
    part = width // sems.shape[1]
    copies = [
        pltpu.make_async_copy(
            piece.at[g, pl.ds(q * part, part)], out.at[g, pl.ds(start + q * part, part)], sems.at[g, q]
        )
        for g in range(boxes)
        for q in range(sems.shape[1])
    ]
    for copy in copies:
        copy.start()
    for copy in copies:
        copy.wait()


def store(piece, start, cols, whole=None):
    boxes, _, rank, local = piece.shape
    held = [] if whole is None else [whole]
    return pl.pallas_call(
        functools.partial(store_kernel, start),
        in_specs=[pl.BlockSpec(memory_space=pltpu.VMEM)] + [pl.BlockSpec(memory_space=pl.ANY)] * len(held),
        out_specs=pl.BlockSpec(memory_space=pl.ANY),
        out_shape=jax.ShapeDtypeStruct((boxes, cols, rank, local), jnp.bfloat16),
        scratch_shapes=[pltpu.SemaphoreType.DMA((boxes, 4 if piece.shape[1] % 4 == 0 else 1))],
        input_output_aliases={1: 0} if held else {},
        cost_estimate=pl.CostEstimate(flops=1, bytes_accessed=1, transcendentals=0),
    )(piece, *held)


def per_device(coeffs, coupling, pattern, assign):
    local, boxes, rank, cols = coeffs.shape
    peers = lax.axis_size("order")
    per_peer = local // peers
    tail_w = cols - 2 * LANES
    me = lax.axis_index("order").astype(jnp.int32).reshape(1)

    def six(x):
        return x.reshape(peers, per_peer, boxes, rank, x.shape[-1])

    def level_weights(c, l):
        return six(c[l])

    first = six(coeffs[..., :LANES])
    coeffs, coupling_later, first = lax.optimization_barrier((coeffs, coupling, first))
    first_far = from_partner(first, 0)
    weights = [level_weights(coupling, 0)] + [level_weights(coupling_later, l) for l in range(1, LEVELS)]
    flat_pattern = pattern.reshape(-1)

    after = []

    def level(lev, slots, own, far):
        outs = run_level(lev, tail_w, slots, flat_pattern, weights[lev], own, far, after)
        after[:] = outs[:1]
        return outs

    def split(groups, tail_at):
        return [[("t", tail_at, 0) if j == TAIL else ("m", 0, j, j) for j in group] for group in groups]

    def own_slots(group):
        return [("t", 0, i) if j == TAIL else ("m", 0, i, j) for i, j in enumerate(group)]

    def places(groups):
        found = {j: (at, i) for at, group in enumerate(groups) for i, j in enumerate(group)}
        return [found[j] for j in range(per_peer)]

    chunks = list(level(0, split(FIRST, 0), [first], [first_far]))
    second = six(coeffs[..., LANES : 2 * LANES])
    tail = six(coeffs[..., 2 * LANES :]).transpose(0, 2, 3, 1, 4).reshape(peers, boxes, rank, per_peer * tail_w)
    tail = jnp.pad(tail, ((0, 0), (0, 0), (0, 0), (0, LANES - per_peer * tail_w)))[:, None]
    chunks += level(
        0, split(SECOND, 1), [second, tail], [from_partner(second, 0), from_partner(tail, 0)]
    )
    groups = FIRST + SECOND
    tail_chunk = [TAIL in group for group in groups].index(True)
    far = [[from_partner(chunk, 1)] for chunk in chunks]
    chunks = [[chunk] for chunk in chunks]
    where = [own_slots(group) for group in groups]
    done = [None] * len(chunks)
    whole = None
    for k, lev in ORDER:
        if (k, lev) == EARLY:
            early = place(tail_w, places(FIRST), me, assign, done[: len(FIRST)], LANES)
            whole = store(early.transpose(1, 3, 2, 0), 0, cols)
            after.append(whole)
        after += [done[w] for w in WAITS.get((k, lev), ())]
        width = PIECE if lev + 1 < LEVELS else len(where[k])
        pieces = [where[k][i : i + width] for i in range(0, len(where[k]), width)]
        chunks[k] = level(lev, pieces, chunks[k], far[k])
        if lev + 1 < LEVELS:
            far[k] = [from_partner(piece, lev + 1) for piece in chunks[k]]
            where[k] = [
                slot[:1] + (at, i) + slot[3:] for at, piece in enumerate(pieces) for i, slot in enumerate(piece)
            ]
        else:
            done[k] = lax.all_to_all(chunks[k][0], "order", split_axis=0, concat_axis=0, tiled=True)
    tail_slot = groups[tail_chunk].index(TAIL)
    ends = place(tail_w, [(0, tail_slot)] * per_peer, me, assign, [done[tail_chunk]], tail_w, after)
    whole = store(ends.transpose(1, 3, 2, 0), 2 * LANES, cols, whole)
    late = place(tail_w, places(SECOND), me, assign, done[len(FIRST) :], LANES, [whole])
    whole = store(late.transpose(1, 3, 2, 0), LANES, cols, whole)
    return whole.transpose(3, 0, 2, 1)


def solution(mesh):
    return jax.shard_map(
        per_device,
        mesh=mesh,
        in_specs=(
            P("order", "lat", None, None),
            P(None, "order", "lat", None, None),
            P(None, "order", "lat"),
            P(),
        ),
        out_specs=P("order", "lat", None, None),
        check_vma=False,
    )
```

time: 384 us -> 334 us (0.87)
  waiting for transfers between devices: 181 us -> 147 us
  Pallas kernels: 85.6 us -> 74.8 us
  starting transfers between devices: 62.9 us -> 58.2 us
    all_to_all x4, waiting for transfers between devices: 73.7 us -> 40.7 us  [per_device(): lax.all_to_all(chunks[k][0], 'order', split_axis=0, concat_axis=0, tiled=...]
    pallas_call x15 -> x20, Pallas kernels: 85.6 us -> 74.8 us  [the longest x14 58.3 us: run_level(): pl.pallas_call(functools.partial(level_kernel, spec, lev, tail_w), in_spe...]
    ppermute x15, starting transfers between devices: 36.9 us -> 30.2 us  [from_partner(): return lax.ppermute(value, 'lat', [(i, i ^ 1 << bit) for i in range(size)])]
    pallas_call x1 -> x3, local copies, waits for them, and re-layouts: 8.79 us -> 13.5 us  [place(): pl.pallas_call(functools.partial(place_kernel, tail_w, slots), in_specs=[...]
    slice x2 -> x3, local copies, waits for them, and re-layouts: 9.5 us -> 5.22 us  [per_device(): second = six(coeffs[..., LANES:2 * LANES])]
    slice x5 -> x7, local copies, waits for them, and re-layouts: 17.7 us -> 17.1 us  [level_weights(): return six(c[l])]
    unnamed x25 -> x37, local copies, waits for them, and re-layouts: 8.56 us -> 8.89 us
  transfers between devices with their start and end apart: 19 -> 19, of which waited for: 9 -> 11; matrix products, arithmetic and copies ran while one was open for 7% -> 10% of each run, Pallas kernels for 22% -> 20%
where the time goes in v2:
time: 334 us; the launch traced here: 333 us
  waiting for transfers between devices  147 us (44%)
  Pallas kernels  74.8 us (22%)
  starting transfers between devices  58.2 us (17%)
  local copies, waits for them, and re-layouts  52.8 us (16%)
    ppermute x15, waiting for transfers between devices, from_partner(): return lax.ppermute(value, 'lat', [(i, i ^ 1 << bit) for i in range(size)])  107 us
    pallas_call x14, Pallas kernels, run_level(): pl.pallas_call(functools.partial(level_kernel, spec, lev, tail_w), in_spe...  58.3 us
    all_to_all x4, waiting for transfers between devices, per_device(): lax.all_to_all(chunks[k][0], 'order', split_axis=0, concat_axis=0, tiled=...  40.7 us
    ppermute x15, starting transfers between devices, from_partner(): return lax.ppermute(value, 'lat', [(i, i ^ 1 << bit) for i in range(size)])  30.2 us
    all_to_all x4, starting transfers between devices, per_device(): lax.all_to_all(chunks[k][0], 'order', split_axis=0, concat_axis=0, tiled=...  28 us
    slice x7, local copies, waits for them, and re-layouts, level_weights(): return six(c[l])  17.1 us
    pallas_call x3, local copies, waits for them, and re-layouts, place(): pl.pallas_call(functools.partial(place_kernel, tail_w, slots), in_specs=[...  13.5 us
    unnamed x37, local copies, waits for them, and re-layouts  8.89 us
  transfers between devices with their start and end apart: 19, of which 11 were waited for; matrix products, arithmetic and copies ran while one was open for 10% of the time, Pallas kernels for 20%

profile of v2, /device:TPU:32, one launch (start us, length us, event | category | flops | bytes accessed | tf_op | source)
XLA Modules:
  0.0 333.4 jit_solution(4795739996427759151)
XLA Ops:
  0.0 1.6 slice-done
  1.6 3.6 %copy.18 = bf16[96,2,32,128]{3,2,1,0:T(8,128)(2,1)} copy(bf16[96,2,32,128]{0,2,3,1:T(8,128)(2,1)S(1)} %slice-done) | data formatting | bytes 3145728 | tf_op jit(solution)/shard_map/slice | solution.py:151
  5.2 1.6 slice-done.1
  6.8 3.6 %copy.23 = bf16[96,2,32,128]{3,2,1,0:T(8,128)(2,1)} copy(bf16[96,2,32,128]{0,2,3,1:T(8,128)(2,1)S(1)} %slice-done.1) | data formatting | bytes 3145728 | tf_op jit(solution)/shard_map/slice | solution.py:175
  12.0 3.0 copy.22
  15.0 4.9 %shard_map.46 = (bf16[16,3,2,32,128]{4,3,2,1,0:T(8,128)(2,1)}, bf16[16,3,2,32,128]{4,3,2,1,0:T(8,128)(2,1)}) custom-call(s32[768]{0:T(1024)} %reshape.19.pat_ref, bf16[16,6,2,32,64]{4,3,2,1,0:T(8,128)(2,1)} %bitcast.30, bf16[16,6,2,32,128]{4,3,2,1,0:T(8,128)(2,1)} %bitcast.37, bf16[16,6,2,32,128]{4,3,2,1,0:T(8,128)(2,1)} %collective-permute-done.2.refs_1_), custom_call_target="tpu_custom_call" | custom-call | flops 1 | bytes 1 | tf_op jit(solution)/shard_map/pallas_call | solution.py:61
  19.9 6.3 %collective-permute-start.5 = (bf16[16,3,2,32,128]{4,3,2,1,0:T(8,128)(2,1)}, bf16[16,3,2,32,128]{4,3,2,1,0:T(8,128)(2,1)}, u32[]{:S(2)}, u32[]{:S(2)}) collective-permute-start(bf16[16,3,2,32,128]{4,3,2,1,0:T(8,128)(2,1)} %get-tuple-element.15.refs_4_.refs_0_), channel_id=1, source_target_pairs={{0,2},{1,3},{2,0},{3,1},{4,6},{5,7},{6,4},{7,5},{8,10},{9,11},{10,... | collective-permute-start | bytes 2359304 | tf_op jit(solution)/shard_map/ppermute | solution.py:23
  26.9 1.4 copy.26
  28.4 3.7 %fusion = (bf16[1,96,2,32,64]{1,4,3,2,0:T(8,128)(2,1)}, bf16[1,96,2,32,64]{1,4,3,2,0:T(8,128)(2,1)S(1)}, bf16[1,96,2,32,64]{1,4,3,2,0:T(8,128)(2,1)S(1)}) fusion(bf16[4,96,2,32,64]{1,4,3,2,0:T(8,128)(2,1)} %param.5), kind=kLoop, calls=%fused_computation.1 | loop fusion | bytes 4718592 | tf_op jit(solution)/shard_map/slice | solution.py:149
  32.2 4.2 %copy.21 = bf16[1,96,2,32,64]{4,3,2,1,0:T(8,128)(2,1)} copy(bf16[1,96,2,32,64]{1,4,3,2,0:T(8,128)(2,1)} %get-tuple-element.19) | data formatting | bytes 1572864 | tf_op jit(solution)/shard_map/slice | solution.py:149
  37.0 5.9 %shard_map.47 = (bf16[16,4,2,32,128]{4,3,2,1,0:T(8,128)(2,1)}, bf16[16,3,2,32,128]{4,3,2,1,0:T(8,128)(2,1)}) custom-call(s32[768]{0:T(1024)} %reshape.19.pat_ref, bf16[16,6,2,32,64]{4,3,2,1,0:T(8,128)(2,1)} %bitcast.31, bf16[16,6,2,32,128]{4,3,2,1,0:T(8,128)(2,1)} %bitcast.35, bf16[16,1,2,32,128]{4,3,2,1,0:T(8,128)(2,1)} %copy-done.6, ...), custom_call_target="tpu_custom_call" | custom-call | flops 1 | bytes 1 | tf_op jit(solution)/shard_map/pallas_call | solution.py:61
  42.9 26.4 %collective-permute-done.5.refs_1_ = bf16[16,3,2,32,128]{4,3,2,1,0:T(8,128)(2,1)} collective-permute-done((bf16[16,3,2,32,128]{4,3,2,1,0:T(8,128)(2,1)}, bf16[16,3,2,32,128]{4,3,2,1,0:T(8,128)(2,1)}, u32[]{:S(2)}, u32[]{:S(2)}) %collective-permute-start.5) | collective-permute-done | bytes 786464 | tf_op jit(solution)/shard_map/ppermute | solution.py:23
  69.3 3.7 %shard_map.48.refs_2_.refs_0_ = bf16[16,3,2,32,128]{4,3,2,1,0:T(8,128)(2,1)} custom-call(s32[768]{0:T(1024)} %reshape.19.pat_ref, bf16[16,6,2,32,64]{4,3,2,1,0:T(8,128)(2,1)} %bitcast.22, bf16[16,3,2,32,128]{4,3,2,1,0:T(8,128)(2,1)} %get-tuple-element.15.refs_4_.refs_0_, bf16[16,3,2,32,128]{4,3,2,1,0:T(8,128)(2,1)} %collective-permute-done.5.refs_1_, ...), custom_call_target="tpu_custom_call" | custom-call | flops 1 | bytes 1 | tf_op jit(solution)/shard_map/pallas_call | solution.py:61
  73.1 1.5 collective-permute-start.7
  74.6 3.0 copy.20
  77.7 17.3 %collective-permute-done.4.refs_1_ = bf16[16,3,2,32,128]{4,3,2,1,0:T(8,128)(2,1)} collective-permute-done((bf16[16,3,2,32,128]{4,3,2,1,0:T(8,128)(2,1)S(1)}, bf16[16,3,2,32,128]{4,3,2,1,0:T(8,128)(2,1)}, u32[]{:S(2)}, u32[]{:S(2)}) %collective-permute-start.4) | collective-permute-done | bytes 786464 | tf_op jit(solution)/shard_map/ppermute | solution.py:23
  95.0 3.6 %shard_map.49.refs_2_.refs_0_ = bf16[16,3,2,32,128]{4,3,2,1,0:T(8,128)(2,1)} custom-call(s32[768]{0:T(1024)} %reshape.19.pat_ref, bf16[16,6,2,32,64]{4,3,2,1,0:T(8,128)(2,1)} %bitcast.23, bf16[16,3,2,32,128]{4,3,2,1,0:T(8,128)(2,1)} %get-tuple-element.17.refs_0_, bf16[16,3,2,32,128]{4,3,2,1,0:T(8,128)(2,1)} %collective-permute-done.4.refs_1_, ...), custom_call_target="tpu_custom_call" | custom-call | flops 1 | bytes 1 | tf_op jit(solution)/shard_map/pallas_call | solution.py:61
  98.6 3.8 %shard_map.50.refs_0_.refs_2_ = bf16[16,3,2,32,128]{4,3,2,1,0:T(8,128)(2,1)} custom-call(s32[768]{0:T(1024)} %reshape.19.pat_ref, bf16[16,6,2,32,64]{4,3,2,1,0:T(8,128)(2,1)} %bitcast.26, bf16[16,3,2,32,128]{4,3,2,1,0:T(8,128)(2,1)} %shard_map.48.refs_2_.refs_0_, bf16[16,3,2,32,128]{4,3,2,1,0:T(8,128)(2,1)} %collective-permute-done.7.refs_1_, ...), custom_call_target="tpu_custom_call" | custom-call | flops 1 | bytes 1 | tf_op jit(solution)/shard_map/pallas_call | solution.py:61
  102.4 3.2 collective-permute-start.8
  105.6 5.4 %collective-permute-start.3 = (bf16[16,4,2,32,128]{4,3,2,1,0:T(8,128)(2,1)}, bf16[16,4,2,32,128]{4,3,2,1,0:T(8,128)(2,1)}, u32[]{:S(2)}, u32[]{:S(2)}) collective-permute-start(bf16[16,4,2,32,128]{4,3,2,1,0:T(8,128)(2,1)} %get-tuple-element.16.refs_2_.refs_0_), channel_id=1, source_target_pairs={{0,2},{1,3},{2,0},{3,1},{4,6},{5,7},{6,4},{7,5},{8,10},{9,11},{10,... | collective-permute-start | bytes 3145736 | tf_op jit(solution)/shard_map/ppermute | solution.py:23
  111.7 3.1 copy.19
  114.8 9.8 %collective-permute-done.8.refs_1_ = bf16[16,3,2,32,128]{4,3,2,1,0:T(8,128)(2,1)S(1)} collective-permute-done((bf16[16,3,2,32,128]{4,3,2,1,0:T(8,128)(2,1)}, bf16[16,3,2,32,128]{4,3,2,1,0:T(8,128)(2,1)S(1)}, u32[]{:S(2)}, u32[]{:S(2)}) %collective-permute-start.8) | collective-permute-done | bytes 786464 | tf_op jit(solution)/shard_map/ppermute | solution.py:23
  124.6 0.9 copy-done.14
  125.5 3.6 %shard_map.51.refs_2_ = bf16[16,3,2,32,128]{4,3,2,1,0:T(8,128)(2,1)} custom-call(s32[768]{0:T(1024)} %reshape.19.pat_ref, bf16[16,6,2,32,64]{4,3,2,1,0:T(8,128)(2,1)} %bitcast.18, bf16[16,3,2,32,128]{4,3,2,1,0:T(8,128)(2,1)} %shard_map.50.refs_0_.refs_2_, bf16[16,3,2,32,128]{4,3,2,1,0:T(8,128)(2,1)} %copy-done.14, ...), custom_call_target="tpu_custom_call" | custom-call | flops 1 | bytes 1 | tf_op jit(solution)/shard_map/pallas_call | solution.py:61
  129.1 8.5 %all-to-all-start = ((bf16[16,3,2,32,128]{4,3,2,1,0:T(8,128)(2,1)}), bf16[16,3,2,32,128]{4,3,2,1,0:T(8,128)(2,1)S(1)}, u32[]{:S(2)}, u32[]{:S(2)}) async-start(bf16[16,3,2,32,128]{4,3,2,1,0:T(8,128)(2,1)} %shard_map.51.refs_2_), calls=%async_computation | async-start | bytes 1572864 | tf_op jit(solution)/shard_map/all_to_all | solution.py:203
  137.6 2.2 collective-permute-done.6.refs_1_
  139.9 0.9 copy-done.13
  140.8 3.7 %shard_map.52.refs_2_.refs_0_ = bf16[16,3,2,32,128]{4,3,2,1,0:T(8,128)(2,1)} custom-call(s32[768]{0:T(1024)} %reshape.19.pat_ref, bf16[16,6,2,32,64]{4,3,2,1,0:T(8,128)(2,1)} %bitcast.27, bf16[16,3,2,32,128]{4,3,2,1,0:T(8,128)(2,1)} %shard_map.49.refs_2_.refs_0_, bf16[16,3,2,32,128]{4,3,2,1,0:T(8,128)(2,1)} %copy-done.13, ...), custom_call_target="tpu_custom_call" | custom-call | flops 1 | bytes 1 | tf_op jit(solution)/shard_map/pallas_call | solution.py:61
  144.5 1.8 collective-permute-start.10
  146.3 4.6 %collective-permute-done.3.refs_1_ = bf16[16,4,2,32,128]{4,3,2,1,0:T(8,128)(2,1)} collective-permute-done((bf16[16,4,2,32,128]{4,3,2,1,0:T(8,128)(2,1)}, bf16[16,4,2,32,128]{4,3,2,1,0:T(8,128)(2,1)}, u32[]{:S(2)}, u32[]{:S(2)}) %collective-permute-start.3) | collective-permute-done | bytes 1048608 | tf_op jit(solution)/shard_map/ppermute | solution.py:23
  151.0 4.8 %shard_map.53.refs_2_.refs_0_ = bf16[16,4,2,32,128]{4,3,2,1,0:T(8,128)(2,1)} custom-call(s32[768]{0:T(1024)} %reshape.19.pat_ref, bf16[16,6,2,32,64]{4,3,2,1,0:T(8,128)(2,1)} %bitcast.24, bf16[16,4,2,32,128]{4,3,2,1,0:T(8,128)(2,1)} %get-tuple-element.16.refs_2_.refs_0_, bf16[16,4,2,32,128]{4,3,2,1,0:T(8,128)(2,1)} %collective-permute-done.3.refs_1_, ...), custom_call_target="tpu_custom_call" | custom-call | flops 1 | bytes 1 | tf_op jit(solution)/shard_map/pallas_call | solution.py:61
  156.4 5.5 %collective-permute-start.12 = (bf16[16,3,2,32,128]{4,3,2,1,0:T(8,128)(2,1)S(1)}, bf16[16,3,2,32,128]{4,3,2,1,0:T(8,128)(2,1)}, u32[]{:S(2)}, u32[]{:S(2)}) collective-permute-start(bf16[16,3,2,32,128]{4,3,2,1,0:T(8,128)(2,1)S(1)} %copy-done.10), channel_id=1, source_target_pairs={{0,2},{1,3},{2,0},{3,1},{4,6},{5,7},{6,4},{7,5},{8,10},{9,11},{10,... | collective-permute-start | bytes 2359304 | tf_op jit(solution)/shard_map/ppermute | solution.py:23
  161.9 4.8 %collective-permute-done.10.refs_1_ = bf16[16,3,2,32,128]{4,3,2,1,0:T(8,128)(2,1)S(1)} collective-permute-done((bf16[16,3,2,32,128]{4,3,2,1,0:T(8,128)(2,1)}, bf16[16,3,2,32,128]{4,3,2,1,0:T(8,128)(2,1)S(1)}, u32[]{:S(2)}, u32[]{:S(2)}) %collective-permute-start.10) | collective-permute-done | bytes 786464 | tf_op jit(solution)/shard_map/ppermute | solution.py:23
  166.7 0.9 copy-done.12
  167.6 3.7 %shard_map.54.refs_2_ = bf16[16,3,2,32,128]{4,3,2,1,0:T(8,128)(2,1)} custom-call(s32[768]{0:T(1024)} %reshape.19.pat_ref, bf16[16,6,2,32,64]{4,3,2,1,0:T(8,128)(2,1)} %bitcast.19, bf16[16,3,2,32,128]{4,3,2,1,0:T(8,128)(2,1)} %shard_map.52.refs_2_.refs_0_, bf16[16,3,2,32,128]{4,3,2,1,0:T(8,128)(2,1)} %copy-done.12, ...), custom_call_target="tpu_custom_call" | custom-call | flops 1 | bytes 1 | tf_op jit(solution)/shard_map/pallas_call | solution.py:61
  171.3 30.9 %all-to-all-done.refs_3_.refs_0_.refs_4_ = bf16[16,3,2,32,128]{4,3,2,1,0:T(8,128)(2,1)S(1)} async-done(((bf16[16,3,2,32,128]{4,3,2,1,0:T(8,128)(2,1)}), bf16[16,3,2,32,128]{4,3,2,1,0:T(8,128)(2,1)S(1)}, u32[]{:S(2)}, u32[]{:S(2)}) %all-to-all-start) | async-done | bytes 786464 | tf_op jit(solution)/shard_map/all_to_all | solution.py:203
  202.2 5.2 %all-to-all-start.2 = ((bf16[16,3,2,32,128]{4,3,2,1,0:T(8,128)(2,1)}), bf16[16,3,2,32,128]{4,3,2,1,0:T(8,128)(2,1)S(1)}, u32[]{:S(2)}, u32[]{:S(2)}) async-start(bf16[16,3,2,32,128]{4,3,2,1,0:T(8,128)(2,1)} %shard_map.54.refs_2_), calls=%async_computation.2 | async-start | bytes 1572864 | tf_op jit(solution)/shard_map/all_to_all | solution.py:203
  207.4 1.0 copy-done.7
  208.4 4.9 %shard_map.55.refs_2_.refs_0_ = bf16[16,4,2,32,128]{4,3,2,1,0:T(8,128)(2,1)} custom-call(s32[768]{0:T(1024)} %reshape.19.pat_ref, bf16[16,6,2,32,64]{4,3,2,1,0:T(8,128)(2,1)} %bitcast.28, bf16[16,4,2,32,128]{4,3,2,1,0:T(8,128)(2,1)} %shard_map.53.refs_2_.refs_0_, bf16[16,4,2,32,128]{4,3,2,1,0:T(8,128)(2,1)} %copy-done.7, ...), custom_call_target="tpu_custom_call" | custom-call | flops 1 | bytes 1 | tf_op jit(solution)/shard_map/pallas_call | solution.py:61
  213.6 3.6 %shard_map.56.refs_0_.refs_2_ = bf16[16,3,2,32,128]{4,3,2,1,0:T(8,128)(2,1)} custom-call(s32[768]{0:T(1024)} %reshape.19.pat_ref, bf16[16,6,2,32,64]{4,3,2,1,0:T(8,128)(2,1)} %bitcast.25, bf16[16,3,2,32,128]{4,3,2,1,0:T(8,128)(2,1)} %get-tuple-element.18.refs_0_, bf16[16,3,2,32,128]{4,3,2,1,0:T(8,128)(2,1)} %collective-permute-done.12.refs_1_, ...), custom_call_target="tpu_custom_call" | custom-call | flops 1 | bytes 1 | tf_op jit(solution)/shard_map/pallas_call | solution.py:61
  217.3 1.6 collective-permute-start.13
  218.9 35.9 %collective-permute-done.13.refs_1_ = bf16[16,3,2,32,128]{4,3,2,1,0:T(8,128)(2,1)S(1)} collective-permute-done((bf16[16,3,2,32,128]{4,3,2,1,0:T(8,128)(2,1)}, bf16[16,3,2,32,128]{4,3,2,1,0:T(8,128)(2,1)S(1)}, u32[]{:S(2)}, u32[]{:S(2)}) %collective-permute-start.13) | collective-permute-done | bytes 786464 | tf_op jit(solution)/shard_map/ppermute | solution.py:23
  254.8 0.9 copy-done.15
  255.7 3.7 %shard_map.57.refs_2_.refs_0_ = bf16[16,3,2,32,128]{4,3,2,1,0:T(8,128)(2,1)} custom-call(s32[768]{0:T(1024)} %reshape.19.pat_ref, bf16[16,6,2,32,64]{4,3,2,1,0:T(8,128)(2,1)} %bitcast.29, bf16[16,3,2,32,128]{4,3,2,1,0:T(8,128)(2,1)} %shard_map.56.refs_0_.refs_2_, bf16[16,3,2,32,128]{4,3,2,1,0:T(8,128)(2,1)} %copy-done.15, ...), custom_call_target="tpu_custom_call" | custom-call | flops 1 | bytes 1 | tf_op jit(solution)/shard_map/pallas_call | solution.py:61
  259.4 1.0 copy-done.8
  260.4 4.8 %shard_map.58.refs_2_ = bf16[16,4,2,32,128]{4,3,2,1,0:T(8,128)(2,1)} custom-call(s32[768]{0:T(1024)} %reshape.19.pat_ref, bf16[16,6,2,32,64]{4,3,2,1,0:T(8,128)(2,1)} %bitcast.20, bf16[16,4,2,32,128]{4,3,2,1,0:T(8,128)(2,1)} %shard_map.55.refs_2_.refs_0_, bf16[16,4,2,32,128]{4,3,2,1,0:T(8,128)(2,1)} %copy-done.8, ...), custom_call_target="tpu_custom_call" | custom-call | flops 1 | bytes 1 | tf_op jit(solution)/shard_map/pallas_call | solution.py:61
  265.1 7.7 %all-to-all-start.1 = ((bf16[16,4,2,32,128]{4,3,2,1,0:T(8,128)(2,1)}), bf16[16,4,2,32,128]{4,3,2,1,0:T(8,128)(2,1)S(1)}, u32[]{:S(2)}, u32[]{:S(2)}) async-start(bf16[16,4,2,32,128]{4,3,2,1,0:T(8,128)(2,1)} %shard_map.58.refs_2_), calls=%async_computation.1 | async-start | bytes 2097152 | tf_op jit(solution)/shard_map/all_to_all | solution.py:203
  272.8 3.0 collective-permute-start.14
  275.8 2.7 shard_map.59
  278.5 4.9 %copy.27 = bf16[96,2,32,128]{0,2,3,1:T(8,128)(2,1)} copy(bf16[96,2,32,128]{3,2,1,0:T(8,128)(2,1)} %shard_map.59) | data formatting | bytes 3145728 | tf_op jit(solution)/shard_map/pallas_call | solution.py:98
  283.4 3.0 shard_map.60.refs_3_.refs_1_
  286.3 5.5 %collective-permute-done.14.refs_1_ = bf16[16,3,2,32,128]{4,3,2,1,0:T(8,128)(2,1)S(1)} collective-permute-done((bf16[16,3,2,32,128]{4,3,2,1,0:T(8,128)(2,1)S(1)}, bf16[16,3,2,32,128]{4,3,2,1,0:T(8,128)(2,1)S(1)}, u32[]{:S(2)}, u32[]{:S(2)}) %collective-permute-start.14) | collective-permute-done | bytes 786464 | tf_op jit(solution)/shard_map/ppermute | solution.py:23
  291.8 0.9 copy-done.9
  292.7 3.7 %shard_map.61.refs_1_ = bf16[16,3,2,32,128]{4,3,2,1,0:T(8,128)(2,1)} custom-call(s32[768]{0:T(1024)} %reshape.19.pat_ref, bf16[16,6,2,32,64]{4,3,2,1,0:T(8,128)(2,1)} %bitcast.21, bf16[16,3,2,32,128]{4,3,2,1,0:T(8,128)(2,1)} %shard_map.57.refs_2_.refs_0_, bf16[16,3,2,32,128]{4,3,2,1,0:T(8,128)(2,1)} %copy-done.9, ...), custom_call_target="tpu_custom_call" | custom-call | flops 1 | bytes 1 | tf_op jit(solution)/shard_map/pallas_call | solution.py:61
  296.4 0.9 all-to-all-done.1.refs_0_
  297.2 6.7 %all-to-all-start.3 = ((bf16[16,3,2,32,128]{4,3,2,1,0:T(8,128)(2,1)}), bf16[16,3,2,32,128]{4,3,2,1,0:T(8,128)(2,1)S(1)}, u32[]{:S(2)}, u32[]{:S(2)}) async-start(bf16[16,3,2,32,128]{4,3,2,1,0:T(8,128)(2,1)} %shard_map.61.refs_1_), calls=%async_computation.3 | async-start | bytes 1572864 | tf_op jit(solution)/shard_map/all_to_all | solution.py:203
  303.9 3.3 shard_map.62
  307.2 3.8 %copy.28 = bf16[96,2,32,18]{0,2,3,1:T(8,128)(2,1)} copy(bf16[96,2,32,18]{3,2,1,0:T(8,128)(2,1)} %shard_map.62) | data formatting | bytes 442368 | tf_op jit(solution)/shard_map/pallas_call | solution.py:98
  311.0 1.7 shard_map.63.refs_2_.refs_1_
  312.7 8.9 %all-to-all-done.3.refs_1_ = bf16[16,3,2,32,128]{4,3,2,1,0:T(8,128)(2,1)S(1)} async-done(((bf16[16,3,2,32,128]{4,3,2,1,0:T(8,128)(2,1)}), bf16[16,3,2,32,128]{4,3,2,1,0:T(8,128)(2,1)S(1)}, u32[]{:S(2)}, u32[]{:S(2)}) %all-to-all-start.3) | async-done | bytes 786464 | tf_op jit(solution)/shard_map/all_to_all | solution.py:203
  321.7 0.9 copy-done.4
  322.5 2.8 shard_map.64
  325.4 4.9 %copy.29 = bf16[96,2,32,128]{0,2,3,1:T(8,128)(2,1)} copy(bf16[96,2,32,128]{3,2,1,0:T(8,128)(2,1)} %shard_map.64) | data formatting | bytes 3145728 | tf_op jit(solution)/shard_map/pallas_call | solution.py:98
  330.2 3.0 shard_map.65
  (53 shorter events, 4.8 us)
Async XLA Ops:
  0.0 1.6 slice-start
  5.2 1.6 slice-start.1
  5.2 9.8 %collective-permute-start.2 = (bf16[16,6,2,32,128]{4,3,2,1,0:T(8,128)(2,1)}, bf16[16,6,2,32,128]{4,3,2,1,0:T(8,128)(2,1)}, u32[]{:S(2)}, u32[]{:S(2)}) collective-permute-start(bf16[16,6,2,32,128]{4,3,2,1,0:T(8,128)(2,1)} %bitcast.36), channel_id=1, source_target_pairs={{0,1},{1,0},{2,3},{3,2},{4,5},{5,4},{6,7},{7,6},{8,9},{9,8},{10,11... | collective-permute-start | bytes 4718600 | tf_op jit(solution)/shard_map/ppermute | solution.py:23
  10.4 0.7 copy-start.17
  10.4 1.6 slice-start.3
  10.4 25.9 %collective-permute-start = (bf16[16,6,2,32,128]{4,3,2,1,0:T(8,128)(2,1)}, bf16[16,6,2,32,128]{4,3,2,1,0:T(8,128)(2,1)}, u32[]{:S(2)}, u32[]{:S(2)}) collective-permute-start(bf16[16,6,2,32,128]{4,3,2,1,0:T(8,128)(2,1)} %bitcast.34), channel_id=1, source_target_pairs={{0,1},{1,0},{2,3},{3,2},{4,5},{5,4},{6,7},{7,6},{8,9},{9,8},{10,11... | collective-permute-start | bytes 4718600 | tf_op jit(solution)/shard_map/ppermute | solution.py:23
  15.0 11.2 %slice-start.2 = ((bf16[96,2,32,274]{0,2,3,1:T(8,128)(2,1)}), bf16[96,2,32,18]{0,2,3,1:T(8,128)(2,1)S(1)}, s32[]{:S(2)}) async-start(bf16[96,2,32,274]{0,2,3,1:T(8,128)(2,1)} %param.4), calls=%async_computation.6 | async-start | bytes 589824 | tf_op jit(solution)/shard_map/slice | solution.py:176
  19.9 49.4 %collective-permute-start.5 = (bf16[16,3,2,32,128]{4,3,2,1,0:T(8,128)(2,1)}, bf16[16,3,2,32,128]{4,3,2,1,0:T(8,128)(2,1)}, u32[]{:S(2)}, u32[]{:S(2)}) collective-permute-start(bf16[16,3,2,32,128]{4,3,2,1,0:T(8,128)(2,1)} %get-tuple-element.15.refs_4_.refs_0_), channel_id=1, source_target_pairs={{0,2},{1,3},{2,0},{3,1},{4,6},{5,7},{6,4},{7,5},{8,10},{9,11},{10,... | collective-permute-start | bytes 2359304 | tf_op jit(solution)/shard_map/ppermute | solution.py:23
  28.3 3.9 %copy-start.6 = (bf16[16,1,2,32,128]{4,3,2,1,0:T(8,128)(2,1)}, bf16[16,1,2,32,128]{4,3,2,1,0:T(8,128)(2,1)S(1)}, u32[]{:S(2)}) copy-start(bf16[16,1,2,32,128]{4,3,2,1,0:T(8,128)(2,1)S(1)} %pad_bitcast_fusion.refs_1_) | copy-start | bytes 786436
  28.3 8.0 %collective-permute-start.1 = (bf16[16,1,2,32,128]{4,3,2,1,0:T(8,128)(2,1)S(1)}, bf16[16,1,2,32,128]{4,3,2,1,0:T(8,128)(2,1)S(1)}, u32[]{:S(2)}, u32[]{:S(2)}) collective-permute-start(bf16[16,1,2,32,128]{4,3,2,1,0:T(8,128)(2,1)S(1)} %pad_bitcast_fusion.refs_1_), channel_id=1, source_target_pairs={{0,1},{1,0},{2,3},{3,2},{4,5},{5,4},{6,7},{7,6},{8,9},{9,8},{10,11... | collective-permute-start | bytes 786440 | tf_op jit(solution)/shard_map/ppermute | solution.py:23
  32.2 4.2 %copy-start.11 = (bf16[16,3,2,32,128]{4,3,2,1,0:T(8,128)(2,1)S(1)}, bf16[16,3,2,32,128]{4,3,2,1,0:T(8,128)(2,1)}, u32[]{:S(2)}) copy-start(bf16[16,3,2,32,128]{4,3,2,1,0:T(8,128)(2,1)} %get-tuple-element.17.refs_0_) | copy-start | bytes 2359300
  36.3 58.6 %collective-permute-start.4 = (bf16[16,3,2,32,128]{4,3,2,1,0:T(8,128)(2,1)S(1)}, bf16[16,3,2,32,128]{4,3,2,1,0:T(8,128)(2,1)}, u32[]{:S(2)}, u32[]{:S(2)}) collective-permute-start(bf16[16,3,2,32,128]{4,3,2,1,0:T(8,128)(2,1)S(1)} %copy-done.11), channel_id=1, source_target_pairs={{0,2},{1,3},{2,0},{3,1},{4,6},{5,7},{6,4},{7,5},{8,10},{9,11},{10,... | collective-permute-start | bytes 2359304 | tf_op jit(solution)/shard_map/ppermute | solution.py:23
  36.3 0.7 copy-start.16
  73.1 25.6 %collective-permute-start.7 = (bf16[16,3,2,32,128]{4,3,2,1,0:T(8,128)(2,1)}, bf16[16,3,2,32,128]{4,3,2,1,0:T(8,128)(2,1)}, u32[]{:S(2)}, u32[]{:S(2)}) collective-permute-start(bf16[16,3,2,32,128]{4,3,2,1,0:T(8,128)(2,1)} %shard_map.48.refs_2_.refs_0_), channel_id=1, source_target_pairs={{0,4},{1,5},{2,6},{3,7},{4,0},{5,1},{6,2},{7,3},{8,12},{9,13},{10,... | collective-permute-start | bytes 2359304 | tf_op jit(solution)/shard_map/ppermute | solution.py:23
  98.6 12.4 %copy-start.3 = (bf16[16,3,2,32,128]{4,3,2,1,0:T(8,128)(2,1)S(1)}, bf16[16,3,2,32,128]{4,3,2,1,0:T(8,128)(2,1)}, u32[]{:S(2)}) copy-start(bf16[16,3,2,32,128]{4,3,2,1,0:T(8,128)(2,1)} %shard_map.49.refs_2_.refs_0_) | copy-start | bytes 2359300
  102.4 22.2 %collective-permute-start.8 = (bf16[16,3,2,32,128]{4,3,2,1,0:T(8,128)(2,1)}, bf16[16,3,2,32,128]{4,3,2,1,0:T(8,128)(2,1)S(1)}, u32[]{:S(2)}, u32[]{:S(2)}) collective-permute-start(bf16[16,3,2,32,128]{4,3,2,1,0:T(8,128)(2,1)} %shard_map.50.refs_0_.refs_2_), channel_id=1, source_target_pairs={{0,8},{1,9},{2,10},{3,11},{4,12},{5,13},{6,14},{7,15},{8,0},{9,1},... | collective-permute-start | bytes 2359304 | tf_op jit(solution)/shard_map/ppermute | solution.py:23
  105.6 45.3 %collective-permute-start.3 = (bf16[16,4,2,32,128]{4,3,2,1,0:T(8,128)(2,1)}, bf16[16,4,2,32,128]{4,3,2,1,0:T(8,128)(2,1)}, u32[]{:S(2)}, u32[]{:S(2)}) collective-permute-start(bf16[16,4,2,32,128]{4,3,2,1,0:T(8,128)(2,1)} %get-tuple-element.16.refs_2_.refs_0_), channel_id=1, source_target_pairs={{0,2},{1,3},{2,0},{3,1},{4,6},{5,7},{6,4},{7,5},{8,10},{9,11},{10,... | collective-permute-start | bytes 3145736 | tf_op jit(solution)/shard_map/ppermute | solution.py:23
  111.0 28.9 %collective-permute-start.6 = (bf16[16,3,2,32,128]{4,3,2,1,0:T(8,128)(2,1)S(1)}, bf16[16,3,2,32,128]{4,3,2,1,0:T(8,128)(2,1)S(1)}, u32[]{:S(2)}, u32[]{:S(2)}) collective-permute-start(bf16[16,3,2,32,128]{4,3,2,1,0:T(8,128)(2,1)S(1)} %copy-done.3), channel_id=1, source_target_pairs={{0,4},{1,5},{2,6},{3,7},{4,0},{5,1},{6,2},{7,3},{8,12},{9,13},{10,... | collective-permute-start | bytes 2359304 | tf_op jit(solution)/shard_map/ppermute | solution.py:23
  124.6 0.9 copy-start.14
  129.1 73.1 %all-to-all-start = ((bf16[16,3,2,32,128]{4,3,2,1,0:T(8,128)(2,1)}), bf16[16,3,2,32,128]{4,3,2,1,0:T(8,128)(2,1)S(1)}, u32[]{:S(2)}, u32[]{:S(2)}) async-start(bf16[16,3,2,32,128]{4,3,2,1,0:T(8,128)(2,1)} %shard_map.51.refs_2_), calls=%async_computation | async-start | bytes 1572864 | tf_op jit(solution)/shard_map/all_to_all | solution.py:203
  139.9 0.9 copy-start.13
  144.5 11.9 %copy-start.10 = (bf16[16,3,2,32,128]{4,3,2,1,0:T(8,128)(2,1)S(1)}, bf16[16,3,2,32,128]{4,3,2,1,0:T(8,128)(2,1)}, u32[]{:S(2)}) copy-start(bf16[16,3,2,32,128]{4,3,2,1,0:T(8,128)(2,1)} %get-tuple-element.18.refs_0_) | copy-start | bytes 2359300
  144.5 22.2 %collective-permute-start.10 = (bf16[16,3,2,32,128]{4,3,2,1,0:T(8,128)(2,1)}, bf16[16,3,2,32,128]{4,3,2,1,0:T(8,128)(2,1)S(1)}, u32[]{:S(2)}, u32[]{:S(2)}) collective-permute-start(bf16[16,3,2,32,128]{4,3,2,1,0:T(8,128)(2,1)} %shard_map.52.refs_2_.refs_0_), channel_id=1, source_target_pairs={{0,8},{1,9},{2,10},{3,11},{4,12},{5,13},{6,14},{7,15},{8,0},{9,1},... | collective-permute-start | bytes 2359304 | tf_op jit(solution)/shard_map/ppermute | solution.py:23
  155.7 51.7 %collective-permute-start.9 = (bf16[16,4,2,32,128]{4,3,2,1,0:T(8,128)(2,1)}, bf16[16,4,2,32,128]{4,3,2,1,0:T(8,128)(2,1)S(1)}, u32[]{:S(2)}, u32[]{:S(2)}) collective-permute-start(bf16[16,4,2,32,128]{4,3,2,1,0:T(8,128)(2,1)} %shard_map.53.refs_2_.refs_0_), channel_id=1, source_target_pairs={{0,4},{1,5},{2,6},{3,7},{4,0},{5,1},{6,2},{7,3},{8,12},{9,13},{10,... | collective-permute-start | bytes 3145736 | tf_op jit(solution)/shard_map/ppermute | solution.py:23
  156.4 57.3 %collective-permute-start.12 = (bf16[16,3,2,32,128]{4,3,2,1,0:T(8,128)(2,1)S(1)}, bf16[16,3,2,32,128]{4,3,2,1,0:T(8,128)(2,1)}, u32[]{:S(2)}, u32[]{:S(2)}) collective-permute-start(bf16[16,3,2,32,128]{4,3,2,1,0:T(8,128)(2,1)S(1)} %copy-done.10), channel_id=1, source_target_pairs={{0,2},{1,3},{2,0},{3,1},{4,6},{5,7},{6,4},{7,5},{8,10},{9,11},{10,... | collective-permute-start | bytes 2359304 | tf_op jit(solution)/shard_map/ppermute | solution.py:23
  166.7 0.9 copy-start.12
  202.2 11.0 %copy-start = (bf16[16,3,2,32,128]{4,3,2,1,0:T(8,128)(2,1)}, bf16[16,3,2,32,128]{4,3,2,1,0:T(8,128)(2,1)S(1)}, u32[]{:S(2)}) copy-start(bf16[16,3,2,32,128]{4,3,2,1,0:T(8,128)(2,1)S(1)} %all-to-all-done.refs_3_.refs_0_.refs_4_) | copy-start | bytes 2359300
  202.2 62.9 %all-to-all-start.2 = ((bf16[16,3,2,32,128]{4,3,2,1,0:T(8,128)(2,1)}), bf16[16,3,2,32,128]{4,3,2,1,0:T(8,128)(2,1)S(1)}, u32[]{:S(2)}, u32[]{:S(2)}) async-start(bf16[16,3,2,32,128]{4,3,2,1,0:T(8,128)(2,1)} %shard_map.54.refs_2_), calls=%async_computation.2 | async-start | bytes 1572864 | tf_op jit(solution)/shard_map/all_to_all | solution.py:203
  207.4 1.0 copy-start.7
  213.2 46.1 %collective-permute-start.11 = (bf16[16,4,2,32,128]{4,3,2,1,0:T(8,128)(2,1)}, bf16[16,4,2,32,128]{4,3,2,1,0:T(8,128)(2,1)S(1)}, u32[]{:S(2)}, u32[]{:S(2)}) collective-permute-start(bf16[16,4,2,32,128]{4,3,2,1,0:T(8,128)(2,1)} %shard_map.55.refs_2_.refs_0_), channel_id=1, source_target_pairs={{0,8},{1,9},{2,10},{3,11},{4,12},{5,13},{6,14},{7,15},{8,0},{9,1},... | collective-permute-start | bytes 3145736 | tf_op jit(solution)/shard_map/ppermute | solution.py:23
  217.3 37.5 %collective-permute-start.13 = (bf16[16,3,2,32,128]{4,3,2,1,0:T(8,128)(2,1)}, bf16[16,3,2,32,128]{4,3,2,1,0:T(8,128)(2,1)S(1)}, u32[]{:S(2)}, u32[]{:S(2)}) collective-permute-start(bf16[16,3,2,32,128]{4,3,2,1,0:T(8,128)(2,1)} %shard_map.56.refs_0_.refs_2_), channel_id=1, source_target_pairs={{0,4},{1,5},{2,6},{3,7},{4,0},{5,1},{6,2},{7,3},{8,12},{9,13},{10,... | collective-permute-start | bytes 2359304 | tf_op jit(solution)/shard_map/ppermute | solution.py:23
  254.8 0.9 copy-start.15
  259.4 1.0 copy-start.8
  265.1 7.7 %copy-start.2 = (bf16[16,3,2,32,128]{4,3,2,1,0:T(8,128)(2,1)S(1)}, bf16[16,3,2,32,128]{4,3,2,1,0:T(8,128)(2,1)}, u32[]{:S(2)}) copy-start(bf16[16,3,2,32,128]{4,3,2,1,0:T(8,128)(2,1)} %shard_map.57.refs_2_.refs_0_) | copy-start | bytes 2359300
  265.1 10.6 %copy-start.5 = (bf16[16,3,2,32,128]{4,3,2,1,0:T(8,128)(2,1)}, bf16[16,3,2,32,128]{4,3,2,1,0:T(8,128)(2,1)S(1)}, u32[]{:S(2)}) copy-start(bf16[16,3,2,32,128]{4,3,2,1,0:T(8,128)(2,1)S(1)} %all-to-all-done.2.refs_1_) | copy-start | bytes 2359300
  265.1 32.1 %all-to-all-start.1 = ((bf16[16,4,2,32,128]{4,3,2,1,0:T(8,128)(2,1)}), bf16[16,4,2,32,128]{4,3,2,1,0:T(8,128)(2,1)S(1)}, u32[]{:S(2)}, u32[]{:S(2)}) async-start(bf16[16,4,2,32,128]{4,3,2,1,0:T(8,128)(2,1)} %shard_map.58.refs_2_), calls=%async_computation.1 | async-start | bytes 2097152 | tf_op jit(solution)/shard_map/all_to_all | solution.py:203
  272.8 19.0 %collective-permute-start.14 = (bf16[16,3,2,32,128]{4,3,2,1,0:T(8,128)(2,1)S(1)}, bf16[16,3,2,32,128]{4,3,2,1,0:T(8,128)(2,1)S(1)}, u32[]{:S(2)}, u32[]{:S(2)}) collective-permute-start(bf16[16,3,2,32,128]{4,3,2,1,0:T(8,128)(2,1)S(1)} %copy-done.2), channel_id=1, source_target_pairs={{0,8},{1,9},{2,10},{3,11},{4,12},{5,13},{6,14},{7,15},{8,0},{9,1},... | collective-permute-start | bytes 2359304 | tf_op jit(solution)/shard_map/ppermute | solution.py:23
  291.8 0.9 copy-start.9
  297.2 6.7 %copy-start.1 = (bf16[16,4,2,32,128]{4,3,2,1,0:T(8,128)(2,1)}, bf16[16,4,2,32,128]{4,3,2,1,0:T(8,128)(2,1)S(1)}, u32[]{:S(2)}) copy-start(bf16[16,4,2,32,128]{4,3,2,1,0:T(8,128)(2,1)S(1)} %all-to-all-done.1.refs_0_) | copy-start | bytes 3145732
  297.2 24.4 %all-to-all-start.3 = ((bf16[16,3,2,32,128]{4,3,2,1,0:T(8,128)(2,1)}), bf16[16,3,2,32,128]{4,3,2,1,0:T(8,128)(2,1)S(1)}, u32[]{:S(2)}, u32[]{:S(2)}) async-start(bf16[16,3,2,32,128]{4,3,2,1,0:T(8,128)(2,1)} %shard_map.61.refs_1_), calls=%async_computation.3 | async-start | bytes 1572864 | tf_op jit(solution)/shard_map/all_to_all | solution.py:203
  321.7 0.9 copy-start.4

commit v3 on v2

v3 whole, which is shorter than its diff:
```python
import functools

import jax
import jax.numpy as jnp
from jax import lax
from jax.experimental import pallas as pl
from jax.experimental.pallas import tpu as pltpu
from jax.sharding import PartitionSpec as P

LANES = 128
TAIL = -1
FIRST = ((0, 1, 2, 3, 4, 5),)
SECOND = ((-1, 0, 1, 2), (3, 4, 5))
ORDER = ((0, 1), (0, 2), (1, 1), (1, 2), (2, 1), (0, 3), (2, 2), (1, 3), (2, 3))
WAITS = {}
EARLY = (2, 3)


def from_partner(value, mask):
    size = lax.axis_size("lat")
    return lax.ppermute(value, "lat", [(i, i ^ mask) for i in range(size)])


def product(weights, own, far):
    rhs = jnp.concatenate([own, far], axis=0)
    return jnp.dot(weights, rhs, preferred_element_type=jnp.float32)


def slot_value(slot, tail_w, per_peer, rank, term):
    if slot[0] == "m":
        return term(slot[3]).astype(jnp.bfloat16)
    lane = lax.broadcasted_iota(jnp.int32, (rank, LANES), 1)
    acc = term(0)
    for order in range(1, per_peer):
        acc = jnp.where(lane < order * tail_w, acc, term(order))
    return acc.astype(jnp.bfloat16)


def level_kernel(spec, lev, tail_w, at_ref, pat_ref, w_ref, *refs):
    n_in = spec["n_in"]
    own, far, outs = refs[:n_in], refs[n_in : 2 * n_in], refs[-spec["n_out"] :]
    peers, per_peer, boxes, rank = w_ref.shape[:4]
    total = peers * per_peer

    def group(out, slots, c, row):
        for at, slot in enumerate(slots):
            for g in range(boxes):

                def term(order):
                    sel = pat_ref[(lev * total + c * per_peer + order) * boxes + g]
                    mine, other = own[slot[1]], far[slot[1]]
                    return product(w_ref[c, order, g], mine[c, slot[2], g], other[c, slot[2], sel])

                out[row, at, g] = slot_value(slot, tail_w, per_peer, rank, term)

    if spec["spread"]:
        part = peers // len(outs)
        for d, out in enumerate(outs):
            first = (at_ref[1] ^ d) * part

            def body(i, carry):
                group(out, spec["slots"][0], first + i, i)
                return carry

            lax.fori_loop(0, part, body, 0, unroll=2)
    else:

        def body(c, carry):
            for out, slots in zip(outs, spec["slots"]):
                group(out, slots, c, c)
            return carry

        lax.fori_loop(0, peers, body, 0, unroll=4)


SMEM = pl.BlockSpec(memory_space=pltpu.SMEM)
VMEM = pl.BlockSpec(memory_space=pltpu.VMEM)
ANY = pl.BlockSpec(memory_space=pl.ANY)
CHEAP = pl.CostEstimate(flops=1, bytes_accessed=1, transcendentals=0)


def run_level(lev, tail_w, slots, at, pattern, weights, own, far, after, spread):
    peers, _, boxes, rank, _ = weights.shape
    shapes = [(peers, len(s), boxes, rank, LANES) for s in slots]
    if spread:
        shapes = [(peers // spread, *shapes[0][1:])] * spread
    spec = {"n_in": len(own), "slots": slots, "spread": spread, "n_out": len(shapes)}
    return pl.pallas_call(
        functools.partial(level_kernel, spec, lev, tail_w),
        in_specs=[SMEM, SMEM] + [VMEM] * (1 + 2 * len(own)) + [ANY] * len(after),
        out_specs=[VMEM] * len(shapes),
        out_shape=[jax.ShapeDtypeStruct(shape, jnp.bfloat16) for shape in shapes],
        cost_estimate=CHEAP,
    )(at, pattern, weights, *own, *far, *after)


def pack_kernel(at_ref, low_ref, high_ref, *outs):
    part = outs[0].shape[0]
    half = low_ref.shape[-1]
    for d, out in enumerate(outs):
        first = (at_ref[1] ^ d) * part
        out[:, :, :, :, :half] = low_ref[pl.ds(first, part)]
        out[:, :, :, :, half:] = high_ref[pl.ds(first, part)]


def pack(at, low, high, ys):
    peers, per_peer, boxes, rank, half = low.shape
    shape = jax.ShapeDtypeStruct((peers // ys, per_peer, boxes, rank, 2 * half), jnp.bfloat16)
    return pl.pallas_call(
        pack_kernel,
        in_specs=[SMEM, VMEM, VMEM],
        out_specs=[VMEM] * ys,
        out_shape=[shape] * ys,
        cost_estimate=CHEAP,
    )(at, low, high)


def last_kernel(spec, tail_w, pat_ref, *refs):
    ys, slots = spec["ys"], spec["slots"]
    weights, blocks = refs[:ys], refs[ys : 2 * ys]
    outs, mid = refs[-ys - 1 : -1], refs[-1]
    part, per_peer, boxes, rank, width = weights[0].shape
    half = width // 2

    def level(step, i, source, target):
        for d in range(ys):
            for at, slot in enumerate(slots):
                for g in range(boxes):

                    def term(order):
                        sel = pat_ref[(((d * 2 + step) * part + i) * per_peer + order) * boxes + g]
                        w = weights[d][i, order, g][:, step * half : (step + 1) * half]
                        return product(w, source(d)[i, at, g], source(d ^ (1 + step))[i, at, sel])

                    target(d)[i, at, g] = slot_value(slot, tail_w, per_peer, rank, term)

    def first(i, carry):
        level(0, i, lambda d: blocks[d], lambda d: mid.at[d])
        return carry

    def second(i, carry):
        level(1, i, lambda d: mid.at[d], lambda d: outs[d])
        return carry

    lax.fori_loop(0, part, first, 0)
    lax.fori_loop(0, part, second, 0)


def run_last(tail_w, slots, pattern, weights, blocks, after):
    ys = len(blocks)
    shape = jax.ShapeDtypeStruct(blocks[0].shape, jnp.bfloat16)
    return pl.pallas_call(
        functools.partial(last_kernel, {"ys": ys, "slots": slots}, tail_w),
        in_specs=[SMEM] + [VMEM] * (2 * ys) + [ANY] * len(after),
        out_specs=[VMEM] * ys,
        out_shape=[shape] * ys,
        scratch_shapes=[pltpu.VMEM((ys, *blocks[0].shape), jnp.bfloat16)],
        cost_estimate=CHEAP,
    )(pattern, *weights, *blocks, *after)


def join_kernel(ys, at_ref, *refs):
    out = refs[-1]
    part = refs[0].shape[0]
    for d in range(ys):
        first = (at_ref[1] ^ d) * part
        out[pl.ds(first, part)] = refs[d][...]


def join(at, parts, after):
    ys = len(parts)
    part, *rest = parts[0].shape
    return pl.pallas_call(
        functools.partial(join_kernel, ys),
        in_specs=[SMEM] + [VMEM] * ys + [ANY] * len(after),
        out_specs=VMEM,
        out_shape=jax.ShapeDtypeStruct((ys * part, *rest), jnp.bfloat16),
        cost_estimate=CHEAP,
    )(at, *parts, *after)


def place_kernel(tail_w, slots, me_ref, assign_ref, *refs):
    out_ref = refs[-1]
    peers, per_peer, boxes = refs[0].shape[0], len(slots), refs[0].shape[2]
    local = peers * per_peer
    me = me_ref[0]

    def peer(k, carry):
        for j, (src, at) in enumerate(slots):
            to = assign_ref[k * local + me * per_peer + j] - me * local
            for g in range(boxes):
                value = refs[src][k, at, g]
                if out_ref.shape[-1] < LANES:
                    value = value.astype(jnp.float32)
                    if j:
                        value = pltpu.roll(value, LANES - j * tail_w, 1)
                    value = value[:, :tail_w].astype(jnp.bfloat16)
                out_ref[to, g] = value
        return carry

    lax.fori_loop(0, peers, peer, 0, unroll=2)


def place(tail_w, slots, parts, me, assign, cols, after=()):
    peers, _, boxes, rank, _ = parts[0].shape
    vmem = pl.BlockSpec(memory_space=pltpu.VMEM)
    smem = pl.BlockSpec(memory_space=pltpu.SMEM)
    return pl.pallas_call(
        functools.partial(place_kernel, tail_w, slots),
        in_specs=[smem, smem] + [vmem] * len(parts) + [pl.BlockSpec(memory_space=pl.ANY)] * len(after),
        out_specs=vmem,
        out_shape=jax.ShapeDtypeStruct((peers * len(slots), boxes, rank, cols), jnp.bfloat16),
        cost_estimate=pl.CostEstimate(flops=1, bytes_accessed=1, transcendentals=0),
    )(me, assign, *parts, *after)


def store_kernel(start, *refs):
    piece, out, sems = refs[0], refs[-2], refs[-1]
    boxes, width = piece.shape[:2]
    part = width // sems.shape[1]
    copies = [
        pltpu.make_async_copy(
            piece.at[g, pl.ds(q * part, part)], out.at[g, pl.ds(start + q * part, part)], sems.at[g, q]
        )
        for g in range(boxes)
        for q in range(sems.shape[1])
    ]
    for copy in copies:
        copy.start()
    for copy in copies:
        copy.wait()


def store(piece, start, cols, whole=None):
    boxes, _, rank, local = piece.shape
    held = [] if whole is None else [whole]
    return pl.pallas_call(
        functools.partial(store_kernel, start),
        in_specs=[pl.BlockSpec(memory_space=pltpu.VMEM)] + [pl.BlockSpec(memory_space=pl.ANY)] * len(held),
        out_specs=pl.BlockSpec(memory_space=pl.ANY),
        out_shape=jax.ShapeDtypeStruct((boxes, cols, rank, local), jnp.bfloat16),
        scratch_shapes=[pltpu.SemaphoreType.DMA((boxes, 4 if piece.shape[1] % 4 == 0 else 1))],
        input_output_aliases={1: 0} if held else {},
        cost_estimate=pl.CostEstimate(flops=1, bytes_accessed=1, transcendentals=0),
    )(piece, *held)


def per_device(coeffs, coupling, pattern, assign):
    local, boxes, rank, cols = coeffs.shape
    peers = lax.axis_size("order")
    per_peer = local // peers
    tail_w = cols - 2 * LANES
    order_at = lax.axis_index("order").astype(jnp.int32)
    lat_at = lax.axis_index("lat").astype(jnp.int32)
    ys = lax.axis_size("lat") >> 2
    me = jnp.stack([order_at, lat_at >> 2])

    def six(x):
        return x.reshape(peers, per_peer, boxes, rank, x.shape[-1])

    def level_weights(c, l):
        return six(c[l])

    first = six(coeffs[..., :LANES])
    coeffs, coupling_later, first = lax.optimization_barrier((coeffs, coupling, first))
    first_far = from_partner(first, 1)
    weights = [level_weights(coupling, 0)] + [level_weights(coupling_later, l) for l in range(1, coupling.shape[0])]
    flat_pattern = pattern.reshape(-1)

    after = []

    def level(lev, slots, own, far, spread=0):
        outs = run_level(lev, tail_w, slots, me, flat_pattern, weights[lev], own, far, after, spread)
        after[:] = outs[:1]
        return outs

    def split(groups, tail_at):
        return [[("t", tail_at, 0) if j == TAIL else ("m", 0, j, j) for j in group] for group in groups]

    def own_slots(group):
        return [("t", 0, i) if j == TAIL else ("m", 0, i, j) for i, j in enumerate(group)]

    def places(members):
        arrays, found = [], {}
        for m in members:
            array, offset = done[m]
            if not arrays or arrays[-1] is not array:
                arrays.append(array)
            for i, j in enumerate(groups[m]):
                found[j] = (len(arrays) - 1, offset + i)
        return [found[j] for j in range(per_peer)], arrays

    chunks = list(level(0, split(FIRST, 0), [first], [first_far]))
    second = six(coeffs[..., LANES : 2 * LANES])
    tail = six(coeffs[..., 2 * LANES :]).transpose(0, 2, 3, 1, 4).reshape(peers, boxes, rank, per_peer * tail_w)
    tail = jnp.pad(tail, ((0, 0), (0, 0), (0, 0), (0, LANES - per_peer * tail_w)))[:, None]
    chunks += level(
        0, split(SECOND, 1), [second, tail], [from_partner(second, 1), from_partner(tail, 1)]
    )
    groups = FIRST + SECOND
    tail_chunk = [TAIL in group for group in groups].index(True)
    far = [from_partner(chunk, 2) for chunk in chunks]
    packed = pack(me, weights[2], weights[3], ys)
    packed = [packed[0]] + [from_partner(packed[d], 4 * d) for d in range(1, ys)]
    after.append(packed[0])
    by_peer = pattern[2:].reshape(2, ys, -1).transpose(1, 0, 2).reshape(ys, -1)
    choices = [lax.dynamic_index_in_dim(by_peer, me[1] ^ d, 0, keepdims=False) for d in range(ys)]
    choices = jnp.concatenate([choices[0]] + [from_partner(choices[d], 4 * d) for d in range(1, ys)])

    where = [own_slots(group) for group in groups]
    done = [None] * len(chunks)
    whole = None
    for k, step in ORDER:
        if (k, step) == EARLY:
            early = place(tail_w, *places(range(len(FIRST))), me, assign, LANES)
            whole = store(early.transpose(1, 3, 2, 0), 0, cols)
            after.append(whole)
        after += [done[w][0] for w in WAITS.get((k, step), ())]
        if step == 1:
            outs = level(1, [where[k]], [chunks[k]], [far[k]], ys)
        elif step == 2:
            outs = run_last(tail_w, where[k], choices, packed, chunks[k], after)
        else:
            outs = [join(me, chunks[k], after)]
            done[k] = (lax.all_to_all(outs[0], "order", split_axis=0, concat_axis=0, tiled=True), 0)
        after[:] = outs[:1]
        chunks[k] = [outs[0]] + [from_partner(out, 4 * (d + 1)) for d, out in enumerate(outs[1:])]
    array, offset = done[tail_chunk]
    tail_slot = offset + groups[tail_chunk].index(TAIL)
    ends = place(tail_w, [(0, tail_slot)] * per_peer, [array], me, assign, tail_w, after)
    whole = store(ends.transpose(1, 3, 2, 0), 2 * LANES, cols, whole)
    late = place(tail_w, *places(range(len(FIRST), len(groups))), me, assign, LANES, [whole])
    whole = store(late.transpose(1, 3, 2, 0), LANES, cols, whole)
    return whole.transpose(3, 0, 2, 1)


def solution(mesh):
    return jax.shard_map(
        per_device,
        mesh=mesh,
        in_specs=(
            P("order", "lat", None, None),
            P(None, "order", "lat", None, None),
            P(None, "order", "lat"),
            P(),
        ),
        out_specs=P("order", "lat", None, None),
        check_vma=False,
    )
```

time: 334 us -> 314 us (0.940)
  waiting for transfers between devices: 147 us -> 95.2 us
  starting transfers between devices: 58.2 us -> 94 us
  Pallas kernels: 74.8 us -> 68.6 us
    all_to_all x4 -> x3, waiting for transfers between devices: 40.7 us -> 5.12 us  [per_device(): lax.all_to_all(outs[0], 'order', split_axis=0, concat_axis=0, tiled=True)]
    pallas_call x14 -> x5, Pallas kernels: 58.3 us -> 25.2 us  [run_level(): pl.pallas_call(functools.partial(level_kernel, spec, lev, tail_w), in_spe...]
    pallas_call x0 -> x7, Pallas kernels: none -> 26.9 us  [the longest x3 16.4 us: run_last(): pl.pallas_call(functools.partial(last_kernel, {'ys': ys, 'slots': slots},...]
    ppermute x15 -> x30, starting transfers between devices: 30.2 us -> 53.5 us  [from_partner(): return lax.ppermute(value, 'lat', [(i, i ^ mask) for i in range(size)])]
    ppermute x15 -> x30, waiting for transfers between devices: 107 us -> 90.1 us  [from_partner(): return lax.ppermute(value, 'lat', [(i, i ^ mask) for i in range(size)])]
    all_to_all x4 -> x3, starting transfers between devices: 28 us -> 40.5 us  [per_device(): lax.all_to_all(outs[0], 'order', split_axis=0, concat_axis=0, tiled=True)]
    unnamed x37 -> x65, local copies, waits for them, and re-layouts: 8.89 us -> 9.16 us
  transfers between devices with their start and end apart: 19 -> 33, of which waited for: 11 -> 14; matrix products, arithmetic and copies ran while one was open for 10% -> 10% of each run, Pallas kernels for 20% -> 19%
where the time goes in v3:
time: 314 us; the launch traced here: 311 us
  waiting for transfers between devices  95.2 us (30%)
  starting transfers between devices  94 us (30%)
  Pallas kernels  68.6 us (22%)
  local copies, waits for them, and re-layouts  51 us (16%)
    ppermute x30, waiting for transfers between devices, from_partner(): return lax.ppermute(value, 'lat', [(i, i ^ mask) for i in range(size)])  90.1 us
    ppermute x30, starting transfers between devices, from_partner(): return lax.ppermute(value, 'lat', [(i, i ^ mask) for i in range(size)])  53.5 us
    all_to_all x3, starting transfers between devices, per_device(): lax.all_to_all(outs[0], 'order', split_axis=0, concat_axis=0, tiled=True)  40.5 us
    pallas_call x5, Pallas kernels, run_level(): pl.pallas_call(functools.partial(level_kernel, spec, lev, tail_w), in_spe...  25.2 us
    pallas_call x3, Pallas kernels, run_last(): pl.pallas_call(functools.partial(last_kernel, {'ys': ys, 'slots': slots},...  16.4 us
    slice x7, local copies, waits for them, and re-layouts, level_weights(): return six(c[l])  14.8 us
    pallas_call x3, local copies, waits for them, and re-layouts, place(): pl.pallas_call(functools.partial(place_kernel, tail_w, slots), in_specs=[...  13.6 us
    unnamed x65, local copies, waits for them, and re-layouts  9.16 us
  transfers between devices with their start and end apart: 33, of which 14 were waited for; matrix products, arithmetic and copies ran while one was open for 10% of the time, Pallas kernels for 19%

profile of v3, /device:TPU:32, one launch (start us, length us, event | category | flops | bytes accessed | tf_op | source)
XLA Modules:
  0.0 310.6 jit_solution(17488041923224503955)
XLA Ops:
  0.0 1.6 slice-done
  1.6 3.6 %copy.33 = bf16[96,2,32,128]{3,2,1,0:T(8,128)(2,1)} copy(bf16[96,2,32,128]{0,2,3,1:T(8,128)(2,1)S(1)} %slice-done) | data formatting | bytes 3145728 | tf_op jit(solution)/shard_map/slice | solution.py:264
  5.2 1.6 slice-done.1
  6.7 3.6 %copy.39 = bf16[96,2,32,128]{3,2,1,0:T(8,128)(2,1)} copy(bf16[96,2,32,128]{0,2,3,1:T(8,128)(2,1)S(1)} %slice-done.1) | data formatting | bytes 3145728 | tf_op jit(solution)/shard_map/slice | solution.py:294
  11.9 3.0 copy.38
  15.6 4.9 %shard_map.47.refs_4_.refs_0_ = bf16[16,6,2,32,128]{4,3,2,1,0:T(8,128)(2,1)} custom-call(s32[2]{0:T(128)} %pad_add_fusion.1.at_ref.me_ref, s32[768]{0:T(1024)} %reshape.24.pat_ref, bf16[16,6,2,32,64]{4,3,2,1,0:T(8,128)(2,1)} %bitcast.31, bf16[16,6,2,32,128]{4,3,2,1,0:T(8,128)(2,1)} %bitcast.38, bf16[16,6,2,32,128]{4,3,2,1,0:T(8,128)(2,1)} %collective-permute-done.8.refs_1_), custom_call_target="tpu_custom_call" | custom-call | flops 1 | bytes 1 | tf_op jit(solution)/shard_map/pallas_call | solution.py:88
  20.4 6.3 %collective-permute-start.10 = (bf16[16,6,2,32,128]{4,3,2,1,0:T(8,128)(2,1)}, bf16[16,6,2,32,128]{4,3,2,1,0:T(8,128)(2,1)}, u32[]{:S(2)}, u32[]{:S(2)}) collective-permute-start(bf16[16,6,2,32,128]{4,3,2,1,0:T(8,128)(2,1)} %shard_map.47.refs_4_.refs_0_), channel_id=1, source_target_pairs={{0,2},{1,3},{2,0},{3,1},{4,6},{5,7},{6,4},{7,5},{8,10},{9,11},{10,... | collective-permute-start | bytes 4718600 | tf_op jit(solution)/shard_map/ppermute | solution.py:21
  29.0 1.5 collective-permute-done.7.refs_3_
  32.3 5.9 %shard_map.48 = (bf16[16,4,2,32,128]{4,3,2,1,0:T(8,128)(2,1)}, bf16[16,3,2,32,128]{4,3,2,1,0:T(8,128)(2,1)}) custom-call(s32[2]{0:T(128)} %pad_add_fusion.1.at_ref.me_ref, s32[768]{0:T(1024)} %reshape.24.pat_ref, bf16[16,6,2,32,64]{4,3,2,1,0:T(8,128)(2,1)} %bitcast.32, bf16[16,6,2,32,128]{4,3,2,1,0:T(8,128)(2,1)} %bitcast.36, ...), custom_call_target="tpu_custom_call" | custom-call | flops 1 | bytes 1 | tf_op jit(solution)/shard_map/pallas_call | solution.py:88
  38.2 2.5 fusion.4
  40.8 3.0 copy.34
  43.8 3.1 copy.35
  46.9 3.6 %shard_map.46 = (bf16[4,6,2,32,128]{4,3,2,1,0:T(8,128)(2,1)}, bf16[4,6,2,32,128]{4,3,2,1,0:T(8,128)(2,1)}, bf16[4,6,2,32,128]{4,3,2,1,0:T(8,128)(2,1)}, bf16[4,6,2,32,128]{4,3,2,1,0:T(8,128)(2,1)}) custom-call(s32[2]{0:T(128)} %pad_add_fusion.1.at_ref.me_ref, bf16[16,6,2,32,64]{4,3,2,1,0:T(8,128)(2,1)} %bitcast.39, bf16[16,6,2,32,64]{4,3,2,1,0:T(8,128)(2,1)} %bitcast.40), custom_call_target="tpu_custom_call" | custom-call | flops 1 | bytes 1 | tf_op jit(solution)/shard_map/pallas_call | solution.py:109
  50.5 1.6 collective-permute-start.3
  52.1 2.9 collective-permute-start.4
  55.7 14.6 %collective-permute-done = s32[96]{0:T(128)S(1)} collective-permute-done((s32[96]{0:T(128)S(1)}, s32[96]{0:T(128)S(1)}, u32[]{:S(2)}, u32[]{:S(2)}) %collective-permute-start) | collective-permute-done | bytes 416 | tf_op jit(solution)/shard_map/ppermute | solution.py:21
  70.3 3.2 %collective-permute-start.1 = (s32[96]{0:T(128)S(1)}, s32[96]{0:T(128)S(1)}, u32[]{:S(2)}, u32[]{:S(2)}) collective-permute-start(s32[96]{0:T(128)S(1)} %get-tuple-element.76), channel_id=1, source_target_pairs={{0,8},{1,9},{2,10},{3,11},{4,12},{5,13},{6,14},{7,15},{8,0},{9,1},... | collective-permute-start | bytes 1160 | tf_op jit(solution)/shard_map/ppermute | solution.py:21
  73.5 1.9 collective-permute-done.1
  75.3 3.0 collective-permute-start.5
  78.3 25.4 %collective-permute-done.10.refs_1_ = bf16[16,6,2,32,128]{4,3,2,1,0:T(8,128)(2,1)} collective-permute-done((bf16[16,6,2,32,128]{4,3,2,1,0:T(8,128)(2,1)}, bf16[16,6,2,32,128]{4,3,2,1,0:T(8,128)(2,1)}, u32[]{:S(2)}, u32[]{:S(2)}) %collective-permute-start.10) | collective-permute-done | bytes 1572896 | tf_op jit(solution)/shard_map/ppermute | solution.py:21
  103.7 3.0 collective-permute-start.2
  106.7 3.0 copy.37
  109.8 5.3 %shard_map.49 = (bf16[4,6,2,32,128]{4,3,2,1,0:T(8,128)(2,1)}, bf16[4,6,2,32,128]{4,3,2,1,0:T(8,128)(2,1)}, bf16[4,6,2,32,128]{4,3,2,1,0:T(8,128)(2,1)}, bf16[4,6,2,32,128]{4,3,2,1,0:T(8,128)(2,1)}) custom-call(s32[2]{0:T(128)} %pad_add_fusion.1.at_ref.me_ref, s32[768]{0:T(1024)} %reshape.24.pat_ref, bf16[16,6,2,32,64]{4,3,2,1,0:T(8,128)(2,1)} %bitcast.28, ...), custom_call_target="tpu_custom_call" | custom-call | flops 1 | bytes 1 | tf_op jit(solution)/shard_map/pallas_call | solution.py:88
  115.2 1.6 collective-permute-start.12
  116.7 3.0 collective-permute-start.13
  119.8 6.0 %collective-permute-start.20 = (bf16[16,3,2,32,128]{4,3,2,1,0:T(8,128)(2,1)S(1)}, bf16[16,3,2,32,128]{4,3,2,1,0:T(8,128)(2,1)S(1)}, u32[]{:S(2)}, u32[]{:S(2)}) collective-permute-start(bf16[16,3,2,32,128]{4,3,2,1,0:T(8,128)(2,1)S(1)} %copy-done.8), channel_id=1, source_target_pairs={{0,2},{1,3},{2,0},{3,1},{4,6},{5,7},{6,4},{7,5},{8,10},{9,11},{10,... | collective-permute-start | bytes 2359304 | tf_op jit(solution)/shard_map/ppermute | solution.py:21
  127.3 5.2 %collective-permute-done.12.refs_6_ = bf16[4,6,2,32,128]{4,3,2,1,0:T(8,128)(2,1)} collective-permute-done((bf16[4,6,2,32,128]{4,3,2,1,0:T(8,128)(2,1)}, bf16[4,6,2,32,128]{4,3,2,1,0:T(8,128)(2,1)}, u32[]{:S(2)}, u32[]{:S(2)}) %collective-permute-start.12) | collective-permute-done | bytes 393248 | tf_op jit(solution)/shard_map/ppermute | solution.py:21
  132.5 2.6 collective-permute-done.13.refs_7_
  135.1 5.7 %shard_map.50 = (bf16[4,6,2,32,128]{4,3,2,1,0:T(8,128)(2,1)}, bf16[4,6,2,32,128]{4,3,2,1,0:T(8,128)(2,1)}, bf16[4,6,2,32,128]{4,3,2,1,0:T(8,128)(2,1)}, bf16[4,6,2,32,128]{4,3,2,1,0:T(8,128)(2,1)}) custom-call(s32[384]{0:T(512)} %pad_add_fusion.pat_ref, bf16[4,6,2,32,128]{4,3,2,1,0:T(8,128)(2,1)} %get-tuple-element.39.refs_3_.refs_0_, ...), custom_call_target="tpu_custom_call" | custom-call | flops 1 | bytes 1 | tf_op jit(solution)/shard_map/pallas_call | solution.py:152
  140.9 5.1 %collective-permute-done.9.refs_1_ = bf16[16,4,2,32,128]{4,3,2,1,0:T(8,128)(2,1)} collective-permute-done((bf16[16,4,2,32,128]{4,3,2,1,0:T(8,128)(2,1)}, bf16[16,4,2,32,128]{4,3,2,1,0:T(8,128)(2,1)}, u32[]{:S(2)}, u32[]{:S(2)}) %collective-permute-start.9) | collective-permute-done | bytes 1048608 | tf_op jit(solution)/shard_map/ppermute | solution.py:21
  145.9 5.1 %shard_map.51 = (bf16[4,4,2,32,128]{4,3,2,1,0:T(8,128)(2,1)}, bf16[4,4,2,32,128]{4,3,2,1,0:T(8,128)(2,1)}, bf16[4,4,2,32,128]{4,3,2,1,0:T(8,128)(2,1)}, bf16[4,4,2,32,128]{4,3,2,1,0:T(8,128)(2,1)}) custom-call(s32[2]{0:T(128)} %pad_add_fusion.1.at_ref.me_ref, s32[768]{0:T(1024)} %reshape.24.pat_ref, bf16[16,6,2,32,64]{4,3,2,1,0:T(8,128)(2,1)} %bitcast.29, ...), custom_call_target="tpu_custom_call" | custom-call | flops 1 | bytes 1 | tf_op jit(solution)/shard_map/pallas_call | solution.py:88
  151.0 1.6 collective-permute-start.14
  152.6 2.9 collective-permute-start.15
  155.6 1.6 collective-permute-start.25
  157.2 3.3 %collective-permute-done.14.refs_5_ = bf16[4,4,2,32,128]{4,3,2,1,0:T(8,128)(2,1)S(1)} collective-permute-done((bf16[4,4,2,32,128]{4,3,2,1,0:T(8,128)(2,1)}, bf16[4,4,2,32,128]{4,3,2,1,0:T(8,128)(2,1)S(1)}, u32[]{:S(2)}, u32[]{:S(2)}) %collective-permute-start.14) | collective-permute-done | bytes 262176 | tf_op jit(solution)/shard_map/ppermute | solution.py:21
  160.5 3.0 collective-permute-start.26
  163.5 5.2 %collective-permute-done.15.refs_6_ = bf16[4,4,2,32,128]{4,3,2,1,0:T(8,128)(2,1)S(1)} collective-permute-done((bf16[4,4,2,32,128]{4,3,2,1,0:T(8,128)(2,1)}, bf16[4,4,2,32,128]{4,3,2,1,0:T(8,128)(2,1)S(1)}, u32[]{:S(2)}, u32[]{:S(2)}) %collective-permute-start.15) | collective-permute-done | bytes 262176 | tf_op jit(solution)/shard_map/ppermute | solution.py:21
  168.9 14.6 %collective-permute-done.16.refs_7_ = bf16[4,4,2,32,128]{4,3,2,1,0:T(8,128)(2,1)S(1)} collective-permute-done((bf16[4,4,2,32,128]{4,3,2,1,0:T(8,128)(2,1)}, bf16[4,4,2,32,128]{4,3,2,1,0:T(8,128)(2,1)S(1)}, u32[]{:S(2)}, u32[]{:S(2)}) %collective-permute-start.16) | collective-permute-done | bytes 262176 | tf_op jit(solution)/shard_map/ppermute | solution.py:21
  184.2 6.2 %shard_map.52 = (bf16[4,4,2,32,128]{4,3,2,1,0:T(8,128)(2,1)}, bf16[4,4,2,32,128]{4,3,2,1,0:T(8,128)(2,1)}, bf16[4,4,2,32,128]{4,3,2,1,0:T(8,128)(2,1)}, bf16[4,4,2,32,128]{4,3,2,1,0:T(8,128)(2,1)}) custom-call(s32[384]{0:T(512)} %pad_add_fusion.pat_ref, bf16[4,6,2,32,128]{4,3,2,1,0:T(8,128)(2,1)} %get-tuple-element.39.refs_3_.refs_0_, ...), custom_call_target="tpu_custom_call" | custom-call | flops 1 | bytes 1 | tf_op jit(solution)/shard_map/pallas_call | solution.py:152
  191.3 4.0 %shard_map.53 = (bf16[4,3,2,32,128]{4,3,2,1,0:T(8,128)(2,1)}, bf16[4,3,2,32,128]{4,3,2,1,0:T(8,128)(2,1)}, bf16[4,3,2,32,128]{4,3,2,1,0:T(8,128)(2,1)}, bf16[4,3,2,32,128]{4,3,2,1,0:T(8,128)(2,1)}) custom-call(s32[2]{0:T(128)} %pad_add_fusion.1.at_ref.me_ref, s32[768]{0:T(1024)} %reshape.24.pat_ref, bf16[16,6,2,32,64]{4,3,2,1,0:T(8,128)(2,1)} %bitcast.30, ...), custom_call_target="tpu_custom_call" | custom-call | flops 1 | bytes 1 | tf_op jit(solution)/shard_map/pallas_call | solution.py:88
  196.4 2.6 shard_map.54.refs_8_
  199.0 25.3 %all-to-all-start.1 = ((bf16[16,6,2,32,128]{4,3,2,1,0:T(8,128)(2,1)}), bf16[16,6,2,32,128]{4,3,2,1,0:T(8,128)(2,1)S(1)}, u32[]{:S(2)}, u32[]{:S(2)}) async-start(bf16[16,6,2,32,128]{4,3,2,1,0:T(8,128)(2,1)} %shard_map.54.refs_8_), calls=%async_computation.1 | async-start | bytes 3145728 | tf_op jit(solution)/shard_map/all_to_all | solution.py:325
  224.4 2.0 collective-permute-start.17
  226.4 1.4 collective-permute-start.18
  229.2 2.0 collective-permute-start.22
  232.6 6.6 %collective-permute-done.22.refs_6_ = bf16[4,3,2,32,128]{4,3,2,1,0:T(8,128)(2,1)S(1)} collective-permute-done((bf16[4,3,2,32,128]{4,3,2,1,0:T(8,128)(2,1)}, bf16[4,3,2,32,128]{4,3,2,1,0:T(8,128)(2,1)S(1)}, u32[]{:S(2)}, u32[]{:S(2)}) %collective-permute-start.22) | collective-permute-done | bytes 196640 | tf_op jit(solution)/shard_map/ppermute | solution.py:21
  239.2 3.2 %collective-permute-done.23.refs_7_ = bf16[4,3,2,32,128]{4,3,2,1,0:T(8,128)(2,1)S(1)} collective-permute-done((bf16[4,3,2,32,128]{4,3,2,1,0:T(8,128)(2,1)}, bf16[4,3,2,32,128]{4,3,2,1,0:T(8,128)(2,1)S(1)}, u32[]{:S(2)}, u32[]{:S(2)}) %collective-permute-start.23) | collective-permute-done | bytes 196640 | tf_op jit(solution)/shard_map/ppermute | solution.py:21
  243.1 4.5 %shard_map.55 = (bf16[4,3,2,32,128]{4,3,2,1,0:T(8,128)(2,1)}, bf16[4,3,2,32,128]{4,3,2,1,0:T(8,128)(2,1)}, bf16[4,3,2,32,128]{4,3,2,1,0:T(8,128)(2,1)}, bf16[4,3,2,32,128]{4,3,2,1,0:T(8,128)(2,1)}) custom-call(s32[384]{0:T(512)} %pad_add_fusion.pat_ref, bf16[4,6,2,32,128]{4,3,2,1,0:T(8,128)(2,1)} %get-tuple-element.39.refs_3_.refs_0_, ...), custom_call_target="tpu_custom_call" | custom-call | flops 1 | bytes 1 | tf_op jit(solution)/shard_map/pallas_call | solution.py:152
  248.5 2.3 shard_map.56.refs_4_
  250.8 7.7 %all-to-all-start = ((bf16[16,4,2,32,128]{4,3,2,1,0:T(8,128)(2,1)}), bf16[16,4,2,32,128]{4,3,2,1,0:T(8,128)(2,1)S(1)}, u32[]{:S(2)}, u32[]{:S(2)}) async-start(bf16[16,4,2,32,128]{4,3,2,1,0:T(8,128)(2,1)} %shard_map.56.refs_4_), calls=%async_computation | async-start | bytes 2097152 | tf_op jit(solution)/shard_map/all_to_all | solution.py:325
  258.6 2.7 collective-permute-start.28
  261.3 1.9 collective-permute-start.29
  263.2 2.8 shard_map.57
  266.0 4.9 %copy.43 = bf16[96,2,32,128]{0,2,3,1:T(8,128)(2,1)} copy(bf16[96,2,32,128]{3,2,1,0:T(8,128)(2,1)} %shard_map.57) | data formatting | bytes 3145728 | tf_op jit(solution)/shard_map/pallas_call | solution.py:208
  270.8 3.0 shard_map.58.refs_5_.refs_1_
  275.2 2.2 shard_map.59.refs_1_
  277.4 7.5 %all-to-all-start.2 = ((bf16[16,3,2,32,128]{4,3,2,1,0:T(8,128)(2,1)}), bf16[16,3,2,32,128]{4,3,2,1,0:T(8,128)(2,1)S(1)}, u32[]{:S(2)}, u32[]{:S(2)}) async-start(bf16[16,3,2,32,128]{4,3,2,1,0:T(8,128)(2,1)} %shard_map.59.refs_1_), calls=%async_computation.2 | async-start | bytes 1572864 | tf_op jit(solution)/shard_map/all_to_all | solution.py:325
  284.9 3.3 %shard_map.60 = bf16[96,2,32,18]{3,2,1,0:T(8,128)(2,1)} custom-call(s32[2]{0:T(128)} %pad_add_fusion.1.at_ref.me_ref, s32[1536]{0:T(1024)} %assign_ref.5, bf16[16,4,2,32,128]{4,3,2,1,0:T(8,128)(2,1)} %copy-done, bf16[16,3,2,32,128]{4,3,2,1,0:T(8,128)(2,1)} %shard_map.59.refs_1_), custom_call_target="tpu_custom_call" | custom-call | flops 1 | bytes 1 | tf_op jit(solution)/shard_map/pallas_call | solution.py:208
  288.2 3.8 %copy.44 = bf16[96,2,32,18]{0,2,3,1:T(8,128)(2,1)} copy(bf16[96,2,32,18]{3,2,1,0:T(8,128)(2,1)} %shard_map.60) | data formatting | bytes 442368 | tf_op jit(solution)/shard_map/pallas_call | solution.py:208
  292.0 1.7 shard_map.61.refs_2_.refs_1_
  293.7 5.1 %all-to-all-done.2.refs_1_ = bf16[16,3,2,32,128]{4,3,2,1,0:T(8,128)(2,1)S(1)} async-done(((bf16[16,3,2,32,128]{4,3,2,1,0:T(8,128)(2,1)}), bf16[16,3,2,32,128]{4,3,2,1,0:T(8,128)(2,1)S(1)}, u32[]{:S(2)}, u32[]{:S(2)}) %all-to-all-start.2) | async-done | bytes 786464 | tf_op jit(solution)/shard_map/all_to_all | solution.py:325
  299.8 2.8 shard_map.62
  302.6 4.9 %copy.45 = bf16[96,2,32,128]{0,2,3,1:T(8,128)(2,1)} copy(bf16[96,2,32,128]{3,2,1,0:T(8,128)(2,1)} %shard_map.62) | data formatting | bytes 3145728 | tf_op jit(solution)/shard_map/pallas_call | solution.py:208
  307.5 3.0 shard_map.63
  (116 shorter events, 18.5 us)
Async XLA Ops:
  0.0 1.6 slice-start
  5.1 1.6 slice-start.1
  5.1 10.4 %collective-permute-start.8 = (bf16[16,6,2,32,128]{4,3,2,1,0:T(8,128)(2,1)}, bf16[16,6,2,32,128]{4,3,2,1,0:T(8,128)(2,1)}, u32[]{:S(2)}, u32[]{:S(2)}) collective-permute-start(bf16[16,6,2,32,128]{4,3,2,1,0:T(8,128)(2,1)} %bitcast.37), channel_id=1, source_target_pairs={{0,1},{1,0},{2,3},{3,2},{4,5},{5,4},{6,7},{7,6},{8,9},{9,8},{10,11... | collective-permute-start | bytes 4718600 | tf_op jit(solution)/shard_map/ppermute | solution.py:21
  10.3 1.6 slice-start.3
  10.3 20.2 %collective-permute-start.6 = (bf16[16,6,2,32,128]{4,3,2,1,0:T(8,128)(2,1)}, bf16[16,6,2,32,128]{4,3,2,1,0:T(8,128)(2,1)S(1)}, u32[]{:S(2)}, u32[]{:S(2)}) collective-permute-start(bf16[16,6,2,32,128]{4,3,2,1,0:T(8,128)(2,1)} %bitcast.35), channel_id=1, source_target_pairs={{0,1},{1,0},{2,3},{3,2},{4,5},{5,4},{6,7},{7,6},{8,9},{9,8},{10,11... | collective-permute-start | bytes 4718600 | tf_op jit(solution)/shard_map/ppermute | solution.py:21
  15.6 11.2 %slice-start.2 = ((bf16[96,2,32,274]{0,2,3,1:T(8,128)(2,1)}), bf16[96,2,32,18]{0,2,3,1:T(8,128)(2,1)S(1)}, s32[]{:S(2)}) async-start(bf16[96,2,32,274]{0,2,3,1:T(8,128)(2,1)} %param.4), calls=%async_computation.5 | async-start | bytes 589824 | tf_op jit(solution)/shard_map/slice | solution.py:295
  20.4 83.3 %collective-permute-start.10 = (bf16[16,6,2,32,128]{4,3,2,1,0:T(8,128)(2,1)}, bf16[16,6,2,32,128]{4,3,2,1,0:T(8,128)(2,1)}, u32[]{:S(2)}, u32[]{:S(2)}) collective-permute-start(bf16[16,6,2,32,128]{4,3,2,1,0:T(8,128)(2,1)} %shard_map.47.refs_4_.refs_0_), channel_id=1, source_target_pairs={{0,2},{1,3},{2,0},{3,1},{4,6},{5,7},{6,4},{7,5},{8,10},{9,11},{10,... | collective-permute-start | bytes 4718600 | tf_op jit(solution)/shard_map/ppermute | solution.py:21
  28.8 1.6 copy-start.7
  28.9 1.6 collective-permute-start.7
  31.2 1.2 copy-start.6
  38.2 107.7 %collective-permute-start.9 = (bf16[16,4,2,32,128]{4,3,2,1,0:T(8,128)(2,1)}, bf16[16,4,2,32,128]{4,3,2,1,0:T(8,128)(2,1)}, u32[]{:S(2)}, u32[]{:S(2)}) collective-permute-start(bf16[16,4,2,32,128]{4,3,2,1,0:T(8,128)(2,1)} %get-tuple-element.45.refs_2_.refs_0_), channel_id=1, source_target_pairs={{0,2},{1,3},{2,0},{3,1},{4,6},{5,7},{6,4},{7,5},{8,10},{9,11},{10,... | collective-permute-start | bytes 3145736 | tf_op jit(solution)/shard_map/ppermute | solution.py:21
  46.9 8.0 %slice-start.4 = ((s32[4,96,2]{1,2,0:T(2,128)}), s32[2,96,2]{1,2,0:T(2,128)S(1)}, s32[]{:S(2)}) async-start(s32[4,96,2]{1,2,0:T(2,128)} %param.6), calls=%async_computation.7 | async-start | bytes 4096 | tf_op jit(solution)/shard_map/slice | solution.py:306
  50.5 64.7 %collective-permute-start.3 = (bf16[4,6,2,32,128]{4,3,2,1,0:T(8,128)(2,1)}, bf16[4,6,2,32,128]{4,3,2,1,0:T(8,128)(2,1)S(1)}, u32[]{:S(2)}, u32[]{:S(2)}) collective-permute-start(bf16[4,6,2,32,128]{4,3,2,1,0:T(8,128)(2,1)} %get-tuple-element.40), channel_id=1, source_target_pairs={{0,4},{1,5},{2,6},{3,7},{4,0},{5,1},{6,2},{7,3},{8,12},{9,13},{10,... | collective-permute-start | bytes 1179656 | tf_op jit(solution)/shard_map/ppermute | solution.py:21
  52.1 64.7 %collective-permute-start.4 = (bf16[4,6,2,32,128]{4,3,2,1,0:T(8,128)(2,1)}, bf16[4,6,2,32,128]{4,3,2,1,0:T(8,128)(2,1)S(1)}, u32[]{:S(2)}, u32[]{:S(2)}) collective-permute-start(bf16[4,6,2,32,128]{4,3,2,1,0:T(8,128)(2,1)} %get-tuple-element.41), channel_id=1, source_target_pairs={{0,8},{1,9},{2,10},{3,11},{4,12},{5,13},{6,14},{7,15},{8,0},{9,1},... | collective-permute-start | bytes 1179656 | tf_op jit(solution)/shard_map/ppermute | solution.py:21
  55.3 15.0 %collective-permute-start = (s32[96]{0:T(128)S(1)}, s32[96]{0:T(128)S(1)}, u32[]{:S(2)}, u32[]{:S(2)}) collective-permute-start(s32[96]{0:T(128)S(1)} %get-tuple-element.77), channel_id=1, source_target_pairs={{0,4},{1,5},{2,6},{3,7},{4,0},{5,1},{6,2},{7,3},{8,12},{9,13},{10,... | collective-permute-start | bytes 1160 | tf_op jit(solution)/shard_map/ppermute | solution.py:21
  70.3 5.0 %collective-permute-start.1 = (s32[96]{0:T(128)S(1)}, s32[96]{0:T(128)S(1)}, u32[]{:S(2)}, u32[]{:S(2)}) collective-permute-start(s32[96]{0:T(128)S(1)} %get-tuple-element.76), channel_id=1, source_target_pairs={{0,8},{1,9},{2,10},{3,11},{4,12},{5,13},{6,14},{7,15},{8,0},{9,1},... | collective-permute-start | bytes 1160 | tf_op jit(solution)/shard_map/ppermute | solution.py:21
  75.3 44.4 %collective-permute-start.5 = (bf16[4,6,2,32,128]{4,3,2,1,0:T(8,128)(2,1)}, bf16[4,6,2,32,128]{4,3,2,1,0:T(8,128)(2,1)S(1)}, u32[]{:S(2)}, u32[]{:S(2)}) collective-permute-start(bf16[4,6,2,32,128]{4,3,2,1,0:T(8,128)(2,1)} %get-tuple-element.42), channel_id=1, source_target_pairs={{0,12},{1,13},{2,14},{3,15},{4,8},{5,9},{6,10},{7,11},{8,4},{9,5},... | collective-permute-start | bytes 1179656 | tf_op jit(solution)/shard_map/ppermute | solution.py:21
  103.7 11.3 %collective-permute-start.2 = (s32[96]{0:T(128)S(1)}, s32[96]{0:T(128)S(1)}, u32[]{:S(2)}, u32[]{:S(2)}) collective-permute-start(s32[96]{0:T(128)S(1)} %get-tuple-element.75), channel_id=1, source_target_pairs={{0,12},{1,13},{2,14},{3,15},{4,8},{5,9},{6,10},{7,11},{8,4},{9,5},... | collective-permute-start | bytes 1160 | tf_op jit(solution)/shard_map/ppermute | solution.py:21
  109.8 10.0 %copy-start.8 = (bf16[16,3,2,32,128]{4,3,2,1,0:T(8,128)(2,1)S(1)}, bf16[16,3,2,32,128]{4,3,2,1,0:T(8,128)(2,1)}, u32[]{:S(2)}) copy-start(bf16[16,3,2,32,128]{4,3,2,1,0:T(8,128)(2,1)} %get-tuple-element.59.refs_0_) | copy-start | bytes 2359300
  115.0 12.3 %collective-permute-start.11 = (bf16[4,6,2,32,128]{4,3,2,1,0:T(8,128)(2,1)}, bf16[4,6,2,32,128]{4,3,2,1,0:T(8,128)(2,1)S(1)}, u32[]{:S(2)}, u32[]{:S(2)}) collective-permute-start(bf16[4,6,2,32,128]{4,3,2,1,0:T(8,128)(2,1)} %get-tuple-element.47), channel_id=1, source_target_pairs={{0,4},{1,5},{2,6},{3,7},{4,0},{5,1},{6,2},{7,3},{8,12},{9,13},{10,... | collective-permute-start | bytes 1179656 | tf_op jit(solution)/shard_map/ppermute | solution.py:21
  115.2 19.9 %copy-start.2 = (bf16[4,6,2,32,128]{4,3,2,1,0:T(8,128)(2,1)}, bf16[4,6,2,32,128]{4,3,2,1,0:T(8,128)(2,1)S(1)}, u32[]{:S(2)}) copy-start(bf16[4,6,2,32,128]{4,3,2,1,0:T(8,128)(2,1)S(1)} %collective-permute-done.3.refs_1_) | copy-start | bytes 1179652
  115.2 17.3 %collective-permute-start.12 = (bf16[4,6,2,32,128]{4,3,2,1,0:T(8,128)(2,1)}, bf16[4,6,2,32,128]{4,3,2,1,0:T(8,128)(2,1)}, u32[]{:S(2)}, u32[]{:S(2)}) collective-permute-start(bf16[4,6,2,32,128]{4,3,2,1,0:T(8,128)(2,1)} %get-tuple-element.48), channel_id=1, source_target_pairs={{0,8},{1,9},{2,10},{3,11},{4,12},{5,13},{6,14},{7,15},{8,0},{9,1},... | collective-permute-start | bytes 1179656 | tf_op jit(solution)/shard_map/ppermute | solution.py:21
  116.7 18.4 %copy-start.3 = (bf16[4,6,2,32,128]{4,3,2,1,0:T(8,128)(2,1)}, bf16[4,6,2,32,128]{4,3,2,1,0:T(8,128)(2,1)S(1)}, u32[]{:S(2)}) copy-start(bf16[4,6,2,32,128]{4,3,2,1,0:T(8,128)(2,1)S(1)} %collective-permute-done.4.refs_2_) | copy-start | bytes 1179652
  116.7 18.4 %collective-permute-start.13 = (bf16[4,6,2,32,128]{4,3,2,1,0:T(8,128)(2,1)}, bf16[4,6,2,32,128]{4,3,2,1,0:T(8,128)(2,1)}, u32[]{:S(2)}, u32[]{:S(2)}) collective-permute-start(bf16[4,6,2,32,128]{4,3,2,1,0:T(8,128)(2,1)} %get-tuple-element.49), channel_id=1, source_target_pairs={{0,12},{1,13},{2,14},{3,15},{4,8},{5,9},{6,10},{7,11},{8,4},{9,5},... | collective-permute-start | bytes 1179656 | tf_op jit(solution)/shard_map/ppermute | solution.py:21
  119.8 15.4 %copy-start.4 = (bf16[4,6,2,32,128]{4,3,2,1,0:T(8,128)(2,1)}, bf16[4,6,2,32,128]{4,3,2,1,0:T(8,128)(2,1)S(1)}, u32[]{:S(2)}) copy-start(bf16[4,6,2,32,128]{4,3,2,1,0:T(8,128)(2,1)S(1)} %collective-permute-done.5.refs_3_) | copy-start | bytes 1179652
  119.8 70.7 %collective-permute-start.20 = (bf16[16,3,2,32,128]{4,3,2,1,0:T(8,128)(2,1)S(1)}, bf16[16,3,2,32,128]{4,3,2,1,0:T(8,128)(2,1)S(1)}, u32[]{:S(2)}, u32[]{:S(2)}) collective-permute-start(bf16[16,3,2,32,128]{4,3,2,1,0:T(8,128)(2,1)S(1)} %copy-done.8), channel_id=1, source_target_pairs={{0,2},{1,3},{2,0},{3,1},{4,6},{5,7},{6,4},{7,5},{8,10},{9,11},{10,... | collective-permute-start | bytes 2359304 | tf_op jit(solution)/shard_map/ppermute | solution.py:21
  127.3 7.8 %copy-start.10 = (bf16[4,6,2,32,128]{4,3,2,1,0:T(8,128)(2,1)}, bf16[4,6,2,32,128]{4,3,2,1,0:T(8,128)(2,1)S(1)}, u32[]{:S(2)}) copy-start(bf16[4,6,2,32,128]{4,3,2,1,0:T(8,128)(2,1)S(1)} %collective-permute-done.11.refs_5_) | copy-start | bytes 1179652
  151.0 9.5 %collective-permute-start.14 = (bf16[4,4,2,32,128]{4,3,2,1,0:T(8,128)(2,1)}, bf16[4,4,2,32,128]{4,3,2,1,0:T(8,128)(2,1)S(1)}, u32[]{:S(2)}, u32[]{:S(2)}) collective-permute-start(bf16[4,4,2,32,128]{4,3,2,1,0:T(8,128)(2,1)} %get-tuple-element.52), channel_id=1, source_target_pairs={{0,4},{1,5},{2,6},{3,7},{4,0},{5,1},{6,2},{7,3},{8,12},{9,13},{10,... | collective-permute-start | bytes 786440 | tf_op jit(solution)/shard_map/ppermute | solution.py:21
  152.6 16.0 %collective-permute-start.15 = (bf16[4,4,2,32,128]{4,3,2,1,0:T(8,128)(2,1)}, bf16[4,4,2,32,128]{4,3,2,1,0:T(8,128)(2,1)S(1)}, u32[]{:S(2)}, u32[]{:S(2)}) collective-permute-start(bf16[4,4,2,32,128]{4,3,2,1,0:T(8,128)(2,1)} %get-tuple-element.53), channel_id=1, source_target_pairs={{0,8},{1,9},{2,10},{3,11},{4,12},{5,13},{6,14},{7,15},{8,0},{9,1},... | collective-permute-start | bytes 786440 | tf_op jit(solution)/shard_map/ppermute | solution.py:21
  155.5 39.9 %collective-permute-start.24 = (bf16[4,6,2,32,128]{4,3,2,1,0:T(8,128)(2,1)}, bf16[4,6,2,32,128]{4,3,2,1,0:T(8,128)(2,1)S(1)}, u32[]{:S(2)}, u32[]{:S(2)}) collective-permute-start(bf16[4,6,2,32,128]{4,3,2,1,0:T(8,128)(2,1)} %get-tuple-element.64), channel_id=1, source_target_pairs={{0,4},{1,5},{2,6},{3,7},{4,0},{5,1},{6,2},{7,3},{8,12},{9,13},{10,... | collective-permute-start | bytes 1179656 | tf_op jit(solution)/shard_map/ppermute | solution.py:21
  155.6 39.7 %collective-permute-start.25 = (bf16[4,6,2,32,128]{4,3,2,1,0:T(8,128)(2,1)}, bf16[4,6,2,32,128]{4,3,2,1,0:T(8,128)(2,1)S(1)}, u32[]{:S(2)}, u32[]{:S(2)}) collective-permute-start(bf16[4,6,2,32,128]{4,3,2,1,0:T(8,128)(2,1)} %get-tuple-element.65), channel_id=1, source_target_pairs={{0,8},{1,9},{2,10},{3,11},{4,12},{5,13},{6,14},{7,15},{8,0},{9,1},... | collective-permute-start | bytes 1179656 | tf_op jit(solution)/shard_map/ppermute | solution.py:21
  160.5 23.0 %copy-start.17 = (bf16[4,4,2,32,128]{4,3,2,1,0:T(8,128)(2,1)}, bf16[4,4,2,32,128]{4,3,2,1,0:T(8,128)(2,1)S(1)}, u32[]{:S(2)}) copy-start(bf16[4,4,2,32,128]{4,3,2,1,0:T(8,128)(2,1)S(1)} %collective-permute-done.14.refs_5_) | copy-start | bytes 786436
  160.5 34.9 %collective-permute-start.26 = (bf16[4,6,2,32,128]{4,3,2,1,0:T(8,128)(2,1)}, bf16[4,6,2,32,128]{4,3,2,1,0:T(8,128)(2,1)S(1)}, u32[]{:S(2)}, u32[]{:S(2)}) collective-permute-start(bf16[4,6,2,32,128]{4,3,2,1,0:T(8,128)(2,1)} %get-tuple-element.66), channel_id=1, source_target_pairs={{0,12},{1,13},{2,14},{3,15},{4,8},{5,9},{6,10},{7,11},{8,4},{9,5},... | collective-permute-start | bytes 1179656 | tf_op jit(solution)/shard_map/ppermute | solution.py:21
  168.6 14.9 %copy-start.18 = (bf16[4,4,2,32,128]{4,3,2,1,0:T(8,128)(2,1)}, bf16[4,4,2,32,128]{4,3,2,1,0:T(8,128)(2,1)S(1)}, u32[]{:S(2)}) copy-start(bf16[4,4,2,32,128]{4,3,2,1,0:T(8,128)(2,1)S(1)} %collective-permute-done.15.refs_6_) | copy-start | bytes 786436
  168.6 14.9 %collective-permute-start.16 = (bf16[4,4,2,32,128]{4,3,2,1,0:T(8,128)(2,1)}, bf16[4,4,2,32,128]{4,3,2,1,0:T(8,128)(2,1)S(1)}, u32[]{:S(2)}, u32[]{:S(2)}) collective-permute-start(bf16[4,4,2,32,128]{4,3,2,1,0:T(8,128)(2,1)} %get-tuple-element.54), channel_id=1, source_target_pairs={{0,12},{1,13},{2,14},{3,15},{4,8},{5,9},{6,10},{7,11},{8,4},{9,5},... | collective-permute-start | bytes 786440 | tf_op jit(solution)/shard_map/ppermute | solution.py:21
  183.5 0.7 copy-start.20
  190.4 0.9 copy-start.9
  195.4 0.8 copy-start.11
  195.4 0.9 copy-start.12
  195.4 1.0 copy-start.13
  199.0 25.3 %copy-start.31 = (bf16[4,3,2,32,128]{4,3,2,1,0:T(8,128)(2,1)S(1)}, bf16[4,3,2,32,128]{4,3,2,1,0:T(8,128)(2,1)}, u32[]{:S(2)}) copy-start(bf16[4,3,2,32,128]{4,3,2,1,0:T(8,128)(2,1)} %get-tuple-element.61) | copy-start | bytes 589828
  199.0 27.4 %copy-start.29 = (bf16[4,4,2,32,128]{4,3,2,1,0:T(8,128)(2,1)S(1)}, bf16[4,4,2,32,128]{4,3,2,1,0:T(8,128)(2,1)}, u32[]{:S(2)}) copy-start(bf16[4,4,2,32,128]{4,3,2,1,0:T(8,128)(2,1)} %get-tuple-element.57) | copy-start | bytes 786436
  199.0 28.9 %copy-start.28 = (bf16[4,4,2,32,128]{4,3,2,1,0:T(8,128)(2,1)S(1)}, bf16[4,4,2,32,128]{4,3,2,1,0:T(8,128)(2,1)}, u32[]{:S(2)}) copy-start(bf16[4,4,2,32,128]{4,3,2,1,0:T(8,128)(2,1)} %get-tuple-element.58) | copy-start | bytes 786436
  199.0 51.8 %all-to-all-start.1 = ((bf16[16,6,2,32,128]{4,3,2,1,0:T(8,128)(2,1)}), bf16[16,6,2,32,128]{4,3,2,1,0:T(8,128)(2,1)S(1)}, u32[]{:S(2)}, u32[]{:S(2)}) async-start(bf16[16,6,2,32,128]{4,3,2,1,0:T(8,128)(2,1)} %shard_map.54.refs_8_), calls=%async_computation.1 | async-start | bytes 3145728 | tf_op jit(solution)/shard_map/all_to_all | solution.py:325
  224.3 6.9 %collective-permute-start.21 = (bf16[4,3,2,32,128]{4,3,2,1,0:T(8,128)(2,1)S(1)}, bf16[4,3,2,32,128]{4,3,2,1,0:T(8,128)(2,1)S(1)}, u32[]{:S(2)}, u32[]{:S(2)}) collective-permute-start(bf16[4,3,2,32,128]{4,3,2,1,0:T(8,128)(2,1)S(1)} %copy-done.31), channel_id=1, source_target_pairs={{0,4},{1,5},{2,6},{3,7},{4,0},{5,1},{6,2},{7,3},{8,12},{9,13},{10,... | collective-permute-start | bytes 589832 | tf_op jit(solution)/shard_map/ppermute | solution.py:21
  224.4 23.2 %collective-permute-start.17 = (bf16[4,4,2,32,128]{4,3,2,1,0:T(8,128)(2,1)}, bf16[4,4,2,32,128]{4,3,2,1,0:T(8,128)(2,1)S(1)}, u32[]{:S(2)}, u32[]{:S(2)}) collective-permute-start(bf16[4,4,2,32,128]{4,3,2,1,0:T(8,128)(2,1)} %get-tuple-element.56), channel_id=1, source_target_pairs={{0,4},{1,5},{2,6},{3,7},{4,0},{5,1},{6,2},{7,3},{8,12},{9,13},{10,... | collective-permute-start | bytes 786440 | tf_op jit(solution)/shard_map/ppermute | solution.py:21
  226.4 21.2 %collective-permute-start.18 = (bf16[4,4,2,32,128]{4,3,2,1,0:T(8,128)(2,1)S(1)}, bf16[4,4,2,32,128]{4,3,2,1,0:T(8,128)(2,1)S(1)}, u32[]{:S(2)}, u32[]{:S(2)}) collective-permute-start(bf16[4,4,2,32,128]{4,3,2,1,0:T(8,128)(2,1)S(1)} %copy-done.29), channel_id=1, source_target_pairs={{0,8},{1,9},{2,10},{3,11},{4,12},{5,13},{6,14},{7,15},{8,0},{9,1},... | collective-permute-start | bytes 786440 | tf_op jit(solution)/shard_map/ppermute | solution.py:21
  227.9 19.8 %collective-permute-start.19 = (bf16[4,4,2,32,128]{4,3,2,1,0:T(8,128)(2,1)S(1)}, bf16[4,4,2,32,128]{4,3,2,1,0:T(8,128)(2,1)S(1)}, u32[]{:S(2)}, u32[]{:S(2)}) collective-permute-start(bf16[4,4,2,32,128]{4,3,2,1,0:T(8,128)(2,1)S(1)} %copy-done.28), channel_id=1, source_target_pairs={{0,12},{1,13},{2,14},{3,15},{4,8},{5,9},{6,10},{7,11},{8,4},{9,5},... | collective-permute-start | bytes 786440 | tf_op jit(solution)/shard_map/ppermute | solution.py:21
  229.2 10.0 %collective-permute-start.22 = (bf16[4,3,2,32,128]{4,3,2,1,0:T(8,128)(2,1)}, bf16[4,3,2,32,128]{4,3,2,1,0:T(8,128)(2,1)S(1)}, u32[]{:S(2)}, u32[]{:S(2)}) collective-permute-start(bf16[4,3,2,32,128]{4,3,2,1,0:T(8,128)(2,1)} %get-tuple-element.62), channel_id=1, source_target_pairs={{0,8},{1,9},{2,10},{3,11},{4,12},{5,13},{6,14},{7,15},{8,0},{9,1},... | collective-permute-start | bytes 589832 | tf_op jit(solution)/shard_map/ppermute | solution.py:21
  231.2 11.2 %copy-start.24 = (bf16[4,3,2,32,128]{4,3,2,1,0:T(8,128)(2,1)}, bf16[4,3,2,32,128]{4,3,2,1,0:T(8,128)(2,1)S(1)}, u32[]{:S(2)}) copy-start(bf16[4,3,2,32,128]{4,3,2,1,0:T(8,128)(2,1)S(1)} %collective-permute-done.21.refs_5_) | copy-start | bytes 589828
  231.2 11.2 %collective-permute-start.23 = (bf16[4,3,2,32,128]{4,3,2,1,0:T(8,128)(2,1)}, bf16[4,3,2,32,128]{4,3,2,1,0:T(8,128)(2,1)S(1)}, u32[]{:S(2)}, u32[]{:S(2)}) collective-permute-start(bf16[4,3,2,32,128]{4,3,2,1,0:T(8,128)(2,1)} %get-tuple-element.63), channel_id=1, source_target_pairs={{0,12},{1,13},{2,14},{3,15},{4,8},{5,9},{6,10},{7,11},{8,4},{9,5},... | collective-permute-start | bytes 589832 | tf_op jit(solution)/shard_map/ppermute | solution.py:21
  239.2 3.2 %copy-start.25 = (bf16[4,3,2,32,128]{4,3,2,1,0:T(8,128)(2,1)}, bf16[4,3,2,32,128]{4,3,2,1,0:T(8,128)(2,1)S(1)}, u32[]{:S(2)}) copy-start(bf16[4,3,2,32,128]{4,3,2,1,0:T(8,128)(2,1)S(1)} %collective-permute-done.22.refs_6_) | copy-start | bytes 589828
  247.6 0.8 copy-start.15
  247.7 0.9 copy-start.16
  250.8 10.5 %copy-start.30 = (bf16[4,3,2,32,128]{4,3,2,1,0:T(8,128)(2,1)S(1)}, bf16[4,3,2,32,128]{4,3,2,1,0:T(8,128)(2,1)}, u32[]{:S(2)}) copy-start(bf16[4,3,2,32,128]{4,3,2,1,0:T(8,128)(2,1)} %get-tuple-element.70) | copy-start | bytes 589828
  250.8 12.4 %copy-start.1 = (bf16[16,6,2,32,128]{4,3,2,1,0:T(8,128)(2,1)}, bf16[16,6,2,32,128]{4,3,2,1,0:T(8,128)(2,1)S(1)}, u32[]{:S(2)}) copy-start(bf16[16,6,2,32,128]{4,3,2,1,0:T(8,128)(2,1)S(1)} %all-to-all-done.1.refs_0_) | copy-start | bytes 4718596
  250.8 26.6 %all-to-all-start = ((bf16[16,4,2,32,128]{4,3,2,1,0:T(8,128)(2,1)}), bf16[16,4,2,32,128]{4,3,2,1,0:T(8,128)(2,1)S(1)}, u32[]{:S(2)}, u32[]{:S(2)}) async-start(bf16[16,4,2,32,128]{4,3,2,1,0:T(8,128)(2,1)} %shard_map.56.refs_4_), calls=%async_computation | async-start | bytes 2097152 | tf_op jit(solution)/shard_map/all_to_all | solution.py:325
  258.5 15.4 %collective-permute-start.27 = (bf16[4,3,2,32,128]{4,3,2,1,0:T(8,128)(2,1)}, bf16[4,3,2,32,128]{4,3,2,1,0:T(8,128)(2,1)S(1)}, u32[]{:S(2)}, u32[]{:S(2)}) collective-permute-start(bf16[4,3,2,32,128]{4,3,2,1,0:T(8,128)(2,1)} %get-tuple-element.68), channel_id=1, source_target_pairs={{0,4},{1,5},{2,6},{3,7},{4,0},{5,1},{6,2},{7,3},{8,12},{9,13},{10,... | collective-permute-start | bytes 589832 | tf_op jit(solution)/shard_map/ppermute | solution.py:21
  258.6 15.3 %collective-permute-start.28 = (bf16[4,3,2,32,128]{4,3,2,1,0:T(8,128)(2,1)}, bf16[4,3,2,32,128]{4,3,2,1,0:T(8,128)(2,1)S(1)}, u32[]{:S(2)}, u32[]{:S(2)}) collective-permute-start(bf16[4,3,2,32,128]{4,3,2,1,0:T(8,128)(2,1)} %get-tuple-element.69), channel_id=1, source_target_pairs={{0,8},{1,9},{2,10},{3,11},{4,12},{5,13},{6,14},{7,15},{8,0},{9,1},... | collective-permute-start | bytes 589832 | tf_op jit(solution)/shard_map/ppermute | solution.py:21
  261.3 12.6 %collective-permute-start.29 = (bf16[4,3,2,32,128]{4,3,2,1,0:T(8,128)(2,1)S(1)}, bf16[4,3,2,32,128]{4,3,2,1,0:T(8,128)(2,1)S(1)}, u32[]{:S(2)}, u32[]{:S(2)}) collective-permute-start(bf16[4,3,2,32,128]{4,3,2,1,0:T(8,128)(2,1)S(1)} %copy-done.30), channel_id=1, source_target_pairs={{0,12},{1,13},{2,14},{3,15},{4,8},{5,9},{6,10},{7,11},{8,4},{9,5},... | collective-permute-start | bytes 589832 | tf_op jit(solution)/shard_map/ppermute | solution.py:21
  273.8 0.7 copy-start.22
  277.4 7.5 %copy-start = (bf16[16,4,2,32,128]{4,3,2,1,0:T(8,128)(2,1)}, bf16[16,4,2,32,128]{4,3,2,1,0:T(8,128)(2,1)S(1)}, u32[]{:S(2)}) copy-start(bf16[16,4,2,32,128]{4,3,2,1,0:T(8,128)(2,1)S(1)} %all-to-all-done.refs_0_) | copy-start | bytes 3145732
  277.4 21.4 %all-to-all-start.2 = ((bf16[16,3,2,32,128]{4,3,2,1,0:T(8,128)(2,1)}), bf16[16,3,2,32,128]{4,3,2,1,0:T(8,128)(2,1)S(1)}, u32[]{:S(2)}, u32[]{:S(2)}) async-start(bf16[16,3,2,32,128]{4,3,2,1,0:T(8,128)(2,1)} %shard_map.59.refs_1_), calls=%async_computation.2 | async-start | bytes 1572864 | tf_op jit(solution)/shard_map/all_to_all | solution.py:325
  298.9 0.9 copy-start.5
  (6 other events, 4.1 us)

commit v4 on v3

--- a/solution.py
+++ b/solution.py
@@ -11,8 +11,9 @@
 TAIL = -1
 FIRST = ((0, 1, 2, 3, 4, 5),)
 SECOND = ((-1, 0, 1, 2), (3, 4, 5))
-ORDER = ((0, 1), (0, 2), (1, 1), (1, 2), (2, 1), (0, 3), (2, 2), (1, 3), (2, 3))
+ORDER = ((0, 1), (0, 2), (1, 1), (2, 1), (0, 3), (1, 2), (2, 2), (1, 3), (2, 3))
 WAITS = {}
+BEHIND = {(0, 3): (1,), (1, 2): (2,)}
 EARLY = (2, 3)
 
 
@@ -316,6 +317,7 @@
             whole = store(early.transpose(1, 3, 2, 0), 0, cols)
             after.append(whole)
         after += [done[w][0] for w in WAITS.get((k, step), ())]
+        after += [piece for w in BEHIND.get((k, step), ()) for piece in chunks[w][1:]]
         if step == 1:
             outs = level(1, [where[k]], [chunks[k]], [far[k]], ys)
         elif step == 2:

time: 314 us -> 309 us (0.984)
  starting transfers between devices: 94 us -> 85.1 us
  waiting for transfers between devices: 95.2 us -> 103 us
    all_to_all x3, starting transfers between devices: 40.5 us -> 34.5 us  [per_device(): lax.all_to_all(outs[0], 'order', split_axis=0, concat_axis=0, tiled=True)]
    all_to_all x3, waiting for transfers between devices: 5.12 us -> 9.36 us  [per_device(): lax.all_to_all(outs[0], 'order', split_axis=0, concat_axis=0, tiled=True)]
    ppermute x30, waiting for transfers between devices: 90.1 us -> 93.8 us  [from_partner(): return lax.ppermute(value, 'lat', [(i, i ^ mask) for i in range(size)])]
    unnamed x65 -> x69, local copies, waits for them, and re-layouts: 9.16 us -> 8.01 us
  transfers between devices with their start and end apart: 33 -> 33, of which waited for: 14 -> 14; matrix products, arithmetic and copies ran while one was open for 10% -> 10% of each run, Pallas kernels for 19% -> 20%
where the time goes in v4:
time: 309 us
  waiting for transfers between devices  103 us (33%)
  starting transfers between devices  85.1 us (28%)
  Pallas kernels  68.7 us (22%)
  local copies, waits for them, and re-layouts  49.8 us (16%)
    ppermute x30, waiting for transfers between devices, from_partner(): return lax.ppermute(value, 'lat', [(i, i ^ mask) for i in range(size)])  93.8 us
    ppermute x30, starting transfers between devices, from_partner(): return lax.ppermute(value, 'lat', [(i, i ^ mask) for i in range(size)])  50.7 us
    all_to_all x3, starting transfers between devices, per_device(): lax.all_to_all(outs[0], 'order', split_axis=0, concat_axis=0, tiled=True)  34.5 us
    pallas_call x5, Pallas kernels, run_level(): pl.pallas_call(functools.partial(level_kernel, spec, lev, tail_w), in_spe...  25.1 us
    pallas_call x3, Pallas kernels, run_last(): pl.pallas_call(functools.partial(last_kernel, {'ys': ys, 'slots': slots},...  16.4 us
    slice x7, local copies, waits for them, and re-layouts, level_weights(): return six(c[l])  14.8 us
    pallas_call x3, local copies, waits for them, and re-layouts, place(): pl.pallas_call(functools.partial(place_kernel, tail_w, slots), in_specs=[...  13.6 us
    all_to_all x3, waiting for transfers between devices, per_device(): lax.all_to_all(outs[0], 'order', split_axis=0, concat_axis=0, tiled=True)  9.36 us
  transfers between devices with their start and end apart: 33, of which 14 were waited for; matrix products, arithmetic and copies ran while one was open for 10% of the time, Pallas kernels for 20%

profile of v4, /device:TPU:32, one launch (start us, length us, event | category | flops | bytes accessed | tf_op | source)
XLA Modules:
  0.0 308.6 jit_solution(10219623405567271673)
XLA Ops:
  0.0 1.6 slice-done
  1.6 3.5 %copy.33 = bf16[96,2,32,128]{3,2,1,0:T(8,128)(2,1)} copy(bf16[96,2,32,128]{0,2,3,1:T(8,128)(2,1)S(1)} %slice-done) | data formatting | bytes 3145728 | tf_op jit(solution)/shard_map/slice | solution.py:265
  5.1 1.6 slice-done.1
  6.7 3.6 %copy.39 = bf16[96,2,32,128]{3,2,1,0:T(8,128)(2,1)} copy(bf16[96,2,32,128]{0,2,3,1:T(8,128)(2,1)S(1)} %slice-done.1) | data formatting | bytes 3145728 | tf_op jit(solution)/shard_map/slice | solution.py:295
  11.9 3.0 copy.38
  15.5 4.9 %shard_map.47.refs_4_.refs_0_ = bf16[16,6,2,32,128]{4,3,2,1,0:T(8,128)(2,1)} custom-call(s32[2]{0:T(128)} %pad_add_fusion.1.at_ref.me_ref, s32[768]{0:T(1024)} %reshape.24.pat_ref, bf16[16,6,2,32,64]{4,3,2,1,0:T(8,128)(2,1)} %bitcast.31, bf16[16,6,2,32,128]{4,3,2,1,0:T(8,128)(2,1)} %bitcast.38, bf16[16,6,2,32,128]{4,3,2,1,0:T(8,128)(2,1)} %collective-permute-done.8.refs_1_), custom_call_target="tpu_custom_call" | custom-call | flops 1 | bytes 1 | tf_op jit(solution)/shard_map/pallas_call | solution.py:89
  20.4 6.3 %collective-permute-start.10 = (bf16[16,6,2,32,128]{4,3,2,1,0:T(8,128)(2,1)}, bf16[16,6,2,32,128]{4,3,2,1,0:T(8,128)(2,1)}, u32[]{:S(2)}, u32[]{:S(2)}) collective-permute-start(bf16[16,6,2,32,128]{4,3,2,1,0:T(8,128)(2,1)} %shard_map.47.refs_4_.refs_0_), channel_id=1, source_target_pairs={{0,2},{1,3},{2,0},{3,1},{4,6},{5,7},{6,4},{7,5},{8,10},{9,11},{10,... | collective-permute-start | bytes 4718600 | tf_op jit(solution)/shard_map/ppermute | solution.py:22
  27.4 1.4 copy.42
  29.3 1.7 collective-permute-start
  31.0 2.9 collective-permute-start.1
  34.6 1.1 copy-done.6
  35.7 5.8 %shard_map.48 = (bf16[16,4,2,32,128]{4,3,2,1,0:T(8,128)(2,1)}, bf16[16,3,2,32,128]{4,3,2,1,0:T(8,128)(2,1)}) custom-call(s32[2]{0:T(128)} %pad_add_fusion.1.at_ref.me_ref, s32[768]{0:T(1024)} %reshape.24.pat_ref, bf16[16,6,2,32,64]{4,3,2,1,0:T(8,128)(2,1)} %bitcast.32, bf16[16,6,2,32,128]{4,3,2,1,0:T(8,128)(2,1)} %bitcast.36, ...), custom_call_target="tpu_custom_call" | custom-call | flops 1 | bytes 1 | tf_op jit(solution)/shard_map/pallas_call | solution.py:89
  41.6 2.5 fusion.4
  44.1 3.0 copy.34
  47.2 3.1 %copy.35 = bf16[1,96,2,32,64]{4,3,2,1,0:T(8,128)(2,1)} copy(bf16[1,96,2,32,64]{1,4,3,2,0:T(8,128)(2,1)S(1)} %get-tuple-element.72) | data formatting | bytes 1572864 | tf_op jit(solution)/shard_map/slice | solution.py:263
  50.3 3.6 %shard_map.46 = (bf16[4,6,2,32,128]{4,3,2,1,0:T(8,128)(2,1)}, bf16[4,6,2,32,128]{4,3,2,1,0:T(8,128)(2,1)}, bf16[4,6,2,32,128]{4,3,2,1,0:T(8,128)(2,1)}, bf16[4,6,2,32,128]{4,3,2,1,0:T(8,128)(2,1)}) custom-call(s32[2]{0:T(128)} %pad_add_fusion.1.at_ref.me_ref, bf16[16,6,2,32,64]{4,3,2,1,0:T(8,128)(2,1)} %bitcast.39, bf16[16,6,2,32,64]{4,3,2,1,0:T(8,128)(2,1)} %bitcast.40), custom_call_target="tpu_custom_call" | custom-call | flops 1 | bytes 1 | tf_op jit(solution)/shard_map/pallas_call | solution.py:110
  54.1 3.9 %collective-permute-start.4 = (bf16[4,6,2,32,128]{4,3,2,1,0:T(8,128)(2,1)}, bf16[4,6,2,32,128]{4,3,2,1,0:T(8,128)(2,1)S(1)}, u32[]{:S(2)}, u32[]{:S(2)}) collective-permute-start(bf16[4,6,2,32,128]{4,3,2,1,0:T(8,128)(2,1)} %get-tuple-element.41), channel_id=1, source_target_pairs={{0,8},{1,9},{2,10},{3,11},{4,12},{5,13},{6,14},{7,15},{8,0},{9,1},... | collective-permute-start | bytes 1179656 | tf_op jit(solution)/shard_map/ppermute | solution.py:22
  58.6 45.1 %collective-permute-done.10.refs_1_ = bf16[16,6,2,32,128]{4,3,2,1,0:T(8,128)(2,1)} collective-permute-done((bf16[16,6,2,32,128]{4,3,2,1,0:T(8,128)(2,1)}, bf16[16,6,2,32,128]{4,3,2,1,0:T(8,128)(2,1)}, u32[]{:S(2)}, u32[]{:S(2)}) %collective-permute-start.10) | collective-permute-done | bytes 1572896 | tf_op jit(solution)/shard_map/ppermute | solution.py:22
  103.7 5.9 %collective-permute-start.20 = (bf16[16,3,2,32,128]{4,3,2,1,0:T(8,128)(2,1)S(1)}, bf16[16,3,2,32,128]{4,3,2,1,0:T(8,128)(2,1)}, u32[]{:S(2)}, u32[]{:S(2)}) collective-permute-start(bf16[16,3,2,32,128]{4,3,2,1,0:T(8,128)(2,1)S(1)} %copy-done.14), channel_id=1, source_target_pairs={{0,2},{1,3},{2,0},{3,1},{4,6},{5,7},{6,4},{7,5},{8,10},{9,11},{10,... | collective-permute-start | bytes 2359304 | tf_op jit(solution)/shard_map/ppermute | solution.py:22
  109.6 3.0 copy.37
  112.6 5.2 %shard_map.49 = (bf16[4,6,2,32,128]{4,3,2,1,0:T(8,128)(2,1)}, bf16[4,6,2,32,128]{4,3,2,1,0:T(8,128)(2,1)}, bf16[4,6,2,32,128]{4,3,2,1,0:T(8,128)(2,1)}, bf16[4,6,2,32,128]{4,3,2,1,0:T(8,128)(2,1)}) custom-call(s32[2]{0:T(128)} %pad_add_fusion.1.at_ref.me_ref, s32[768]{0:T(1024)} %reshape.24.pat_ref, bf16[16,6,2,32,64]{4,3,2,1,0:T(8,128)(2,1)} %bitcast.28, ...), custom_call_target="tpu_custom_call" | custom-call | flops 1 | bytes 1 | tf_op jit(solution)/shard_map/pallas_call | solution.py:89
  117.8 1.7 collective-permute-start.11
  119.5 2.9 collective-permute-start.12
  123.3 6.9 %collective-permute-done.11.refs_5_ = bf16[4,6,2,32,128]{4,3,2,1,0:T(8,128)(2,1)S(1)} collective-permute-done((bf16[4,6,2,32,128]{4,3,2,1,0:T(8,128)(2,1)}, bf16[4,6,2,32,128]{4,3,2,1,0:T(8,128)(2,1)S(1)}, u32[]{:S(2)}, u32[]{:S(2)}) %collective-permute-start.11) | collective-permute-done | bytes 393248 | tf_op jit(solution)/shard_map/ppermute | solution.py:22
  130.2 7.2 %collective-permute-done.12.refs_6_ = bf16[4,6,2,32,128]{4,3,2,1,0:T(8,128)(2,1)S(1)} collective-permute-done((bf16[4,6,2,32,128]{4,3,2,1,0:T(8,128)(2,1)}, bf16[4,6,2,32,128]{4,3,2,1,0:T(8,128)(2,1)S(1)}, u32[]{:S(2)}, u32[]{:S(2)}) %collective-permute-start.12) | collective-permute-done | bytes 393248 | tf_op jit(solution)/shard_map/ppermute | solution.py:22
  137.4 2.6 collective-permute-done.13.refs_7_
  140.8 5.7 %shard_map.50 = (bf16[4,6,2,32,128]{4,3,2,1,0:T(8,128)(2,1)}, bf16[4,6,2,32,128]{4,3,2,1,0:T(8,128)(2,1)}, bf16[4,6,2,32,128]{4,3,2,1,0:T(8,128)(2,1)}, bf16[4,6,2,32,128]{4,3,2,1,0:T(8,128)(2,1)}) custom-call(s32[384]{0:T(512)} %pad_add_fusion.pat_ref, bf16[4,6,2,32,128]{4,3,2,1,0:T(8,128)(2,1)} %get-tuple-element.39.refs_3_.refs_0_, ...), custom_call_target="tpu_custom_call" | custom-call | flops 1 | bytes 1 | tf_op jit(solution)/shard_map/pallas_call | solution.py:153
  146.5 5.2 %shard_map.51 = (bf16[4,4,2,32,128]{4,3,2,1,0:T(8,128)(2,1)}, bf16[4,4,2,32,128]{4,3,2,1,0:T(8,128)(2,1)}, bf16[4,4,2,32,128]{4,3,2,1,0:T(8,128)(2,1)}, bf16[4,4,2,32,128]{4,3,2,1,0:T(8,128)(2,1)}) custom-call(s32[2]{0:T(128)} %pad_add_fusion.1.at_ref.me_ref, s32[768]{0:T(1024)} %reshape.24.pat_ref, bf16[16,6,2,32,64]{4,3,2,1,0:T(8,128)(2,1)} %bitcast.29, ...), custom_call_target="tpu_custom_call" | custom-call | flops 1 | bytes 1 | tf_op jit(solution)/shard_map/pallas_call | solution.py:89
  152.7 1.0 collective-permute-start.17
  153.7 2.6 collective-permute-start.18
  156.3 1.1 collective-permute-start.19
  157.4 15.4 %collective-permute-done.20.refs_1_ = bf16[16,3,2,32,128]{4,3,2,1,0:T(8,128)(2,1)} collective-permute-done((bf16[16,3,2,32,128]{4,3,2,1,0:T(8,128)(2,1)S(1)}, bf16[16,3,2,32,128]{4,3,2,1,0:T(8,128)(2,1)}, u32[]{:S(2)}, u32[]{:S(2)}) %collective-permute-start.20) | collective-permute-done | bytes 786464 | tf_op jit(solution)/shard_map/ppermute | solution.py:22
  172.8 3.2 %collective-permute-start.15 = (bf16[4,4,2,32,128]{4,3,2,1,0:T(8,128)(2,1)}, bf16[4,4,2,32,128]{4,3,2,1,0:T(8,128)(2,1)S(1)}, u32[]{:S(2)}, u32[]{:S(2)}) collective-permute-start(bf16[4,4,2,32,128]{4,3,2,1,0:T(8,128)(2,1)} %get-tuple-element.53), channel_id=1, source_target_pairs={{0,8},{1,9},{2,10},{3,11},{4,12},{5,13},{6,14},{7,15},{8,0},{9,1},... | collective-permute-start | bytes 786440 | tf_op jit(solution)/shard_map/ppermute | solution.py:22
  176.0 1.1 collective-permute-start.16
  177.0 4.0 %shard_map.52 = (bf16[4,3,2,32,128]{4,3,2,1,0:T(8,128)(2,1)}, bf16[4,3,2,32,128]{4,3,2,1,0:T(8,128)(2,1)}, bf16[4,3,2,32,128]{4,3,2,1,0:T(8,128)(2,1)}, bf16[4,3,2,32,128]{4,3,2,1,0:T(8,128)(2,1)}) custom-call(s32[2]{0:T(128)} %pad_add_fusion.1.at_ref.me_ref, s32[768]{0:T(1024)} %reshape.24.pat_ref, bf16[16,6,2,32,64]{4,3,2,1,0:T(8,128)(2,1)} %bitcast.30, ...), custom_call_target="tpu_custom_call" | custom-call | flops 1 | bytes 1 | tf_op jit(solution)/shard_map/pallas_call | solution.py:89
  181.8 5.5 %collective-permute-done.16.refs_7_ = bf16[4,4,2,32,128]{4,3,2,1,0:T(8,128)(2,1)S(1)} collective-permute-done((bf16[4,4,2,32,128]{4,3,2,1,0:T(8,128)(2,1)}, bf16[4,4,2,32,128]{4,3,2,1,0:T(8,128)(2,1)S(1)}, u32[]{:S(2)}, u32[]{:S(2)}) %collective-permute-start.16) | collective-permute-done | bytes 262176 | tf_op jit(solution)/shard_map/ppermute | solution.py:22
  188.5 2.6 shard_map.53.refs_8_
  191.1 20.8 %all-to-all-start.1 = ((bf16[16,6,2,32,128]{4,3,2,1,0:T(8,128)(2,1)}), bf16[16,6,2,32,128]{4,3,2,1,0:T(8,128)(2,1)S(1)}, u32[]{:S(2)}, u32[]{:S(2)}) async-start(bf16[16,6,2,32,128]{4,3,2,1,0:T(8,128)(2,1)} %shard_map.53.refs_8_), calls=%async_computation.1 | async-start | bytes 3145728 | tf_op jit(solution)/shard_map/all_to_all | solution.py:327
  212.0 3.4 %collective-permute-start.22 = (bf16[4,3,2,32,128]{4,3,2,1,0:T(8,128)(2,1)S(1)}, bf16[4,3,2,32,128]{4,3,2,1,0:T(8,128)(2,1)S(1)}, u32[]{:S(2)}, u32[]{:S(2)}) collective-permute-start(bf16[4,3,2,32,128]{4,3,2,1,0:T(8,128)(2,1)S(1)} %copy-done.32), channel_id=1, source_target_pairs={{0,8},{1,9},{2,10},{3,11},{4,12},{5,13},{6,14},{7,15},{8,0},{9,1},... | collective-permute-start | bytes 589832 | tf_op jit(solution)/shard_map/ppermute | solution.py:22
  215.4 1.2 collective-permute-start.23
  217.6 3.6 %collective-permute-done.22.refs_10_.refs_6_ = bf16[4,3,2,32,128]{4,3,2,1,0:T(8,128)(2,1)S(1)} collective-permute-done((bf16[4,3,2,32,128]{4,3,2,1,0:T(8,128)(2,1)S(1)}, bf16[4,3,2,32,128]{4,3,2,1,0:T(8,128)(2,1)S(1)}, u32[]{:S(2)}, u32[]{:S(2)}) %collective-permute-start.22) | collective-permute-done | bytes 196640 | tf_op jit(solution)/shard_map/ppermute | solution.py:22
  221.3 2.0 collective-permute-done.23.refs_11_.refs_7_
  224.0 6.2 %shard_map.54 = (bf16[4,4,2,32,128]{4,3,2,1,0:T(8,128)(2,1)}, bf16[4,4,2,32,128]{4,3,2,1,0:T(8,128)(2,1)}, bf16[4,4,2,32,128]{4,3,2,1,0:T(8,128)(2,1)}, bf16[4,4,2,32,128]{4,3,2,1,0:T(8,128)(2,1)}) custom-call(s32[384]{0:T(512)} %pad_add_fusion.pat_ref, bf16[4,6,2,32,128]{4,3,2,1,0:T(8,128)(2,1)} %get-tuple-element.39.refs_3_.refs_0_, ...), custom_call_target="tpu_custom_call" | custom-call | flops 1 | bytes 1 | tf_op jit(solution)/shard_map/pallas_call | solution.py:153
  230.1 2.7 collective-permute-start.25
  232.8 2.0 collective-permute-start.26
  234.8 4.5 %shard_map.55 = (bf16[4,3,2,32,128]{4,3,2,1,0:T(8,128)(2,1)}, bf16[4,3,2,32,128]{4,3,2,1,0:T(8,128)(2,1)}, bf16[4,3,2,32,128]{4,3,2,1,0:T(8,128)(2,1)}, bf16[4,3,2,32,128]{4,3,2,1,0:T(8,128)(2,1)}) custom-call(s32[384]{0:T(512)} %pad_add_fusion.pat_ref, bf16[4,6,2,32,128]{4,3,2,1,0:T(8,128)(2,1)} %get-tuple-element.39.refs_3_.refs_0_, ...), custom_call_target="tpu_custom_call" | custom-call | flops 1 | bytes 1 | tf_op jit(solution)/shard_map/pallas_call | solution.py:153
  240.3 2.7 collective-permute-done.26.refs_3_
  243.7 2.2 shard_map.56.refs_4_
  246.0 7.7 %all-to-all-start = ((bf16[16,4,2,32,128]{4,3,2,1,0:T(8,128)(2,1)}), bf16[16,4,2,32,128]{4,3,2,1,0:T(8,128)(2,1)S(1)}, u32[]{:S(2)}, u32[]{:S(2)}) async-start(bf16[16,4,2,32,128]{4,3,2,1,0:T(8,128)(2,1)} %shard_map.56.refs_4_), calls=%async_computation | async-start | bytes 2097152 | tf_op jit(solution)/shard_map/all_to_all | solution.py:327
  253.6 3.5 %collective-permute-start.28 = (bf16[4,3,2,32,128]{4,3,2,1,0:T(8,128)(2,1)}, bf16[4,3,2,32,128]{4,3,2,1,0:T(8,128)(2,1)S(1)}, u32[]{:S(2)}, u32[]{:S(2)}) collective-permute-start(bf16[4,3,2,32,128]{4,3,2,1,0:T(8,128)(2,1)} %get-tuple-element.69), channel_id=1, source_target_pairs={{0,8},{1,9},{2,10},{3,11},{4,12},{5,13},{6,14},{7,15},{8,0},{9,1},... | collective-permute-start | bytes 589832 | tf_op jit(solution)/shard_map/ppermute | solution.py:22
  257.1 1.2 collective-permute-start.29
  258.3 2.8 shard_map.57
  261.1 4.9 %copy.43 = bf16[96,2,32,128]{0,2,3,1:T(8,128)(2,1)} copy(bf16[96,2,32,128]{3,2,1,0:T(8,128)(2,1)} %shard_map.57) | data formatting | bytes 3145728 | tf_op jit(solution)/shard_map/pallas_call | solution.py:209
  266.0 3.0 shard_map.58.refs_5_.refs_1_
  270.4 2.2 shard_map.59.refs_1_
  272.6 1.5 all-to-all-done.refs_0_
  274.1 6.0 %all-to-all-start.2 = ((bf16[16,3,2,32,128]{4,3,2,1,0:T(8,128)(2,1)}), bf16[16,3,2,32,128]{4,3,2,1,0:T(8,128)(2,1)S(1)}, u32[]{:S(2)}, u32[]{:S(2)}) async-start(bf16[16,3,2,32,128]{4,3,2,1,0:T(8,128)(2,1)} %shard_map.59.refs_1_), calls=%async_computation.2 | async-start | bytes 1572864 | tf_op jit(solution)/shard_map/all_to_all | solution.py:327
  280.1 3.3 %shard_map.60 = bf16[96,2,32,18]{3,2,1,0:T(8,128)(2,1)} custom-call(s32[2]{0:T(128)} %pad_add_fusion.1.at_ref.me_ref, s32[1536]{0:T(1024)} %assign_ref.5, bf16[16,4,2,32,128]{4,3,2,1,0:T(8,128)(2,1)} %copy-done, bf16[16,3,2,32,128]{4,3,2,1,0:T(8,128)(2,1)} %shard_map.59.refs_1_), custom_call_target="tpu_custom_call" | custom-call | flops 1 | bytes 1 | tf_op jit(solution)/shard_map/pallas_call | solution.py:209
  283.5 3.8 %copy.44 = bf16[96,2,32,18]{0,2,3,1:T(8,128)(2,1)} copy(bf16[96,2,32,18]{3,2,1,0:T(8,128)(2,1)} %shard_map.60) | data formatting | bytes 442368 | tf_op jit(solution)/shard_map/pallas_call | solution.py:209
  287.3 1.7 shard_map.61.refs_2_.refs_1_
  289.0 7.9 %all-to-all-done.2.refs_1_ = bf16[16,3,2,32,128]{4,3,2,1,0:T(8,128)(2,1)S(1)} async-done(((bf16[16,3,2,32,128]{4,3,2,1,0:T(8,128)(2,1)}), bf16[16,3,2,32,128]{4,3,2,1,0:T(8,128)(2,1)S(1)}, u32[]{:S(2)}, u32[]{:S(2)}) %all-to-all-start.2) | async-done | bytes 786464 | tf_op jit(solution)/shard_map/all_to_all | solution.py:327
  297.7 2.8 shard_map.62
  300.6 4.9 %copy.45 = bf16[96,2,32,128]{0,2,3,1:T(8,128)(2,1)} copy(bf16[96,2,32,128]{3,2,1,0:T(8,128)(2,1)} %shard_map.62) | data formatting | bytes 3145728 | tf_op jit(solution)/shard_map/pallas_call | solution.py:209
  305.4 3.0 shard_map.63
  (120 shorter events, 15.2 us)
Async XLA Ops:
  0.0 1.6 slice-start
  5.1 1.6 slice-start.1
  5.1 10.4 %collective-permute-start.8 = (bf16[16,6,2,32,128]{4,3,2,1,0:T(8,128)(2,1)}, bf16[16,6,2,32,128]{4,3,2,1,0:T(8,128)(2,1)}, u32[]{:S(2)}, u32[]{:S(2)}) collective-permute-start(bf16[16,6,2,32,128]{4,3,2,1,0:T(8,128)(2,1)} %bitcast.37), channel_id=1, source_target_pairs={{0,1},{1,0},{2,3},{3,2},{4,5},{5,4},{6,7},{7,6},{8,9},{9,8},{10,11... | collective-permute-start | bytes 4718600 | tf_op jit(solution)/shard_map/ppermute | solution.py:22
  10.3 1.6 slice-start.3
  10.3 23.8 %collective-permute-start.6 = (bf16[16,6,2,32,128]{4,3,2,1,0:T(8,128)(2,1)}, bf16[16,6,2,32,128]{4,3,2,1,0:T(8,128)(2,1)S(1)}, u32[]{:S(2)}, u32[]{:S(2)}) collective-permute-start(bf16[16,6,2,32,128]{4,3,2,1,0:T(8,128)(2,1)} %bitcast.35), channel_id=1, source_target_pairs={{0,1},{1,0},{2,3},{3,2},{4,5},{5,4},{6,7},{7,6},{8,9},{9,8},{10,11... | collective-permute-start | bytes 4718600 | tf_op jit(solution)/shard_map/ppermute | solution.py:22
  15.5 11.2 %slice-start.2 = ((bf16[96,2,32,274]{0,2,3,1:T(8,128)(2,1)}), bf16[96,2,32,18]{0,2,3,1:T(8,128)(2,1)S(1)}, s32[]{:S(2)}) async-start(bf16[96,2,32,274]{0,2,3,1:T(8,128)(2,1)} %param.4), calls=%async_computation.5 | async-start | bytes 589824 | tf_op jit(solution)/shard_map/slice | solution.py:296
  20.4 83.3 %collective-permute-start.10 = (bf16[16,6,2,32,128]{4,3,2,1,0:T(8,128)(2,1)}, bf16[16,6,2,32,128]{4,3,2,1,0:T(8,128)(2,1)}, u32[]{:S(2)}, u32[]{:S(2)}) collective-permute-start(bf16[16,6,2,32,128]{4,3,2,1,0:T(8,128)(2,1)} %shard_map.47.refs_4_.refs_0_), channel_id=1, source_target_pairs={{0,2},{1,3},{2,0},{3,1},{4,6},{5,7},{6,4},{7,5},{8,10},{9,11},{10,... | collective-permute-start | bytes 4718600 | tf_op jit(solution)/shard_map/ppermute | solution.py:22
  26.7 2.2 slice-start.4
  28.8 5.3 %copy-start.10 = (bf16[16,1,2,32,128]{4,3,2,1,0:T(8,128)(2,1)}, bf16[16,1,2,32,128]{4,3,2,1,0:T(8,128)(2,1)S(1)}, u32[]{:S(2)}) copy-start(bf16[16,1,2,32,128]{4,3,2,1,0:T(8,128)(2,1)S(1)} %pad_bitcast_fusion.refs_1_) | copy-start | bytes 786436
  28.8 5.0 %collective-permute-start.7 = (bf16[16,1,2,32,128]{4,3,2,1,0:T(8,128)(2,1)S(1)}, bf16[16,1,2,32,128]{4,3,2,1,0:T(8,128)(2,1)S(1)}, u32[]{:S(2)}, u32[]{:S(2)}) collective-permute-start(bf16[16,1,2,32,128]{4,3,2,1,0:T(8,128)(2,1)S(1)} %pad_bitcast_fusion.refs_1_), channel_id=1, source_target_pairs={{0,1},{1,0},{2,3},{3,2},{4,5},{5,4},{6,7},{7,6},{8,9},{9,8},{10,11... | collective-permute-start | bytes 786440 | tf_op jit(solution)/shard_map/ppermute | solution.py:22
  29.3 24.6 %collective-permute-start = (s32[96]{0:T(128)S(1)}, s32[96]{0:T(128)S(1)}, u32[]{:S(2)}, u32[]{:S(2)}) collective-permute-start(s32[96]{0:T(128)S(1)} %get-tuple-element.77), channel_id=1, source_target_pairs={{0,4},{1,5},{2,6},{3,7},{4,0},{5,1},{6,2},{7,3},{8,12},{9,13},{10,... | collective-permute-start | bytes 1160 | tf_op jit(solution)/shard_map/ppermute | solution.py:22
  31.0 23.1 %collective-permute-start.1 = (s32[96]{0:T(128)S(1)}, s32[96]{0:T(128)S(1)}, u32[]{:S(2)}, u32[]{:S(2)}) collective-permute-start(s32[96]{0:T(128)S(1)} %get-tuple-element.76), channel_id=1, source_target_pairs={{0,8},{1,9},{2,10},{3,11},{4,12},{5,13},{6,14},{7,15},{8,0},{9,1},... | collective-permute-start | bytes 1160 | tf_op jit(solution)/shard_map/ppermute | solution.py:22
  33.9 24.1 %collective-permute-start.2 = (s32[96]{0:T(128)S(1)}, s32[96]{0:T(128)S(1)}, u32[]{:S(2)}, u32[]{:S(2)}) collective-permute-start(s32[96]{0:T(128)S(1)} %get-tuple-element.75), channel_id=1, source_target_pairs={{0,12},{1,13},{2,14},{3,15},{4,8},{5,9},{6,10},{7,11},{8,4},{9,5},... | collective-permute-start | bytes 1160 | tf_op jit(solution)/shard_map/ppermute | solution.py:22
  34.6 1.1 copy-start.6
  41.6 104.9 %collective-permute-start.9 = (bf16[16,4,2,32,128]{4,3,2,1,0:T(8,128)(2,1)}, bf16[16,4,2,32,128]{4,3,2,1,0:T(8,128)(2,1)}, u32[]{:S(2)}, u32[]{:S(2)}) collective-permute-start(bf16[16,4,2,32,128]{4,3,2,1,0:T(8,128)(2,1)} %get-tuple-element.45.refs_2_.refs_0_), channel_id=1, source_target_pairs={{0,2},{1,3},{2,0},{3,1},{4,6},{5,7},{6,4},{7,5},{8,10},{9,11},{10,... | collective-permute-start | bytes 3145736 | tf_op jit(solution)/shard_map/ppermute | solution.py:22
  50.3 53.4 %copy-start.14 = (bf16[16,3,2,32,128]{4,3,2,1,0:T(8,128)(2,1)S(1)}, bf16[16,3,2,32,128]{4,3,2,1,0:T(8,128)(2,1)}, u32[]{:S(2)}) copy-start(bf16[16,3,2,32,128]{4,3,2,1,0:T(8,128)(2,1)} %get-tuple-element.58.refs_0_) | copy-start | bytes 2359300
  53.9 63.9 %collective-permute-start.3 = (bf16[4,6,2,32,128]{4,3,2,1,0:T(8,128)(2,1)}, bf16[4,6,2,32,128]{4,3,2,1,0:T(8,128)(2,1)S(1)}, u32[]{:S(2)}, u32[]{:S(2)}) collective-permute-start(bf16[4,6,2,32,128]{4,3,2,1,0:T(8,128)(2,1)} %get-tuple-element.40), channel_id=1, source_target_pairs={{0,4},{1,5},{2,6},{3,7},{4,0},{5,1},{6,2},{7,3},{8,12},{9,13},{10,... | collective-permute-start | bytes 1179656 | tf_op jit(solution)/shard_map/ppermute | solution.py:22
  54.1 65.4 %collective-permute-start.4 = (bf16[4,6,2,32,128]{4,3,2,1,0:T(8,128)(2,1)}, bf16[4,6,2,32,128]{4,3,2,1,0:T(8,128)(2,1)S(1)}, u32[]{:S(2)}, u32[]{:S(2)}) collective-permute-start(bf16[4,6,2,32,128]{4,3,2,1,0:T(8,128)(2,1)} %get-tuple-element.41), channel_id=1, source_target_pairs={{0,8},{1,9},{2,10},{3,11},{4,12},{5,13},{6,14},{7,15},{8,0},{9,1},... | collective-permute-start | bytes 1179656 | tf_op jit(solution)/shard_map/ppermute | solution.py:22
  57.9 64.4 %collective-permute-start.5 = (bf16[4,6,2,32,128]{4,3,2,1,0:T(8,128)(2,1)}, bf16[4,6,2,32,128]{4,3,2,1,0:T(8,128)(2,1)S(1)}, u32[]{:S(2)}, u32[]{:S(2)}) collective-permute-start(bf16[4,6,2,32,128]{4,3,2,1,0:T(8,128)(2,1)} %get-tuple-element.42), channel_id=1, source_target_pairs={{0,12},{1,13},{2,14},{3,15},{4,8},{5,9},{6,10},{7,11},{8,4},{9,5},... | collective-permute-start | bytes 1179656 | tf_op jit(solution)/shard_map/ppermute | solution.py:22
  103.7 69.1 %collective-permute-start.20 = (bf16[16,3,2,32,128]{4,3,2,1,0:T(8,128)(2,1)S(1)}, bf16[16,3,2,32,128]{4,3,2,1,0:T(8,128)(2,1)}, u32[]{:S(2)}, u32[]{:S(2)}) collective-permute-start(bf16[16,3,2,32,128]{4,3,2,1,0:T(8,128)(2,1)S(1)} %copy-done.14), channel_id=1, source_target_pairs={{0,2},{1,3},{2,0},{3,1},{4,6},{5,7},{6,4},{7,5},{8,10},{9,11},{10,... | collective-permute-start | bytes 2359304 | tf_op jit(solution)/shard_map/ppermute | solution.py:22
  117.8 22.2 %copy-start.2 = (bf16[4,6,2,32,128]{4,3,2,1,0:T(8,128)(2,1)}, bf16[4,6,2,32,128]{4,3,2,1,0:T(8,128)(2,1)S(1)}, u32[]{:S(2)}) copy-start(bf16[4,6,2,32,128]{4,3,2,1,0:T(8,128)(2,1)S(1)} %collective-permute-done.3.refs_1_) | copy-start | bytes 1179652
  117.8 12.4 %collective-permute-start.11 = (bf16[4,6,2,32,128]{4,3,2,1,0:T(8,128)(2,1)}, bf16[4,6,2,32,128]{4,3,2,1,0:T(8,128)(2,1)S(1)}, u32[]{:S(2)}, u32[]{:S(2)}) collective-permute-start(bf16[4,6,2,32,128]{4,3,2,1,0:T(8,128)(2,1)} %get-tuple-element.47), channel_id=1, source_target_pairs={{0,4},{1,5},{2,6},{3,7},{4,0},{5,1},{6,2},{7,3},{8,12},{9,13},{10,... | collective-permute-start | bytes 1179656 | tf_op jit(solution)/shard_map/ppermute | solution.py:22
  119.5 20.5 %copy-start.3 = (bf16[4,6,2,32,128]{4,3,2,1,0:T(8,128)(2,1)}, bf16[4,6,2,32,128]{4,3,2,1,0:T(8,128)(2,1)S(1)}, u32[]{:S(2)}) copy-start(bf16[4,6,2,32,128]{4,3,2,1,0:T(8,128)(2,1)S(1)} %collective-permute-done.4.refs_2_) | copy-start | bytes 1179652
  119.5 17.9 %collective-permute-start.12 = (bf16[4,6,2,32,128]{4,3,2,1,0:T(8,128)(2,1)}, bf16[4,6,2,32,128]{4,3,2,1,0:T(8,128)(2,1)S(1)}, u32[]{:S(2)}, u32[]{:S(2)}) collective-permute-start(bf16[4,6,2,32,128]{4,3,2,1,0:T(8,128)(2,1)} %get-tuple-element.48), channel_id=1, source_target_pairs={{0,8},{1,9},{2,10},{3,11},{4,12},{5,13},{6,14},{7,15},{8,0},{9,1},... | collective-permute-start | bytes 1179656 | tf_op jit(solution)/shard_map/ppermute | solution.py:22
  122.4 17.6 %copy-start.4 = (bf16[4,6,2,32,128]{4,3,2,1,0:T(8,128)(2,1)}, bf16[4,6,2,32,128]{4,3,2,1,0:T(8,128)(2,1)S(1)}, u32[]{:S(2)}) copy-start(bf16[4,6,2,32,128]{4,3,2,1,0:T(8,128)(2,1)S(1)} %collective-permute-done.5.refs_3_) | copy-start | bytes 1179652
  122.4 17.6 %collective-permute-start.13 = (bf16[4,6,2,32,128]{4,3,2,1,0:T(8,128)(2,1)}, bf16[4,6,2,32,128]{4,3,2,1,0:T(8,128)(2,1)S(1)}, u32[]{:S(2)}, u32[]{:S(2)}) collective-permute-start(bf16[4,6,2,32,128]{4,3,2,1,0:T(8,128)(2,1)} %get-tuple-element.49), channel_id=1, source_target_pairs={{0,12},{1,13},{2,14},{3,15},{4,8},{5,9},{6,10},{7,11},{8,4},{9,5},... | collective-permute-start | bytes 1179656 | tf_op jit(solution)/shard_map/ppermute | solution.py:22
  130.2 9.8 %copy-start.18 = (bf16[4,6,2,32,128]{4,3,2,1,0:T(8,128)(2,1)}, bf16[4,6,2,32,128]{4,3,2,1,0:T(8,128)(2,1)S(1)}, u32[]{:S(2)}) copy-start(bf16[4,6,2,32,128]{4,3,2,1,0:T(8,128)(2,1)S(1)} %collective-permute-done.11.refs_5_) | copy-start | bytes 1179652
  137.4 2.6 copy-start.19
  140.0 0.8 copy-start.20
  146.5 9.8 %copy-start.29 = (bf16[4,6,2,32,128]{4,3,2,1,0:T(8,128)(2,1)S(1)}, bf16[4,6,2,32,128]{4,3,2,1,0:T(8,128)(2,1)}, u32[]{:S(2)}) copy-start(bf16[4,6,2,32,128]{4,3,2,1,0:T(8,128)(2,1)} %get-tuple-element.57) | copy-start | bytes 1179652
  151.7 24.3 %collective-permute-start.14 = (bf16[4,4,2,32,128]{4,3,2,1,0:T(8,128)(2,1)}, bf16[4,4,2,32,128]{4,3,2,1,0:T(8,128)(2,1)S(1)}, u32[]{:S(2)}, u32[]{:S(2)}) collective-permute-start(bf16[4,4,2,32,128]{4,3,2,1,0:T(8,128)(2,1)} %get-tuple-element.52), channel_id=1, source_target_pairs={{0,4},{1,5},{2,6},{3,7},{4,0},{5,1},{6,2},{7,3},{8,12},{9,13},{10,... | collective-permute-start | bytes 786440 | tf_op jit(solution)/shard_map/ppermute | solution.py:22
  152.7 34.7 %collective-permute-start.17 = (bf16[4,6,2,32,128]{4,3,2,1,0:T(8,128)(2,1)}, bf16[4,6,2,32,128]{4,3,2,1,0:T(8,128)(2,1)S(1)}, u32[]{:S(2)}, u32[]{:S(2)}) collective-permute-start(bf16[4,6,2,32,128]{4,3,2,1,0:T(8,128)(2,1)} %get-tuple-element.55), channel_id=1, source_target_pairs={{0,4},{1,5},{2,6},{3,7},{4,0},{5,1},{6,2},{7,3},{8,12},{9,13},{10,... | collective-permute-start | bytes 1179656 | tf_op jit(solution)/shard_map/ppermute | solution.py:22
  153.7 33.6 %collective-permute-start.18 = (bf16[4,6,2,32,128]{4,3,2,1,0:T(8,128)(2,1)}, bf16[4,6,2,32,128]{4,3,2,1,0:T(8,128)(2,1)S(1)}, u32[]{:S(2)}, u32[]{:S(2)}) collective-permute-start(bf16[4,6,2,32,128]{4,3,2,1,0:T(8,128)(2,1)} %get-tuple-element.56), channel_id=1, source_target_pairs={{0,8},{1,9},{2,10},{3,11},{4,12},{5,13},{6,14},{7,15},{8,0},{9,1},... | collective-permute-start | bytes 1179656 | tf_op jit(solution)/shard_map/ppermute | solution.py:22
  156.3 31.0 %collective-permute-start.19 = (bf16[4,6,2,32,128]{4,3,2,1,0:T(8,128)(2,1)S(1)}, bf16[4,6,2,32,128]{4,3,2,1,0:T(8,128)(2,1)S(1)}, u32[]{:S(2)}, u32[]{:S(2)}) collective-permute-start(bf16[4,6,2,32,128]{4,3,2,1,0:T(8,128)(2,1)S(1)} %copy-done.29), channel_id=1, source_target_pairs={{0,12},{1,13},{2,14},{3,15},{4,8},{5,9},{6,10},{7,11},{8,4},{9,5},... | collective-permute-start | bytes 1179656 | tf_op jit(solution)/shard_map/ppermute | solution.py:22
  172.8 9.0 %collective-permute-start.15 = (bf16[4,4,2,32,128]{4,3,2,1,0:T(8,128)(2,1)}, bf16[4,4,2,32,128]{4,3,2,1,0:T(8,128)(2,1)S(1)}, u32[]{:S(2)}, u32[]{:S(2)}) collective-permute-start(bf16[4,4,2,32,128]{4,3,2,1,0:T(8,128)(2,1)} %get-tuple-element.53), channel_id=1, source_target_pairs={{0,8},{1,9},{2,10},{3,11},{4,12},{5,13},{6,14},{7,15},{8,0},{9,1},... | collective-permute-start | bytes 786440 | tf_op jit(solution)/shard_map/ppermute | solution.py:22
  176.0 5.1 %copy-start.7 = (bf16[4,4,2,32,128]{4,3,2,1,0:T(8,128)(2,1)}, bf16[4,4,2,32,128]{4,3,2,1,0:T(8,128)(2,1)S(1)}, u32[]{:S(2)}) copy-start(bf16[4,4,2,32,128]{4,3,2,1,0:T(8,128)(2,1)S(1)} %collective-permute-done.14.refs_5_) | copy-start | bytes 786436
  176.0 11.3 %collective-permute-start.16 = (bf16[4,4,2,32,128]{4,3,2,1,0:T(8,128)(2,1)}, bf16[4,4,2,32,128]{4,3,2,1,0:T(8,128)(2,1)S(1)}, u32[]{:S(2)}, u32[]{:S(2)}) collective-permute-start(bf16[4,4,2,32,128]{4,3,2,1,0:T(8,128)(2,1)} %get-tuple-element.54), channel_id=1, source_target_pairs={{0,12},{1,13},{2,14},{3,15},{4,8},{5,9},{6,10},{7,11},{8,4},{9,5},... | collective-permute-start | bytes 786440 | tf_op jit(solution)/shard_map/ppermute | solution.py:22
  181.8 5.6 %copy-start.8 = (bf16[4,4,2,32,128]{4,3,2,1,0:T(8,128)(2,1)}, bf16[4,4,2,32,128]{4,3,2,1,0:T(8,128)(2,1)S(1)}, u32[]{:S(2)}) copy-start(bf16[4,4,2,32,128]{4,3,2,1,0:T(8,128)(2,1)S(1)} %collective-permute-done.15.refs_6_) | copy-start | bytes 786436
  187.3 0.9 copy-start.15
  187.3 1.0 copy-start.16
  187.3 1.1 copy-start.17
  191.1 20.8 %copy-start.33 = (bf16[4,3,2,32,128]{4,3,2,1,0:T(8,128)(2,1)S(1)}, bf16[4,3,2,32,128]{4,3,2,1,0:T(8,128)(2,1)}, u32[]{:S(2)}) copy-start(bf16[4,3,2,32,128]{4,3,2,1,0:T(8,128)(2,1)} %get-tuple-element.60) | copy-start | bytes 589828
  191.1 20.9 %copy-start.32 = (bf16[4,3,2,32,128]{4,3,2,1,0:T(8,128)(2,1)S(1)}, bf16[4,3,2,32,128]{4,3,2,1,0:T(8,128)(2,1)}, u32[]{:S(2)}) copy-start(bf16[4,3,2,32,128]{4,3,2,1,0:T(8,128)(2,1)} %get-tuple-element.61) | copy-start | bytes 589828
  191.1 24.3 %copy-start.31 = (bf16[4,3,2,32,128]{4,3,2,1,0:T(8,128)(2,1)S(1)}, bf16[4,3,2,32,128]{4,3,2,1,0:T(8,128)(2,1)}, u32[]{:S(2)}) copy-start(bf16[4,3,2,32,128]{4,3,2,1,0:T(8,128)(2,1)} %get-tuple-element.62) | copy-start | bytes 589828
  191.1 54.8 %all-to-all-start.1 = ((bf16[16,6,2,32,128]{4,3,2,1,0:T(8,128)(2,1)}), bf16[16,6,2,32,128]{4,3,2,1,0:T(8,128)(2,1)S(1)}, u32[]{:S(2)}, u32[]{:S(2)}) async-start(bf16[16,6,2,32,128]{4,3,2,1,0:T(8,128)(2,1)} %shard_map.53.refs_8_), calls=%async_computation.1 | async-start | bytes 3145728 | tf_op jit(solution)/shard_map/all_to_all | solution.py:327
  211.9 5.8 %collective-permute-start.21 = (bf16[4,3,2,32,128]{4,3,2,1,0:T(8,128)(2,1)S(1)}, bf16[4,3,2,32,128]{4,3,2,1,0:T(8,128)(2,1)S(1)}, u32[]{:S(2)}, u32[]{:S(2)}) collective-permute-start(bf16[4,3,2,32,128]{4,3,2,1,0:T(8,128)(2,1)S(1)} %copy-done.33), channel_id=1, source_target_pairs={{0,4},{1,5},{2,6},{3,7},{4,0},{5,1},{6,2},{7,3},{8,12},{9,13},{10,... | collective-permute-start | bytes 589832 | tf_op jit(solution)/shard_map/ppermute | solution.py:22
  212.0 9.3 %collective-permute-start.22 = (bf16[4,3,2,32,128]{4,3,2,1,0:T(8,128)(2,1)S(1)}, bf16[4,3,2,32,128]{4,3,2,1,0:T(8,128)(2,1)S(1)}, u32[]{:S(2)}, u32[]{:S(2)}) collective-permute-start(bf16[4,3,2,32,128]{4,3,2,1,0:T(8,128)(2,1)S(1)} %copy-done.32), channel_id=1, source_target_pairs={{0,8},{1,9},{2,10},{3,11},{4,12},{5,13},{6,14},{7,15},{8,0},{9,1},... | collective-permute-start | bytes 589832 | tf_op jit(solution)/shard_map/ppermute | solution.py:22
  215.4 7.9 %collective-permute-start.23 = (bf16[4,3,2,32,128]{4,3,2,1,0:T(8,128)(2,1)S(1)}, bf16[4,3,2,32,128]{4,3,2,1,0:T(8,128)(2,1)S(1)}, u32[]{:S(2)}, u32[]{:S(2)}) collective-permute-start(bf16[4,3,2,32,128]{4,3,2,1,0:T(8,128)(2,1)S(1)} %copy-done.31), channel_id=1, source_target_pairs={{0,12},{1,13},{2,14},{3,15},{4,8},{5,9},{6,10},{7,11},{8,4},{9,5},... | collective-permute-start | bytes 589832 | tf_op jit(solution)/shard_map/ppermute | solution.py:22
  217.6 5.7 %copy-start.11 = (bf16[4,3,2,32,128]{4,3,2,1,0:T(8,128)(2,1)}, bf16[4,3,2,32,128]{4,3,2,1,0:T(8,128)(2,1)S(1)}, u32[]{:S(2)}) copy-start(bf16[4,3,2,32,128]{4,3,2,1,0:T(8,128)(2,1)S(1)} %collective-permute-done.21.refs_9_.refs_5_) | copy-start | bytes 589828
  221.3 2.0 copy-start.12
  230.1 9.2 %collective-permute-start.24 = (bf16[4,4,2,32,128]{4,3,2,1,0:T(8,128)(2,1)}, bf16[4,4,2,32,128]{4,3,2,1,0:T(8,128)(2,1)S(1)}, u32[]{:S(2)}, u32[]{:S(2)}) collective-permute-start(bf16[4,4,2,32,128]{4,3,2,1,0:T(8,128)(2,1)} %get-tuple-element.64), channel_id=1, source_target_pairs={{0,4},{1,5},{2,6},{3,7},{4,0},{5,1},{6,2},{7,3},{8,12},{9,13},{10,... | collective-permute-start | bytes 786440 | tf_op jit(solution)/shard_map/ppermute | solution.py:22
  230.1 10.2 %collective-permute-start.25 = (bf16[4,4,2,32,128]{4,3,2,1,0:T(8,128)(2,1)}, bf16[4,4,2,32,128]{4,3,2,1,0:T(8,128)(2,1)S(1)}, u32[]{:S(2)}, u32[]{:S(2)}) collective-permute-start(bf16[4,4,2,32,128]{4,3,2,1,0:T(8,128)(2,1)} %get-tuple-element.65), channel_id=1, source_target_pairs={{0,8},{1,9},{2,10},{3,11},{4,12},{5,13},{6,14},{7,15},{8,0},{9,1},... | collective-permute-start | bytes 786440 | tf_op jit(solution)/shard_map/ppermute | solution.py:22
  232.8 10.2 %collective-permute-start.26 = (bf16[4,4,2,32,128]{4,3,2,1,0:T(8,128)(2,1)}, bf16[4,4,2,32,128]{4,3,2,1,0:T(8,128)(2,1)S(1)}, u32[]{:S(2)}, u32[]{:S(2)}) collective-permute-start(bf16[4,4,2,32,128]{4,3,2,1,0:T(8,128)(2,1)} %get-tuple-element.66), channel_id=1, source_target_pairs={{0,12},{1,13},{2,14},{3,15},{4,8},{5,9},{6,10},{7,11},{8,4},{9,5},... | collective-permute-start | bytes 786440 | tf_op jit(solution)/shard_map/ppermute | solution.py:22
  239.3 3.7 %copy-start.22 = (bf16[4,4,2,32,128]{4,3,2,1,0:T(8,128)(2,1)}, bf16[4,4,2,32,128]{4,3,2,1,0:T(8,128)(2,1)S(1)}, u32[]{:S(2)}) copy-start(bf16[4,4,2,32,128]{4,3,2,1,0:T(8,128)(2,1)S(1)} %collective-permute-done.24.refs_1_) | copy-start | bytes 786436
  240.3 2.7 copy-start.23
  245.9 11.1 %copy-start.30 = (bf16[4,3,2,32,128]{4,3,2,1,0:T(8,128)(2,1)S(1)}, bf16[4,3,2,32,128]{4,3,2,1,0:T(8,128)(2,1)}, u32[]{:S(2)}) copy-start(bf16[4,3,2,32,128]{4,3,2,1,0:T(8,128)(2,1)} %get-tuple-element.70) | copy-start | bytes 589828
  245.9 12.4 %copy-start.1 = (bf16[16,6,2,32,128]{4,3,2,1,0:T(8,128)(2,1)}, bf16[16,6,2,32,128]{4,3,2,1,0:T(8,128)(2,1)S(1)}, u32[]{:S(2)}) copy-start(bf16[16,6,2,32,128]{4,3,2,1,0:T(8,128)(2,1)S(1)} %all-to-all-done.1.refs_0_) | copy-start | bytes 4718596
  246.0 28.1 %all-to-all-start = ((bf16[16,4,2,32,128]{4,3,2,1,0:T(8,128)(2,1)}), bf16[16,4,2,32,128]{4,3,2,1,0:T(8,128)(2,1)S(1)}, u32[]{:S(2)}, u32[]{:S(2)}) async-start(bf16[16,4,2,32,128]{4,3,2,1,0:T(8,128)(2,1)} %shard_map.56.refs_4_), calls=%async_computation | async-start | bytes 2097152 | tf_op jit(solution)/shard_map/all_to_all | solution.py:327
  253.6 15.4 %collective-permute-start.27 = (bf16[4,3,2,32,128]{4,3,2,1,0:T(8,128)(2,1)}, bf16[4,3,2,32,128]{4,3,2,1,0:T(8,128)(2,1)S(1)}, u32[]{:S(2)}, u32[]{:S(2)}) collective-permute-start(bf16[4,3,2,32,128]{4,3,2,1,0:T(8,128)(2,1)} %get-tuple-element.68), channel_id=1, source_target_pairs={{0,4},{1,5},{2,6},{3,7},{4,0},{5,1},{6,2},{7,3},{8,12},{9,13},{10,... | collective-permute-start | bytes 589832 | tf_op jit(solution)/shard_map/ppermute | solution.py:22
  253.6 15.4 %collective-permute-start.28 = (bf16[4,3,2,32,128]{4,3,2,1,0:T(8,128)(2,1)}, bf16[4,3,2,32,128]{4,3,2,1,0:T(8,128)(2,1)S(1)}, u32[]{:S(2)}, u32[]{:S(2)}) collective-permute-start(bf16[4,3,2,32,128]{4,3,2,1,0:T(8,128)(2,1)} %get-tuple-element.69), channel_id=1, source_target_pairs={{0,8},{1,9},{2,10},{3,11},{4,12},{5,13},{6,14},{7,15},{8,0},{9,1},... | collective-permute-start | bytes 589832 | tf_op jit(solution)/shard_map/ppermute | solution.py:22
  257.1 12.0 %collective-permute-start.29 = (bf16[4,3,2,32,128]{4,3,2,1,0:T(8,128)(2,1)S(1)}, bf16[4,3,2,32,128]{4,3,2,1,0:T(8,128)(2,1)S(1)}, u32[]{:S(2)}, u32[]{:S(2)}) collective-permute-start(bf16[4,3,2,32,128]{4,3,2,1,0:T(8,128)(2,1)S(1)} %copy-done.30), channel_id=1, source_target_pairs={{0,12},{1,13},{2,14},{3,15},{4,8},{5,9},{6,10},{7,11},{8,4},{9,5},... | collective-permute-start | bytes 589832 | tf_op jit(solution)/shard_map/ppermute | solution.py:22
  274.1 6.0 %copy-start = (bf16[16,4,2,32,128]{4,3,2,1,0:T(8,128)(2,1)}, bf16[16,4,2,32,128]{4,3,2,1,0:T(8,128)(2,1)S(1)}, u32[]{:S(2)}) copy-start(bf16[16,4,2,32,128]{4,3,2,1,0:T(8,128)(2,1)S(1)} %all-to-all-done.refs_0_) | copy-start | bytes 3145732
  274.1 22.8 %all-to-all-start.2 = ((bf16[16,3,2,32,128]{4,3,2,1,0:T(8,128)(2,1)}), bf16[16,3,2,32,128]{4,3,2,1,0:T(8,128)(2,1)S(1)}, u32[]{:S(2)}, u32[]{:S(2)}) async-start(bf16[16,3,2,32,128]{4,3,2,1,0:T(8,128)(2,1)} %shard_map.59.refs_1_), calls=%async_computation.2 | async-start | bytes 1572864 | tf_op jit(solution)/shard_map/all_to_all | solution.py:327
  296.9 0.9 copy-start.5
  (8 other events, 5.6 us)

commit v5 on v3

--- a/solution.py
+++ b/solution.py
@@ -11,8 +11,9 @@
 TAIL = -1
 FIRST = ((0, 1, 2, 3, 4, 5),)
 SECOND = ((-1, 0, 1, 2), (3, 4, 5))
-ORDER = ((0, 1), (0, 2), (1, 1), (1, 2), (2, 1), (0, 3), (2, 2), (1, 3), (2, 3))
+ORDER = ((0, 1), (0, 2), (1, 1), (0, 3), (2, 1), (1, 2), (2, 2), (1, 3), (2, 3))
 WAITS = {}
+BEHIND = {(0, 3): (2,)}
 EARLY = (2, 3)
 
 
@@ -316,6 +317,8 @@
             whole = store(early.transpose(1, 3, 2, 0), 0, cols)
             after.append(whole)
         after += [done[w][0] for w in WAITS.get((k, step), ())]
+        for w in BEHIND.get((k, step), ()):
+            after += chunks[w][1:] if isinstance(chunks[w], list) else [far[w]]
         if step == 1:
             outs = level(1, [where[k]], [chunks[k]], [far[k]], ys)
         elif step == 2:

time: 314 us -> 304 us (0.968)
  starting transfers between devices: 94 us -> 79.5 us
  waiting for transfers between devices: 95.2 us -> 99.6 us
    all_to_all x3, starting transfers between devices: 40.5 us -> 32.8 us  [per_device(): lax.all_to_all(outs[0], 'order', split_axis=0, concat_axis=0, tiled=True)]
    ppermute x30, starting transfers between devices: 53.5 us -> 46.7 us  [from_partner(): return lax.ppermute(value, 'lat', [(i, i ^ mask) for i in range(size)])]
    ppermute x30, waiting for transfers between devices: 90.1 us -> 95.2 us  [from_partner(): return lax.ppermute(value, 'lat', [(i, i ^ mask) for i in range(size)])]
    unnamed x65 -> x61, local copies, waits for them, and re-layouts: 9.16 us -> 7.65 us
  transfers between devices with their start and end apart: 33 -> 33, of which waited for: 14 -> 11; matrix products, arithmetic and copies ran while one was open for 10% -> 11% of each run, Pallas kernels for 19% -> 20%
where the time goes in v5:
time: 304 us; the launch traced here: 300 us
  waiting for transfers between devices  99.6 us (33%)
  starting transfers between devices  79.5 us (26%)
  Pallas kernels  68.5 us (23%)
  local copies, waits for them, and re-layouts  50.2 us (17%)
    ppermute x30, waiting for transfers between devices, from_partner(): return lax.ppermute(value, 'lat', [(i, i ^ mask) for i in range(size)])  95.2 us
    ppermute x30, starting transfers between devices, from_partner(): return lax.ppermute(value, 'lat', [(i, i ^ mask) for i in range(size)])  46.7 us
    all_to_all x3, starting transfers between devices, per_device(): lax.all_to_all(outs[0], 'order', split_axis=0, concat_axis=0, tiled=True)  32.8 us
    pallas_call x5, Pallas kernels, run_level(): pl.pallas_call(functools.partial(level_kernel, spec, lev, tail_w), in_spe...  25.1 us
    pallas_call x3, Pallas kernels, run_last(): pl.pallas_call(functools.partial(last_kernel, {'ys': ys, 'slots': slots},...  16.3 us
    slice x7, local copies, waits for them, and re-layouts, level_weights(): return six(c[l])  14.9 us
    pallas_call x3, local copies, waits for them, and re-layouts, place(): pl.pallas_call(functools.partial(place_kernel, tail_w, slots), in_specs=[...  13.6 us
    pallas_call x3, Pallas kernels, place(): pl.pallas_call(functools.partial(place_kernel, tail_w, slots), in_specs=[...  8.91 us
  transfers between devices with their start and end apart: 33, of which 11 were waited for; matrix products, arithmetic and copies ran while one was open for 11% of the time, Pallas kernels for 20%

profile of v5, /device:TPU:32, one launch (start us, length us, event | category | flops | bytes accessed | tf_op | source)
XLA Modules:
  0.0 299.8 jit_solution(15580652766911560715)
XLA Ops:
  0.0 1.6 slice-done
  1.6 3.5 %copy.33 = bf16[96,2,32,128]{3,2,1,0:T(8,128)(2,1)} copy(bf16[96,2,32,128]{0,2,3,1:T(8,128)(2,1)S(1)} %slice-done) | data formatting | bytes 3145728 | tf_op jit(solution)/shard_map/slice | solution.py:265
  5.1 1.6 slice-done.1
  6.7 3.6 %copy.39 = bf16[96,2,32,128]{3,2,1,0:T(8,128)(2,1)} copy(bf16[96,2,32,128]{0,2,3,1:T(8,128)(2,1)S(1)} %slice-done.1) | data formatting | bytes 3145728 | tf_op jit(solution)/shard_map/slice | solution.py:295
  11.8 3.2 %copy.38 = bf16[1,96,2,32,64]{4,3,2,1,0:T(8,128)(2,1)} copy(bf16[1,96,2,32,64]{1,4,3,2,0:T(8,128)(2,1)S(1)} %slice-done.3) | data formatting | bytes 1572864 | tf_op jit(solution)/shard_map/slice | solution.py:263
  15.6 4.9 %shard_map.47.refs_4_.refs_0_ = bf16[16,6,2,32,128]{4,3,2,1,0:T(8,128)(2,1)} custom-call(s32[2]{0:T(128)} %pad_add_fusion.1.at_ref.me_ref, s32[768]{0:T(1024)} %reshape.24.pat_ref, bf16[16,6,2,32,64]{4,3,2,1,0:T(8,128)(2,1)} %bitcast.31, bf16[16,6,2,32,128]{4,3,2,1,0:T(8,128)(2,1)} %bitcast.38, bf16[16,6,2,32,128]{4,3,2,1,0:T(8,128)(2,1)} %collective-permute-done.8.refs_1_), custom_call_target="tpu_custom_call" | custom-call | flops 1 | bytes 1 | tf_op jit(solution)/shard_map/pallas_call | solution.py:89
  20.5 6.3 %collective-permute-start.10 = (bf16[16,6,2,32,128]{4,3,2,1,0:T(8,128)(2,1)}, bf16[16,6,2,32,128]{4,3,2,1,0:T(8,128)(2,1)}, u32[]{:S(2)}, u32[]{:S(2)}) collective-permute-start(bf16[16,6,2,32,128]{4,3,2,1,0:T(8,128)(2,1)} %shard_map.47.refs_4_.refs_0_), channel_id=1, source_target_pairs={{0,2},{1,3},{2,0},{3,1},{4,6},{5,7},{6,4},{7,5},{8,10},{9,11},{10,... | collective-permute-start | bytes 4718600 | tf_op jit(solution)/shard_map/ppermute | solution.py:22
  27.1 3.1 %collective-permute-start.2 = (s32[96]{0:T(128)S(1)}, s32[96]{0:T(128)S(1)}, u32[]{:S(2)}, u32[]{:S(2)}) collective-permute-start(s32[96]{0:T(128)S(1)} %get-tuple-element.75), channel_id=1, source_target_pairs={{0,12},{1,13},{2,14},{3,15},{4,8},{5,9},{6,10},{7,11},{8,4},{9,5},... | collective-permute-start | bytes 1160 | tf_op jit(solution)/shard_map/ppermute | solution.py:22
  30.9 1.4 copy.42
  33.1 2.5 fusion.4
  35.6 3.0 %copy.34 = bf16[1,96,2,32,64]{4,3,2,1,0:T(8,128)(2,1)} copy(bf16[1,96,2,32,64]{1,4,3,2,0:T(8,128)(2,1)S(1)} %get-tuple-element.73) | data formatting | bytes 1572864 | tf_op jit(solution)/shard_map/slice | solution.py:263
  38.7 3.1 %copy.35 = bf16[1,96,2,32,64]{4,3,2,1,0:T(8,128)(2,1)} copy(bf16[1,96,2,32,64]{1,4,3,2,0:T(8,128)(2,1)S(1)} %get-tuple-element.72) | data formatting | bytes 1572864 | tf_op jit(solution)/shard_map/slice | solution.py:263
  41.7 3.5 %shard_map.46 = (bf16[4,6,2,32,128]{4,3,2,1,0:T(8,128)(2,1)}, bf16[4,6,2,32,128]{4,3,2,1,0:T(8,128)(2,1)}, bf16[4,6,2,32,128]{4,3,2,1,0:T(8,128)(2,1)}, bf16[4,6,2,32,128]{4,3,2,1,0:T(8,128)(2,1)}) custom-call(s32[2]{0:T(128)} %pad_add_fusion.1.at_ref.me_ref, bf16[16,6,2,32,64]{4,3,2,1,0:T(8,128)(2,1)} %bitcast.39, bf16[16,6,2,32,64]{4,3,2,1,0:T(8,128)(2,1)} %bitcast.40), custom_call_target="tpu_custom_call" | custom-call | flops 1 | bytes 1 | tf_op jit(solution)/shard_map/pallas_call | solution.py:110
  45.4 1.6 collective-permute-start.4
  47.0 3.0 %collective-permute-start.5 = (bf16[4,6,2,32,128]{4,3,2,1,0:T(8,128)(2,1)}, bf16[4,6,2,32,128]{4,3,2,1,0:T(8,128)(2,1)S(1)}, u32[]{:S(2)}, u32[]{:S(2)}) collective-permute-start(bf16[4,6,2,32,128]{4,3,2,1,0:T(8,128)(2,1)} %get-tuple-element.42), channel_id=1, source_target_pairs={{0,12},{1,13},{2,14},{3,15},{4,8},{5,9},{6,10},{7,11},{8,4},{9,5},... | collective-permute-start | bytes 1179656 | tf_op jit(solution)/shard_map/ppermute | solution.py:22
  50.0 5.8 %shard_map.48 = (bf16[16,4,2,32,128]{4,3,2,1,0:T(8,128)(2,1)}, bf16[16,3,2,32,128]{4,3,2,1,0:T(8,128)(2,1)}) custom-call(s32[2]{0:T(128)} %pad_add_fusion.1.at_ref.me_ref, s32[768]{0:T(1024)} %reshape.24.pat_ref, bf16[16,6,2,32,64]{4,3,2,1,0:T(8,128)(2,1)} %bitcast.32, bf16[16,6,2,32,128]{4,3,2,1,0:T(8,128)(2,1)} %bitcast.36, ...), custom_call_target="tpu_custom_call" | custom-call | flops 1 | bytes 1 | tf_op jit(solution)/shard_map/pallas_call | solution.py:89
  55.8 9.5 %collective-permute-done.1 = s32[96]{0:T(128)S(1)} collective-permute-done((s32[96]{0:T(128)S(1)}, s32[96]{0:T(128)S(1)}, u32[]{:S(2)}, u32[]{:S(2)}) %collective-permute-start.1) | collective-permute-done | bytes 416 | tf_op jit(solution)/shard_map/ppermute | solution.py:22
  65.3 38.5 %collective-permute-done.10.refs_1_ = bf16[16,6,2,32,128]{4,3,2,1,0:T(8,128)(2,1)} collective-permute-done((bf16[16,6,2,32,128]{4,3,2,1,0:T(8,128)(2,1)}, bf16[16,6,2,32,128]{4,3,2,1,0:T(8,128)(2,1)}, u32[]{:S(2)}, u32[]{:S(2)}) %collective-permute-start.10) | collective-permute-done | bytes 1572896 | tf_op jit(solution)/shard_map/ppermute | solution.py:22
  103.8 1.6 collective-permute-start
  105.4 3.0 %copy.37 = bf16[1,96,2,32,64]{4,3,2,1,0:T(8,128)(2,1)} copy(bf16[1,96,2,32,64]{1,4,3,2,0:T(8,128)(2,1)S(1)} %get-tuple-element.71) | data formatting | bytes 1572864 | tf_op jit(solution)/shard_map/slice | solution.py:263
  108.4 5.2 %shard_map.49 = (bf16[4,6,2,32,128]{4,3,2,1,0:T(8,128)(2,1)}, bf16[4,6,2,32,128]{4,3,2,1,0:T(8,128)(2,1)}, bf16[4,6,2,32,128]{4,3,2,1,0:T(8,128)(2,1)}, bf16[4,6,2,32,128]{4,3,2,1,0:T(8,128)(2,1)}) custom-call(s32[2]{0:T(128)} %pad_add_fusion.1.at_ref.me_ref, s32[768]{0:T(1024)} %reshape.24.pat_ref, bf16[16,6,2,32,64]{4,3,2,1,0:T(8,128)(2,1)} %bitcast.28, ...), custom_call_target="tpu_custom_call" | custom-call | flops 1 | bytes 1 | tf_op jit(solution)/shard_map/pallas_call | solution.py:89
  114.1 3.2 %collective-permute-start.12 = (bf16[4,6,2,32,128]{4,3,2,1,0:T(8,128)(2,1)}, bf16[4,6,2,32,128]{4,3,2,1,0:T(8,128)(2,1)}, u32[]{:S(2)}, u32[]{:S(2)}) collective-permute-start(bf16[4,6,2,32,128]{4,3,2,1,0:T(8,128)(2,1)} %get-tuple-element.48), channel_id=1, source_target_pairs={{0,8},{1,9},{2,10},{3,11},{4,12},{5,13},{6,14},{7,15},{8,0},{9,1},... | collective-permute-start | bytes 1179656 | tf_op jit(solution)/shard_map/ppermute | solution.py:22
  117.3 1.1 collective-permute-start.13
  118.4 5.9 %collective-permute-start.17 = (bf16[16,3,2,32,128]{4,3,2,1,0:T(8,128)(2,1)}, bf16[16,3,2,32,128]{4,3,2,1,0:T(8,128)(2,1)S(1)}, u32[]{:S(2)}, u32[]{:S(2)}) collective-permute-start(bf16[16,3,2,32,128]{4,3,2,1,0:T(8,128)(2,1)} %get-tuple-element.55.refs_0_), channel_id=1, source_target_pairs={{0,2},{1,3},{2,0},{3,1},{4,6},{5,7},{6,4},{7,5},{8,10},{9,11},{10,... | collective-permute-start | bytes 2359304 | tf_op jit(solution)/shard_map/ppermute | solution.py:22
  124.9 1.1 collective-permute-done.11.refs_5_
  126.0 7.0 %collective-permute-done.12.refs_6_ = bf16[4,6,2,32,128]{4,3,2,1,0:T(8,128)(2,1)} collective-permute-done((bf16[4,6,2,32,128]{4,3,2,1,0:T(8,128)(2,1)}, bf16[4,6,2,32,128]{4,3,2,1,0:T(8,128)(2,1)}, u32[]{:S(2)}, u32[]{:S(2)}) %collective-permute-start.12) | collective-permute-done | bytes 393248 | tf_op jit(solution)/shard_map/ppermute | solution.py:22
  133.0 2.6 collective-permute-done.13.refs_7_
  135.6 5.7 %shard_map.50 = (bf16[4,6,2,32,128]{4,3,2,1,0:T(8,128)(2,1)}, bf16[4,6,2,32,128]{4,3,2,1,0:T(8,128)(2,1)}, bf16[4,6,2,32,128]{4,3,2,1,0:T(8,128)(2,1)}, bf16[4,6,2,32,128]{4,3,2,1,0:T(8,128)(2,1)}) custom-call(s32[384]{0:T(512)} %pad_add_fusion.pat_ref, bf16[4,6,2,32,128]{4,3,2,1,0:T(8,128)(2,1)} %get-tuple-element.39.refs_3_.refs_0_, ...), custom_call_target="tpu_custom_call" | custom-call | flops 1 | bytes 1 | tf_op jit(solution)/shard_map/pallas_call | solution.py:153
  141.4 2.5 collective-permute-start.19
  143.9 2.2 collective-permute-start.20
  146.1 1.0 copy-done.7
  147.0 5.1 %shard_map.51 = (bf16[4,4,2,32,128]{4,3,2,1,0:T(8,128)(2,1)}, bf16[4,4,2,32,128]{4,3,2,1,0:T(8,128)(2,1)}, bf16[4,4,2,32,128]{4,3,2,1,0:T(8,128)(2,1)}, bf16[4,4,2,32,128]{4,3,2,1,0:T(8,128)(2,1)}) custom-call(s32[2]{0:T(128)} %pad_add_fusion.1.at_ref.me_ref, s32[768]{0:T(1024)} %reshape.24.pat_ref, bf16[16,6,2,32,64]{4,3,2,1,0:T(8,128)(2,1)} %bitcast.29, ...), custom_call_target="tpu_custom_call" | custom-call | flops 1 | bytes 1 | tf_op jit(solution)/shard_map/pallas_call | solution.py:89
  152.1 20.6 %collective-permute-done.17.refs_5_.refs_1_ = bf16[16,3,2,32,128]{4,3,2,1,0:T(8,128)(2,1)S(1)} collective-permute-done((bf16[16,3,2,32,128]{4,3,2,1,0:T(8,128)(2,1)}, bf16[16,3,2,32,128]{4,3,2,1,0:T(8,128)(2,1)S(1)}, u32[]{:S(2)}, u32[]{:S(2)}) %collective-permute-start.17) | collective-permute-done | bytes 786464 | tf_op jit(solution)/shard_map/ppermute | solution.py:22
  174.1 2.6 shard_map.52.refs_2_
  176.7 17.7 %all-to-all-start.1 = ((bf16[16,6,2,32,128]{4,3,2,1,0:T(8,128)(2,1)}), bf16[16,6,2,32,128]{4,3,2,1,0:T(8,128)(2,1)S(1)}, u32[]{:S(2)}, u32[]{:S(2)}) async-start(bf16[16,6,2,32,128]{4,3,2,1,0:T(8,128)(2,1)} %shard_map.52.refs_2_), calls=%async_computation.1 | async-start | bytes 3145728 | tf_op jit(solution)/shard_map/all_to_all | solution.py:328
  194.4 3.8 %collective-permute-start.15 = (bf16[4,4,2,32,128]{4,3,2,1,0:T(8,128)(2,1)S(1)}, bf16[4,4,2,32,128]{4,3,2,1,0:T(8,128)(2,1)S(1)}, u32[]{:S(2)}, u32[]{:S(2)}) collective-permute-start(bf16[4,4,2,32,128]{4,3,2,1,0:T(8,128)(2,1)S(1)} %copy-done.25), channel_id=1, source_target_pairs={{0,8},{1,9},{2,10},{3,11},{4,12},{5,13},{6,14},{7,15},{8,0},{9,1},... | collective-permute-start | bytes 786440 | tf_op jit(solution)/shard_map/ppermute | solution.py:22
  198.2 0.9 collective-permute-start.16
  199.1 4.1 %shard_map.53 = (bf16[4,3,2,32,128]{4,3,2,1,0:T(8,128)(2,1)}, bf16[4,3,2,32,128]{4,3,2,1,0:T(8,128)(2,1)}, bf16[4,3,2,32,128]{4,3,2,1,0:T(8,128)(2,1)}, bf16[4,3,2,32,128]{4,3,2,1,0:T(8,128)(2,1)}) custom-call(s32[2]{0:T(128)} %pad_add_fusion.1.at_ref.me_ref, s32[768]{0:T(1024)} %reshape.24.pat_ref, bf16[16,6,2,32,64]{4,3,2,1,0:T(8,128)(2,1)} %bitcast.30, ...), custom_call_target="tpu_custom_call" | custom-call | flops 1 | bytes 1 | tf_op jit(solution)/shard_map/pallas_call | solution.py:89
  203.2 3.7 %collective-permute-done.15.refs_6_ = bf16[4,4,2,32,128]{4,3,2,1,0:T(8,128)(2,1)S(1)} collective-permute-done((bf16[4,4,2,32,128]{4,3,2,1,0:T(8,128)(2,1)S(1)}, bf16[4,4,2,32,128]{4,3,2,1,0:T(8,128)(2,1)S(1)}, u32[]{:S(2)}, u32[]{:S(2)}) %collective-permute-start.15) | collective-permute-done | bytes 262176 | tf_op jit(solution)/shard_map/ppermute | solution.py:22
  206.9 1.8 collective-permute-done.16.refs_7_
  209.3 6.2 %shard_map.54 = (bf16[4,4,2,32,128]{4,3,2,1,0:T(8,128)(2,1)}, bf16[4,4,2,32,128]{4,3,2,1,0:T(8,128)(2,1)}, bf16[4,4,2,32,128]{4,3,2,1,0:T(8,128)(2,1)}, bf16[4,4,2,32,128]{4,3,2,1,0:T(8,128)(2,1)}) custom-call(s32[384]{0:T(512)} %pad_add_fusion.pat_ref, bf16[4,6,2,32,128]{4,3,2,1,0:T(8,128)(2,1)} %get-tuple-element.39.refs_3_.refs_0_, ...), custom_call_target="tpu_custom_call" | custom-call | flops 1 | bytes 1 | tf_op jit(solution)/shard_map/pallas_call | solution.py:153
  215.5 2.3 collective-permute-start.22
  217.8 2.4 collective-permute-start.23
  220.2 1.6 collective-permute-start.26
  221.8 5.6 %collective-permute-done.25.refs_6_ = bf16[4,3,2,32,128]{4,3,2,1,0:T(8,128)(2,1)S(1)} collective-permute-done((bf16[4,3,2,32,128]{4,3,2,1,0:T(8,128)(2,1)S(1)}, bf16[4,3,2,32,128]{4,3,2,1,0:T(8,128)(2,1)S(1)}, u32[]{:S(2)}, u32[]{:S(2)}) %collective-permute-start.25) | collective-permute-done | bytes 196640 | tf_op jit(solution)/shard_map/ppermute | solution.py:22
  227.4 4.8 %collective-permute-done.26.refs_7_ = bf16[4,3,2,32,128]{4,3,2,1,0:T(8,128)(2,1)S(1)} collective-permute-done((bf16[4,3,2,32,128]{4,3,2,1,0:T(8,128)(2,1)S(1)}, bf16[4,3,2,32,128]{4,3,2,1,0:T(8,128)(2,1)S(1)}, u32[]{:S(2)}, u32[]{:S(2)}) %collective-permute-start.26) | collective-permute-done | bytes 196640 | tf_op jit(solution)/shard_map/ppermute | solution.py:22
  232.9 4.4 %shard_map.55 = (bf16[4,3,2,32,128]{4,3,2,1,0:T(8,128)(2,1)}, bf16[4,3,2,32,128]{4,3,2,1,0:T(8,128)(2,1)}, bf16[4,3,2,32,128]{4,3,2,1,0:T(8,128)(2,1)}, bf16[4,3,2,32,128]{4,3,2,1,0:T(8,128)(2,1)}) custom-call(s32[384]{0:T(512)} %pad_add_fusion.pat_ref, bf16[4,6,2,32,128]{4,3,2,1,0:T(8,128)(2,1)} %get-tuple-element.39.refs_3_.refs_0_, ...), custom_call_target="tpu_custom_call" | custom-call | flops 1 | bytes 1 | tf_op jit(solution)/shard_map/pallas_call | solution.py:153
  238.3 2.3 shard_map.56.refs_4_
  240.5 7.7 %all-to-all-start = ((bf16[16,4,2,32,128]{4,3,2,1,0:T(8,128)(2,1)}), bf16[16,4,2,32,128]{4,3,2,1,0:T(8,128)(2,1)S(1)}, u32[]{:S(2)}, u32[]{:S(2)}) async-start(bf16[16,4,2,32,128]{4,3,2,1,0:T(8,128)(2,1)} %shard_map.56.refs_4_), calls=%async_computation | async-start | bytes 2097152 | tf_op jit(solution)/shard_map/all_to_all | solution.py:328
  248.2 3.8 %collective-permute-start.28 = (bf16[4,3,2,32,128]{4,3,2,1,0:T(8,128)(2,1)}, bf16[4,3,2,32,128]{4,3,2,1,0:T(8,128)(2,1)S(1)}, u32[]{:S(2)}, u32[]{:S(2)}) collective-permute-start(bf16[4,3,2,32,128]{4,3,2,1,0:T(8,128)(2,1)} %get-tuple-element.69), channel_id=1, source_target_pairs={{0,8},{1,9},{2,10},{3,11},{4,12},{5,13},{6,14},{7,15},{8,0},{9,1},... | collective-permute-start | bytes 589832 | tf_op jit(solution)/shard_map/ppermute | solution.py:22
  252.0 0.9 collective-permute-start.29
  252.9 2.8 shard_map.57
  255.7 4.9 %copy.43 = bf16[96,2,32,128]{0,2,3,1:T(8,128)(2,1)} copy(bf16[96,2,32,128]{3,2,1,0:T(8,128)(2,1)} %shard_map.57) | data formatting | bytes 3145728 | tf_op jit(solution)/shard_map/pallas_call | solution.py:209
  260.6 3.0 shard_map.58.refs_5_.refs_1_
  265.0 2.2 shard_map.59.refs_1_
  267.2 7.5 %all-to-all-start.2 = ((bf16[16,3,2,32,128]{4,3,2,1,0:T(8,128)(2,1)}), bf16[16,3,2,32,128]{4,3,2,1,0:T(8,128)(2,1)S(1)}, u32[]{:S(2)}, u32[]{:S(2)}) async-start(bf16[16,3,2,32,128]{4,3,2,1,0:T(8,128)(2,1)} %shard_map.59.refs_1_), calls=%async_computation.2 | async-start | bytes 1572864 | tf_op jit(solution)/shard_map/all_to_all | solution.py:328
  274.7 3.3 %shard_map.60 = bf16[96,2,32,18]{3,2,1,0:T(8,128)(2,1)} custom-call(s32[2]{0:T(128)} %pad_add_fusion.1.at_ref.me_ref, s32[1536]{0:T(1024)} %assign_ref.5, bf16[16,4,2,32,128]{4,3,2,1,0:T(8,128)(2,1)} %copy-done, bf16[16,3,2,32,128]{4,3,2,1,0:T(8,128)(2,1)} %shard_map.59.refs_1_), custom_call_target="tpu_custom_call" | custom-call | flops 1 | bytes 1 | tf_op jit(solution)/shard_map/pallas_call | solution.py:209
  278.0 3.8 %copy.44 = bf16[96,2,32,18]{0,2,3,1:T(8,128)(2,1)} copy(bf16[96,2,32,18]{3,2,1,0:T(8,128)(2,1)} %shard_map.60) | data formatting | bytes 442368 | tf_op jit(solution)/shard_map/pallas_call | solution.py:209
  281.8 1.7 shard_map.61.refs_2_.refs_1_
  283.5 4.4 %all-to-all-done.2.refs_1_ = bf16[16,3,2,32,128]{4,3,2,1,0:T(8,128)(2,1)S(1)} async-done(((bf16[16,3,2,32,128]{4,3,2,1,0:T(8,128)(2,1)}), bf16[16,3,2,32,128]{4,3,2,1,0:T(8,128)(2,1)S(1)}, u32[]{:S(2)}, u32[]{:S(2)}) %all-to-all-start.2) | async-done | bytes 786464 | tf_op jit(solution)/shard_map/all_to_all | solution.py:328
  288.0 0.9 copy-done.5
  288.9 2.8 shard_map.62
  291.7 4.9 %copy.45 = bf16[96,2,32,128]{0,2,3,1:T(8,128)(2,1)} copy(bf16[96,2,32,128]{3,2,1,0:T(8,128)(2,1)} %shard_map.62) | data formatting | bytes 3145728 | tf_op jit(solution)/shard_map/pallas_call | solution.py:209
  296.6 3.0 shard_map.63
  (112 shorter events, 10.4 us)
Async XLA Ops:
  0.0 1.6 slice-start
  5.1 1.6 slice-start.1
  5.1 10.5 %collective-permute-start.8 = (bf16[16,6,2,32,128]{4,3,2,1,0:T(8,128)(2,1)}, bf16[16,6,2,32,128]{4,3,2,1,0:T(8,128)(2,1)}, u32[]{:S(2)}, u32[]{:S(2)}) collective-permute-start(bf16[16,6,2,32,128]{4,3,2,1,0:T(8,128)(2,1)} %bitcast.37), channel_id=1, source_target_pairs={{0,1},{1,0},{2,3},{3,2},{4,5},{5,4},{6,7},{7,6},{8,9},{9,8},{10,11... | collective-permute-start | bytes 4718600 | tf_op jit(solution)/shard_map/ppermute | solution.py:22
  10.2 1.6 slice-start.3
  10.2 39.7 %collective-permute-start.6 = (bf16[16,6,2,32,128]{4,3,2,1,0:T(8,128)(2,1)}, bf16[16,6,2,32,128]{4,3,2,1,0:T(8,128)(2,1)}, u32[]{:S(2)}, u32[]{:S(2)}) collective-permute-start(bf16[16,6,2,32,128]{4,3,2,1,0:T(8,128)(2,1)} %bitcast.35), channel_id=1, source_target_pairs={{0,1},{1,0},{2,3},{3,2},{4,5},{5,4},{6,7},{7,6},{8,9},{9,8},{10,11... | collective-permute-start | bytes 4718600 | tf_op jit(solution)/shard_map/ppermute | solution.py:22
  15.6 11.2 %slice-start.4 = ((s32[4,96,2]{1,2,0:T(2,128)}), s32[2,96,2]{1,2,0:T(2,128)S(1)}, s32[]{:S(2)}) async-start(s32[4,96,2]{1,2,0:T(2,128)} %param.6), calls=%async_computation.7 | async-start | bytes 4096 | tf_op jit(solution)/shard_map/slice | solution.py:307
  15.6 14.6 %slice-start.2 = ((bf16[96,2,32,274]{0,2,3,1:T(8,128)(2,1)}), bf16[96,2,32,18]{0,2,3,1:T(8,128)(2,1)S(1)}, s32[]{:S(2)}) async-start(bf16[96,2,32,274]{0,2,3,1:T(8,128)(2,1)} %param.4), calls=%async_computation.5 | async-start | bytes 589824 | tf_op jit(solution)/shard_map/slice | solution.py:296
  20.5 83.3 %collective-permute-start.10 = (bf16[16,6,2,32,128]{4,3,2,1,0:T(8,128)(2,1)}, bf16[16,6,2,32,128]{4,3,2,1,0:T(8,128)(2,1)}, u32[]{:S(2)}, u32[]{:S(2)}) collective-permute-start(bf16[16,6,2,32,128]{4,3,2,1,0:T(8,128)(2,1)} %shard_map.47.refs_4_.refs_0_), channel_id=1, source_target_pairs={{0,2},{1,3},{2,0},{3,1},{4,6},{5,7},{6,4},{7,5},{8,10},{9,11},{10,... | collective-permute-start | bytes 4718600 | tf_op jit(solution)/shard_map/ppermute | solution.py:22
  27.1 18.3 %collective-permute-start.2 = (s32[96]{0:T(128)S(1)}, s32[96]{0:T(128)S(1)}, u32[]{:S(2)}, u32[]{:S(2)}) collective-permute-start(s32[96]{0:T(128)S(1)} %get-tuple-element.75), channel_id=1, source_target_pairs={{0,12},{1,13},{2,14},{3,15},{4,8},{5,9},{6,10},{7,11},{8,4},{9,5},... | collective-permute-start | bytes 1160 | tf_op jit(solution)/shard_map/ppermute | solution.py:22
  33.1 13.9 %collective-permute-start.7 = (bf16[16,1,2,32,128]{4,3,2,1,0:T(8,128)(2,1)}, bf16[16,1,2,32,128]{4,3,2,1,0:T(8,128)(2,1)}, u32[]{:S(2)}, u32[]{:S(2)}) collective-permute-start(bf16[16,1,2,32,128]{4,3,2,1,0:T(8,128)(2,1)} %pad_bitcast_fusion.refs_1_), channel_id=1, source_target_pairs={{0,1},{1,0},{2,3},{3,2},{4,5},{5,4},{6,7},{7,6},{8,9},{9,8},{10,11... | collective-permute-start | bytes 786440 | tf_op jit(solution)/shard_map/ppermute | solution.py:22
  45.3 68.8 %collective-permute-start.3 = (bf16[4,6,2,32,128]{4,3,2,1,0:T(8,128)(2,1)}, bf16[4,6,2,32,128]{4,3,2,1,0:T(8,128)(2,1)S(1)}, u32[]{:S(2)}, u32[]{:S(2)}) collective-permute-start(bf16[4,6,2,32,128]{4,3,2,1,0:T(8,128)(2,1)} %get-tuple-element.40), channel_id=1, source_target_pairs={{0,4},{1,5},{2,6},{3,7},{4,0},{5,1},{6,2},{7,3},{8,12},{9,13},{10,... | collective-permute-start | bytes 1179656 | tf_op jit(solution)/shard_map/ppermute | solution.py:22
  45.4 71.9 %collective-permute-start.4 = (bf16[4,6,2,32,128]{4,3,2,1,0:T(8,128)(2,1)}, bf16[4,6,2,32,128]{4,3,2,1,0:T(8,128)(2,1)S(1)}, u32[]{:S(2)}, u32[]{:S(2)}) collective-permute-start(bf16[4,6,2,32,128]{4,3,2,1,0:T(8,128)(2,1)} %get-tuple-element.41), channel_id=1, source_target_pairs={{0,8},{1,9},{2,10},{3,11},{4,12},{5,13},{6,14},{7,15},{8,0},{9,1},... | collective-permute-start | bytes 1179656 | tf_op jit(solution)/shard_map/ppermute | solution.py:22
  47.0 71.4 %collective-permute-start.5 = (bf16[4,6,2,32,128]{4,3,2,1,0:T(8,128)(2,1)}, bf16[4,6,2,32,128]{4,3,2,1,0:T(8,128)(2,1)S(1)}, u32[]{:S(2)}, u32[]{:S(2)}) collective-permute-start(bf16[4,6,2,32,128]{4,3,2,1,0:T(8,128)(2,1)} %get-tuple-element.42), channel_id=1, source_target_pairs={{0,12},{1,13},{2,14},{3,15},{4,8},{5,9},{6,10},{7,11},{8,4},{9,5},... | collective-permute-start | bytes 1179656 | tf_op jit(solution)/shard_map/ppermute | solution.py:22
  50.0 15.3 %collective-permute-start.1 = (s32[96]{0:T(128)S(1)}, s32[96]{0:T(128)S(1)}, u32[]{:S(2)}, u32[]{:S(2)}) collective-permute-start(s32[96]{0:T(128)S(1)} %get-tuple-element.76), channel_id=1, source_target_pairs={{0,8},{1,9},{2,10},{3,11},{4,12},{5,13},{6,14},{7,15},{8,0},{9,1},... | collective-permute-start | bytes 1160 | tf_op jit(solution)/shard_map/ppermute | solution.py:22
  65.3 80.8 %collective-permute-start.9 = (bf16[16,4,2,32,128]{4,3,2,1,0:T(8,128)(2,1)}, bf16[16,4,2,32,128]{4,3,2,1,0:T(8,128)(2,1)S(1)}, u32[]{:S(2)}, u32[]{:S(2)}) collective-permute-start(bf16[16,4,2,32,128]{4,3,2,1,0:T(8,128)(2,1)} %get-tuple-element.45.refs_2_.refs_0_), channel_id=1, source_target_pairs={{0,2},{1,3},{2,0},{3,1},{4,6},{5,7},{6,4},{7,5},{8,10},{9,11},{10,... | collective-permute-start | bytes 3145736 | tf_op jit(solution)/shard_map/ppermute | solution.py:22
  103.8 9.9 %collective-permute-start = (s32[96]{0:T(128)S(1)}, s32[96]{0:T(128)S(1)}, u32[]{:S(2)}, u32[]{:S(2)}) collective-permute-start(s32[96]{0:T(128)S(1)} %get-tuple-element.77), channel_id=1, source_target_pairs={{0,4},{1,5},{2,6},{3,7},{4,0},{5,1},{6,2},{7,3},{8,12},{9,13},{10,... | collective-permute-start | bytes 1160 | tf_op jit(solution)/shard_map/ppermute | solution.py:22
  113.7 12.4 %collective-permute-start.11 = (bf16[4,6,2,32,128]{4,3,2,1,0:T(8,128)(2,1)}, bf16[4,6,2,32,128]{4,3,2,1,0:T(8,128)(2,1)}, u32[]{:S(2)}, u32[]{:S(2)}) collective-permute-start(bf16[4,6,2,32,128]{4,3,2,1,0:T(8,128)(2,1)} %get-tuple-element.47), channel_id=1, source_target_pairs={{0,4},{1,5},{2,6},{3,7},{4,0},{5,1},{6,2},{7,3},{8,12},{9,13},{10,... | collective-permute-start | bytes 1179656 | tf_op jit(solution)/shard_map/ppermute | solution.py:22
  114.1 21.5 %copy-start.2 = (bf16[4,6,2,32,128]{4,3,2,1,0:T(8,128)(2,1)}, bf16[4,6,2,32,128]{4,3,2,1,0:T(8,128)(2,1)S(1)}, u32[]{:S(2)}) copy-start(bf16[4,6,2,32,128]{4,3,2,1,0:T(8,128)(2,1)S(1)} %collective-permute-done.3.refs_1_) | copy-start | bytes 1179652
  114.1 18.9 %collective-permute-start.12 = (bf16[4,6,2,32,128]{4,3,2,1,0:T(8,128)(2,1)}, bf16[4,6,2,32,128]{4,3,2,1,0:T(8,128)(2,1)}, u32[]{:S(2)}, u32[]{:S(2)}) collective-permute-start(bf16[4,6,2,32,128]{4,3,2,1,0:T(8,128)(2,1)} %get-tuple-element.48), channel_id=1, source_target_pairs={{0,8},{1,9},{2,10},{3,11},{4,12},{5,13},{6,14},{7,15},{8,0},{9,1},... | collective-permute-start | bytes 1179656 | tf_op jit(solution)/shard_map/ppermute | solution.py:22
  117.3 18.3 %copy-start.3 = (bf16[4,6,2,32,128]{4,3,2,1,0:T(8,128)(2,1)}, bf16[4,6,2,32,128]{4,3,2,1,0:T(8,128)(2,1)S(1)}, u32[]{:S(2)}) copy-start(bf16[4,6,2,32,128]{4,3,2,1,0:T(8,128)(2,1)S(1)} %collective-permute-done.4.refs_2_) | copy-start | bytes 1179652
  117.3 18.3 %collective-permute-start.13 = (bf16[4,6,2,32,128]{4,3,2,1,0:T(8,128)(2,1)}, bf16[4,6,2,32,128]{4,3,2,1,0:T(8,128)(2,1)}, u32[]{:S(2)}, u32[]{:S(2)}) collective-permute-start(bf16[4,6,2,32,128]{4,3,2,1,0:T(8,128)(2,1)} %get-tuple-element.49), channel_id=1, source_target_pairs={{0,12},{1,13},{2,14},{3,15},{4,8},{5,9},{6,10},{7,11},{8,4},{9,5},... | collective-permute-start | bytes 1179656 | tf_op jit(solution)/shard_map/ppermute | solution.py:22
  118.4 17.3 %copy-start.4 = (bf16[4,6,2,32,128]{4,3,2,1,0:T(8,128)(2,1)}, bf16[4,6,2,32,128]{4,3,2,1,0:T(8,128)(2,1)S(1)}, u32[]{:S(2)}) copy-start(bf16[4,6,2,32,128]{4,3,2,1,0:T(8,128)(2,1)S(1)} %collective-permute-done.5.refs_3_) | copy-start | bytes 1179652
  118.4 54.4 %collective-permute-start.17 = (bf16[16,3,2,32,128]{4,3,2,1,0:T(8,128)(2,1)}, bf16[16,3,2,32,128]{4,3,2,1,0:T(8,128)(2,1)S(1)}, u32[]{:S(2)}, u32[]{:S(2)}) collective-permute-start(bf16[16,3,2,32,128]{4,3,2,1,0:T(8,128)(2,1)} %get-tuple-element.55.refs_0_), channel_id=1, source_target_pairs={{0,2},{1,3},{2,0},{3,1},{4,6},{5,7},{6,4},{7,5},{8,10},{9,11},{10,... | collective-permute-start | bytes 2359304 | tf_op jit(solution)/shard_map/ppermute | solution.py:22
  141.4 31.4 %collective-permute-start.18 = (bf16[4,6,2,32,128]{4,3,2,1,0:T(8,128)(2,1)}, bf16[4,6,2,32,128]{4,3,2,1,0:T(8,128)(2,1)S(1)}, u32[]{:S(2)}, u32[]{:S(2)}) collective-permute-start(bf16[4,6,2,32,128]{4,3,2,1,0:T(8,128)(2,1)} %get-tuple-element.56), channel_id=1, source_target_pairs={{0,4},{1,5},{2,6},{3,7},{4,0},{5,1},{6,2},{7,3},{8,12},{9,13},{10,... | collective-permute-start | bytes 1179656 | tf_op jit(solution)/shard_map/ppermute | solution.py:22
  141.4 31.4 %collective-permute-start.19 = (bf16[4,6,2,32,128]{4,3,2,1,0:T(8,128)(2,1)}, bf16[4,6,2,32,128]{4,3,2,1,0:T(8,128)(2,1)S(1)}, u32[]{:S(2)}, u32[]{:S(2)}) collective-permute-start(bf16[4,6,2,32,128]{4,3,2,1,0:T(8,128)(2,1)} %get-tuple-element.57), channel_id=1, source_target_pairs={{0,8},{1,9},{2,10},{3,11},{4,12},{5,13},{6,14},{7,15},{8,0},{9,1},... | collective-permute-start | bytes 1179656 | tf_op jit(solution)/shard_map/ppermute | solution.py:22
  143.9 28.9 %collective-permute-start.20 = (bf16[4,6,2,32,128]{4,3,2,1,0:T(8,128)(2,1)}, bf16[4,6,2,32,128]{4,3,2,1,0:T(8,128)(2,1)S(1)}, u32[]{:S(2)}, u32[]{:S(2)}) collective-permute-start(bf16[4,6,2,32,128]{4,3,2,1,0:T(8,128)(2,1)} %get-tuple-element.58), channel_id=1, source_target_pairs={{0,12},{1,13},{2,14},{3,15},{4,8},{5,9},{6,10},{7,11},{8,4},{9,5},... | collective-permute-start | bytes 1179656 | tf_op jit(solution)/shard_map/ppermute | solution.py:22
  146.1 1.0 copy-start.7
  172.7 0.9 copy-start.6
  172.7 1.0 copy-start.8
  172.7 1.2 copy-start.9
  172.8 1.3 copy-start.10
  176.7 17.7 %copy-start.26 = (bf16[4,4,2,32,128]{4,3,2,1,0:T(8,128)(2,1)S(1)}, bf16[4,4,2,32,128]{4,3,2,1,0:T(8,128)(2,1)}, u32[]{:S(2)}) copy-start(bf16[4,4,2,32,128]{4,3,2,1,0:T(8,128)(2,1)} %get-tuple-element.52) | copy-start | bytes 786436
  176.7 17.8 %copy-start.25 = (bf16[4,4,2,32,128]{4,3,2,1,0:T(8,128)(2,1)S(1)}, bf16[4,4,2,32,128]{4,3,2,1,0:T(8,128)(2,1)}, u32[]{:S(2)}) copy-start(bf16[4,4,2,32,128]{4,3,2,1,0:T(8,128)(2,1)} %get-tuple-element.53) | copy-start | bytes 786436
  176.7 21.6 %copy-start.24 = (bf16[4,4,2,32,128]{4,3,2,1,0:T(8,128)(2,1)S(1)}, bf16[4,4,2,32,128]{4,3,2,1,0:T(8,128)(2,1)}, u32[]{:S(2)}) copy-start(bf16[4,4,2,32,128]{4,3,2,1,0:T(8,128)(2,1)} %get-tuple-element.54) | copy-start | bytes 786436
  176.7 63.9 %all-to-all-start.1 = ((bf16[16,6,2,32,128]{4,3,2,1,0:T(8,128)(2,1)}), bf16[16,6,2,32,128]{4,3,2,1,0:T(8,128)(2,1)S(1)}, u32[]{:S(2)}, u32[]{:S(2)}) async-start(bf16[16,6,2,32,128]{4,3,2,1,0:T(8,128)(2,1)} %shard_map.52.refs_2_), calls=%async_computation.1 | async-start | bytes 3145728 | tf_op jit(solution)/shard_map/all_to_all | solution.py:328
  194.3 8.9 %collective-permute-start.14 = (bf16[4,4,2,32,128]{4,3,2,1,0:T(8,128)(2,1)S(1)}, bf16[4,4,2,32,128]{4,3,2,1,0:T(8,128)(2,1)S(1)}, u32[]{:S(2)}, u32[]{:S(2)}) collective-permute-start(bf16[4,4,2,32,128]{4,3,2,1,0:T(8,128)(2,1)S(1)} %copy-done.26), channel_id=1, source_target_pairs={{0,4},{1,5},{2,6},{3,7},{4,0},{5,1},{6,2},{7,3},{8,12},{9,13},{10,... | collective-permute-start | bytes 786440 | tf_op jit(solution)/shard_map/ppermute | solution.py:22
  194.4 12.4 %collective-permute-start.15 = (bf16[4,4,2,32,128]{4,3,2,1,0:T(8,128)(2,1)S(1)}, bf16[4,4,2,32,128]{4,3,2,1,0:T(8,128)(2,1)S(1)}, u32[]{:S(2)}, u32[]{:S(2)}) collective-permute-start(bf16[4,4,2,32,128]{4,3,2,1,0:T(8,128)(2,1)S(1)} %copy-done.25), channel_id=1, source_target_pairs={{0,8},{1,9},{2,10},{3,11},{4,12},{5,13},{6,14},{7,15},{8,0},{9,1},... | collective-permute-start | bytes 786440 | tf_op jit(solution)/shard_map/ppermute | solution.py:22
  198.2 10.4 %collective-permute-start.16 = (bf16[4,4,2,32,128]{4,3,2,1,0:T(8,128)(2,1)S(1)}, bf16[4,4,2,32,128]{4,3,2,1,0:T(8,128)(2,1)S(1)}, u32[]{:S(2)}, u32[]{:S(2)}) collective-permute-start(bf16[4,4,2,32,128]{4,3,2,1,0:T(8,128)(2,1)S(1)} %copy-done.24), channel_id=1, source_target_pairs={{0,12},{1,13},{2,14},{3,15},{4,8},{5,9},{6,10},{7,11},{8,4},{9,5},... | collective-permute-start | bytes 786440 | tf_op jit(solution)/shard_map/ppermute | solution.py:22
  203.2 17.0 %collective-permute-start.24 = (bf16[4,3,2,32,128]{4,3,2,1,0:T(8,128)(2,1)}, bf16[4,3,2,32,128]{4,3,2,1,0:T(8,128)(2,1)S(1)}, u32[]{:S(2)}, u32[]{:S(2)}) collective-permute-start(bf16[4,3,2,32,128]{4,3,2,1,0:T(8,128)(2,1)} %get-tuple-element.64), channel_id=1, source_target_pairs={{0,4},{1,5},{2,6},{3,7},{4,0},{5,1},{6,2},{7,3},{8,12},{9,13},{10,... | collective-permute-start | bytes 589832 | tf_op jit(solution)/shard_map/ppermute | solution.py:22
  203.2 5.5 %copy-start.14 = (bf16[4,4,2,32,128]{4,3,2,1,0:T(8,128)(2,1)}, bf16[4,4,2,32,128]{4,3,2,1,0:T(8,128)(2,1)S(1)}, u32[]{:S(2)}) copy-start(bf16[4,4,2,32,128]{4,3,2,1,0:T(8,128)(2,1)S(1)} %collective-permute-done.14.refs_5_) | copy-start | bytes 786436
  203.2 17.0 %copy-start.29 = (bf16[4,3,2,32,128]{4,3,2,1,0:T(8,128)(2,1)S(1)}, bf16[4,3,2,32,128]{4,3,2,1,0:T(8,128)(2,1)}, u32[]{:S(2)}) copy-start(bf16[4,3,2,32,128]{4,3,2,1,0:T(8,128)(2,1)} %get-tuple-element.65) | copy-start | bytes 589828
  203.2 17.0 %copy-start.28 = (bf16[4,3,2,32,128]{4,3,2,1,0:T(8,128)(2,1)S(1)}, bf16[4,3,2,32,128]{4,3,2,1,0:T(8,128)(2,1)}, u32[]{:S(2)}) copy-start(bf16[4,3,2,32,128]{4,3,2,1,0:T(8,128)(2,1)} %get-tuple-element.66) | copy-start | bytes 589828
  206.9 1.8 copy-start.15
  208.6 0.7 copy-start.16
  215.5 21.9 %collective-permute-start.21 = (bf16[4,4,2,32,128]{4,3,2,1,0:T(8,128)(2,1)}, bf16[4,4,2,32,128]{4,3,2,1,0:T(8,128)(2,1)S(1)}, u32[]{:S(2)}, u32[]{:S(2)}) collective-permute-start(bf16[4,4,2,32,128]{4,3,2,1,0:T(8,128)(2,1)} %get-tuple-element.61), channel_id=1, source_target_pairs={{0,4},{1,5},{2,6},{3,7},{4,0},{5,1},{6,2},{7,3},{8,12},{9,13},{10,... | collective-permute-start | bytes 786440 | tf_op jit(solution)/shard_map/ppermute | solution.py:22
  215.5 21.9 %collective-permute-start.22 = (bf16[4,4,2,32,128]{4,3,2,1,0:T(8,128)(2,1)}, bf16[4,4,2,32,128]{4,3,2,1,0:T(8,128)(2,1)S(1)}, u32[]{:S(2)}, u32[]{:S(2)}) collective-permute-start(bf16[4,4,2,32,128]{4,3,2,1,0:T(8,128)(2,1)} %get-tuple-element.62), channel_id=1, source_target_pairs={{0,8},{1,9},{2,10},{3,11},{4,12},{5,13},{6,14},{7,15},{8,0},{9,1},... | collective-permute-start | bytes 786440 | tf_op jit(solution)/shard_map/ppermute | solution.py:22
  217.8 19.6 %collective-permute-start.23 = (bf16[4,4,2,32,128]{4,3,2,1,0:T(8,128)(2,1)}, bf16[4,4,2,32,128]{4,3,2,1,0:T(8,128)(2,1)S(1)}, u32[]{:S(2)}, u32[]{:S(2)}) collective-permute-start(bf16[4,4,2,32,128]{4,3,2,1,0:T(8,128)(2,1)} %get-tuple-element.63), channel_id=1, source_target_pairs={{0,12},{1,13},{2,14},{3,15},{4,8},{5,9},{6,10},{7,11},{8,4},{9,5},... | collective-permute-start | bytes 786440 | tf_op jit(solution)/shard_map/ppermute | solution.py:22
  220.2 7.2 %collective-permute-start.25 = (bf16[4,3,2,32,128]{4,3,2,1,0:T(8,128)(2,1)S(1)}, bf16[4,3,2,32,128]{4,3,2,1,0:T(8,128)(2,1)S(1)}, u32[]{:S(2)}, u32[]{:S(2)}) collective-permute-start(bf16[4,3,2,32,128]{4,3,2,1,0:T(8,128)(2,1)S(1)} %copy-done.29), channel_id=1, source_target_pairs={{0,8},{1,9},{2,10},{3,11},{4,12},{5,13},{6,14},{7,15},{8,0},{9,1},... | collective-permute-start | bytes 589832 | tf_op jit(solution)/shard_map/ppermute | solution.py:22
  220.2 12.0 %copy-start.20 = (bf16[4,3,2,32,128]{4,3,2,1,0:T(8,128)(2,1)}, bf16[4,3,2,32,128]{4,3,2,1,0:T(8,128)(2,1)S(1)}, u32[]{:S(2)}) copy-start(bf16[4,3,2,32,128]{4,3,2,1,0:T(8,128)(2,1)S(1)} %collective-permute-done.24.refs_5_) | copy-start | bytes 589828
  220.2 12.0 %collective-permute-start.26 = (bf16[4,3,2,32,128]{4,3,2,1,0:T(8,128)(2,1)S(1)}, bf16[4,3,2,32,128]{4,3,2,1,0:T(8,128)(2,1)S(1)}, u32[]{:S(2)}, u32[]{:S(2)}) collective-permute-start(bf16[4,3,2,32,128]{4,3,2,1,0:T(8,128)(2,1)S(1)} %copy-done.28), channel_id=1, source_target_pairs={{0,12},{1,13},{2,14},{3,15},{4,8},{5,9},{6,10},{7,11},{8,4},{9,5},... | collective-permute-start | bytes 589832 | tf_op jit(solution)/shard_map/ppermute | solution.py:22
  227.4 4.8 %copy-start.21 = (bf16[4,3,2,32,128]{4,3,2,1,0:T(8,128)(2,1)}, bf16[4,3,2,32,128]{4,3,2,1,0:T(8,128)(2,1)S(1)}, u32[]{:S(2)}) copy-start(bf16[4,3,2,32,128]{4,3,2,1,0:T(8,128)(2,1)S(1)} %collective-permute-done.25.refs_6_) | copy-start | bytes 589828
  237.4 0.7 copy-start.11
  237.4 0.8 copy-start.12
  237.4 0.8 copy-start.13
  240.5 11.5 %copy-start.27 = (bf16[4,3,2,32,128]{4,3,2,1,0:T(8,128)(2,1)S(1)}, bf16[4,3,2,32,128]{4,3,2,1,0:T(8,128)(2,1)}, u32[]{:S(2)}) copy-start(bf16[4,3,2,32,128]{4,3,2,1,0:T(8,128)(2,1)} %get-tuple-element.70) | copy-start | bytes 589828
  240.5 12.4 %copy-start.1 = (bf16[16,6,2,32,128]{4,3,2,1,0:T(8,128)(2,1)}, bf16[16,6,2,32,128]{4,3,2,1,0:T(8,128)(2,1)S(1)}, u32[]{:S(2)}) copy-start(bf16[16,6,2,32,128]{4,3,2,1,0:T(8,128)(2,1)S(1)} %all-to-all-done.1.refs_0_) | copy-start | bytes 4718596
  240.5 26.6 %all-to-all-start = ((bf16[16,4,2,32,128]{4,3,2,1,0:T(8,128)(2,1)}), bf16[16,4,2,32,128]{4,3,2,1,0:T(8,128)(2,1)S(1)}, u32[]{:S(2)}, u32[]{:S(2)}) async-start(bf16[16,4,2,32,128]{4,3,2,1,0:T(8,128)(2,1)} %shard_map.56.refs_4_), calls=%async_computation | async-start | bytes 2097152 | tf_op jit(solution)/shard_map/all_to_all | solution.py:328
  248.2 15.4 %collective-permute-start.27 = (bf16[4,3,2,32,128]{4,3,2,1,0:T(8,128)(2,1)}, bf16[4,3,2,32,128]{4,3,2,1,0:T(8,128)(2,1)S(1)}, u32[]{:S(2)}, u32[]{:S(2)}) collective-permute-start(bf16[4,3,2,32,128]{4,3,2,1,0:T(8,128)(2,1)} %get-tuple-element.68), channel_id=1, source_target_pairs={{0,4},{1,5},{2,6},{3,7},{4,0},{5,1},{6,2},{7,3},{8,12},{9,13},{10,... | collective-permute-start | bytes 589832 | tf_op jit(solution)/shard_map/ppermute | solution.py:22
  248.2 15.4 %collective-permute-start.28 = (bf16[4,3,2,32,128]{4,3,2,1,0:T(8,128)(2,1)}, bf16[4,3,2,32,128]{4,3,2,1,0:T(8,128)(2,1)S(1)}, u32[]{:S(2)}, u32[]{:S(2)}) collective-permute-start(bf16[4,3,2,32,128]{4,3,2,1,0:T(8,128)(2,1)} %get-tuple-element.69), channel_id=1, source_target_pairs={{0,8},{1,9},{2,10},{3,11},{4,12},{5,13},{6,14},{7,15},{8,0},{9,1},... | collective-permute-start | bytes 589832 | tf_op jit(solution)/shard_map/ppermute | solution.py:22
  252.0 11.6 %collective-permute-start.29 = (bf16[4,3,2,32,128]{4,3,2,1,0:T(8,128)(2,1)S(1)}, bf16[4,3,2,32,128]{4,3,2,1,0:T(8,128)(2,1)S(1)}, u32[]{:S(2)}, u32[]{:S(2)}) collective-permute-start(bf16[4,3,2,32,128]{4,3,2,1,0:T(8,128)(2,1)S(1)} %copy-done.27), channel_id=1, source_target_pairs={{0,12},{1,13},{2,14},{3,15},{4,8},{5,9},{6,10},{7,11},{8,4},{9,5},... | collective-permute-start | bytes 589832 | tf_op jit(solution)/shard_map/ppermute | solution.py:22
  263.6 0.7 copy-start.18
  267.2 7.5 %copy-start = (bf16[16,4,2,32,128]{4,3,2,1,0:T(8,128)(2,1)}, bf16[16,4,2,32,128]{4,3,2,1,0:T(8,128)(2,1)S(1)}, u32[]{:S(2)}) copy-start(bf16[16,4,2,32,128]{4,3,2,1,0:T(8,128)(2,1)S(1)} %all-to-all-done.refs_0_) | copy-start | bytes 3145732
  267.2 20.8 %all-to-all-start.2 = ((bf16[16,3,2,32,128]{4,3,2,1,0:T(8,128)(2,1)}), bf16[16,3,2,32,128]{4,3,2,1,0:T(8,128)(2,1)S(1)}, u32[]{:S(2)}, u32[]{:S(2)}) async-start(bf16[16,3,2,32,128]{4,3,2,1,0:T(8,128)(2,1)} %shard_map.59.refs_1_), calls=%async_computation.2 | async-start | bytes 1572864 | tf_op jit(solution)/shard_map/all_to_all | solution.py:328
  288.0 0.9 copy-start.5
  (4 other events, 2.7 us)
